TPU v7x, 32 devices: a whole 2x2x4 slice. The times are simulated.
32 devices in a mesh: wide: 8 (over z, x), slab: 4 (over y, core).
Axes of the slice: x: 2, y: 2, z: 4, core: 2. Of those that a mesh axis runs over, the one named last changes fastest.
Arguments:
- fields: float32 [4, 512, 64, 512], P(None, 'slab', 'wide'), may hold values from -60 to 60
- start_basis: float32 [512, 128], replicated, may hold values from -6 to 6
Outputs:
- core_tensor: float32 [4, 512, 64, 128], P(None, None, ('wide', 'slab'))
All inputs are finite; a program needn't handle non-finite values.
Results may differ from a plain program's by a relative error of at most 0.0003.
Values sent between devices are 32-bit elements; how exact they have to be, the bound alone decides.
No kernel may reach another device: no remote copies, remote signals or barrier semaphores. Data moves between devices by JAX's collectives and lax.ppermute only.
A program may use at most 64 MiB of HBM per device.

v0:
```python
import jax
import jax.numpy as jnp
from jax import lax
from jax.sharding import PartitionSpec as P

SWEEPS = 4


def partner(value, axis, distance):
    return lax.ppermute(value, axis, [(i, i ^ 1 << distance) for i in range(lax.axis_size(axis))])


def orthonormal(block):
    square = jnp.dot(
        block.T, block, precision=lax.Precision.HIGHEST, preferred_element_type=jnp.float32
    )
    triangle = jnp.linalg.cholesky(square)
    return lax.linalg.triangular_solve(
        triangle, block, left_side=False, lower=True, transpose_a=True
    )


def per_device(fields, start_basis):
    unfolded = fields.reshape(-1, fields.shape[-1])
    count = float(unfolded.shape[0] * lax.axis_size("wide") * lax.axis_size("slab"))
    local_gram = (
        lax.dot_general(
            unfolded,
            unfolded,
            (((0,), (0,)), ((), ())),
            precision=lax.Precision.HIGHEST,
            preferred_element_type=jnp.float32,
        )
        / count
    )
    gram = local_gram
    for level in range(lax.axis_size("wide").bit_length() - 1):
        gram = gram + partner(gram, "wide", level)
    for level in range(lax.axis_size("slab").bit_length() - 1):
        gram = gram + partner(gram, "slab", level)
    basis = start_basis
    for sweep in range(SWEEPS):
        block = jnp.dot(
            gram, basis, precision=lax.Precision.HIGHEST, preferred_element_type=jnp.float32
        )
        basis = orthonormal(block)
    projected = jnp.dot(
        unfolded, basis, precision=lax.Precision.HIGHEST, preferred_element_type=jnp.float32
    )
    projected = projected.reshape(fields.shape[0], fields.shape[1], fields.shape[2], basis.shape[1])
    return lax.all_to_all(projected, "slab", split_axis=2, concat_axis=1, tiled=True)


def solution(mesh):
    in_specs = (P(None, "slab", "wide", None), P())
    out_specs = P(None, None, ("wide", "slab"), None)
    return jax.shard_map(
        per_device, mesh=mesh, in_specs=in_specs, out_specs=out_specs, check_vma=False
    )
```

profile of v0, /device:TPU:1, one launch (start us, length us, event | category | flops | bytes accessed | tf_op | source)
XLA Modules:
  0.0 289.8 jit_solution(2640697481934029900)
XLA Ops:
  0.0 17.5 %fusion = f32[512,512]{1,0:T(8,128)S(1)} fusion(f32[4,128,8,512]{3,2,1,0:T(8,128)} %param.5), kind=kOutput, calls=%fused_computation.2 | convolution fusion | flops 12885164032 | bytes 9437184 | tf_op jit(solution)/shard_map/dot_general | solution.py:27
  17.6 2.1 collective-permute-start
  19.7 22.9 %collective-permute-done = f32[512,512]{1,0:T(8,128)S(1)} collective-permute-done((f32[512,512]{1,0:T(8,128)S(1)}, f32[512,512]{1,0:T(8,128)S(1)}, u32[]{:S(2)}, u32[]{:S(2)}) %collective-permute-start) | collective-permute-done | bytes 1048608 | tf_op jit(solution)/shard_map/ppermute | solution.py:10
  42.5 0.2 add.23
  42.8 1.3 collective-permute-start.1
  44.0 22.2 %collective-permute-done.1 = f32[512,512]{1,0:T(8,128)S(1)} collective-permute-done((f32[512,512]{1,0:T(8,128)S(1)}, f32[512,512]{1,0:T(8,128)S(1)}, u32[]{:S(2)}, u32[]{:S(2)}) %collective-permute-start.1) | collective-permute-done | bytes 1048608 | tf_op jit(solution)/shard_map/ppermute | solution.py:10
  66.2 0.2 add.24
  66.5 2.0 collective-permute-start.2
  68.4 45.8 %collective-permute-done.2 = f32[512,512]{1,0:T(8,128)S(1)} collective-permute-done((f32[512,512]{1,0:T(8,128)S(1)}, f32[512,512]{1,0:T(8,128)S(1)}, u32[]{:S(2)}, u32[]{:S(2)}) %collective-permute-start.2) | collective-permute-done | bytes 1048608 | tf_op jit(solution)/shard_map/ppermute | solution.py:10
  114.3 0.2 add.25
  114.5 1.2 collective-permute-start.3
  115.7 2.3 collective-permute-done.3
  118.2 0.9 collective-permute-start.4
  119.2 23.5 %collective-permute-done.4 = f32[512,512]{1,0:T(8,128)S(1)} collective-permute-done((f32[512,512]{1,0:T(8,128)S(1)}, f32[512,512]{1,0:T(8,128)S(1)}, u32[]{:S(2)}, u32[]{:S(2)}) %collective-permute-start.4) | collective-permute-done | bytes 1048608 | tf_op jit(solution)/shard_map/ppermute | solution.py:10
  142.9 1.0 fusion.19
  143.9 0.6 fusion.20
  144.6 11.7 %cholesky.74 = f32[128,128]{1,0:T(8,128)S(1)} custom-call(f32[128,128]{1,0:T(8,128)S(1)} %fusion.12), custom_call_target="Cholesky" | custom-call | tf_op jit(solution)/shard_map/jit(cholesky)/cholesky | solution.py:17
  156.3 0.6 compare_reduce_fusion.3
  157.0 0.7 fusion.1
  157.7 9.8 %custom-call.8 = f32[1,128,128]{1,2,0:T(8,128)S(1)} custom-call(f32[1,128,128]{2,1,0:T(8,128)S(1)} %fusion.1), custom_call_target="InvertDiagBlocksLowerTriangular" | custom-call | tf_op jit(solution)/shard_map/triangular_solve/custom-call.0 | solution.py:18
  167.5 0.4 convolution_bitcast_fusion.5
  167.9 1.0 fusion.21
  168.9 0.6 fusion.22
  169.6 11.9 %cholesky.85 = f32[128,128]{1,0:T(8,128)S(1)} custom-call(f32[128,128]{1,0:T(8,128)S(1)} %fusion.10), custom_call_target="Cholesky" | custom-call | tf_op jit(solution)/shard_map/jit(cholesky)/cholesky | solution.py:17
  181.5 0.6 compare_reduce_fusion.2
  182.2 0.7 fusion.2
  182.8 9.8 %custom-call.9 = f32[1,128,128]{1,2,0:T(8,128)S(1)} custom-call(f32[1,128,128]{2,1,0:T(8,128)S(1)} %fusion.2), custom_call_target="InvertDiagBlocksLowerTriangular" | custom-call | tf_op jit(solution)/shard_map/triangular_solve/custom-call.0 | solution.py:18
  192.6 0.4 convolution_bitcast_fusion.4
  193.1 1.0 fusion.23
  194.1 0.6 fusion.24
  194.8 11.7 %cholesky.96 = f32[128,128]{1,0:T(8,128)S(1)} custom-call(f32[128,128]{1,0:T(8,128)S(1)} %fusion.8), custom_call_target="Cholesky" | custom-call | tf_op jit(solution)/shard_map/jit(cholesky)/cholesky | solution.py:17
  206.5 0.6 compare_reduce_fusion.1
  207.2 0.7 fusion.3
  207.8 10.2 %custom-call.10 = f32[1,128,128]{1,2,0:T(8,128)S(1)} custom-call(f32[1,128,128]{2,1,0:T(8,128)S(1)} %fusion.3), custom_call_target="InvertDiagBlocksLowerTriangular" | custom-call | tf_op jit(solution)/shard_map/triangular_solve/custom-call.0 | solution.py:18
  218.0 0.4 convolution_bitcast_fusion.3
  218.4 1.0 fusion.25
  219.4 0.6 fusion.26
  220.1 11.7 %cholesky.107 = f32[128,128]{1,0:T(8,128)S(1)} custom-call(f32[128,128]{1,0:T(8,128)S(1)} %fusion.6), custom_call_target="Cholesky" | custom-call | tf_op jit(solution)/shard_map/jit(cholesky)/cholesky | solution.py:17
  231.9 0.6 compare_reduce_fusion
  232.5 0.7 fusion.4
  233.2 9.8 %custom-call.11 = f32[1,128,128]{1,2,0:T(8,128)S(1)} custom-call(f32[1,128,128]{2,1,0:T(8,128)S(1)} %fusion.4), custom_call_target="InvertDiagBlocksLowerTriangular" | custom-call | tf_op jit(solution)/shard_map/triangular_solve/custom-call.0 | solution.py:18
  243.0 0.4 convolution_bitcast_fusion.2
  243.4 12.3 %convolution_bitcast_fusion = f32[4096,128]{0,1:T(8,128)} fusion(f32[512,128]{0,1:T(8,128)S(1)} %convolution_bitcast_fusion.2, f32[4096,512]{1,0:T(8,128)} %bitcast.82), kind=kOutput, calls=%fused_computation | convolution fusion | flops 3221225472 | bytes 10747904 | tf_op jit(solution)/shard_map/dot_general | solution.py:47
  255.7 1.9 copy.30
  257.7 0.4 copy.31
  258.1 28.3 %all_to_all.18 = f32[4,128,8,128]{3,1,0,2:T(8,128)S(1)} all-to-all(f32[4,128,8,128]{3,1,0,2:T(8,128)S(1)} %copy.31), channel_id=1, replica_groups=mesh['wide'=8,'slab'=4] {'slab'}, dimensions={2} | all-to-all | bytes 4194304 | tf_op jit(solution)/shard_map/all_to_all | solution.py:51
  286.4 0.2 copy.33
  286.6 2.9 %copy.34 = f32[4,512,2,128]{3,2,1,0:T(2,128)} copy(f32[4,512,2,128]{3,1,2,0:T(8,128)S(1)} %bitcast.85) | data formatting | bytes 4194304 | tf_op jit(solution)/shard_map/all_to_all | solution.py:51
  (16 shorter events, 1.0 us)
Async XLA Ops:
  0.0 142.9 %copy-start = (f32[512,128]{1,0:T(8,128)S(1)}, f32[512,128]{1,0:T(8,128)}, u32[]{:S(2)}) copy-start(f32[512,128]{1,0:T(8,128)} %param.6) | copy-start | bytes 786436
  17.6 25.0 %collective-permute-start = (f32[512,512]{1,0:T(8,128)S(1)}, f32[512,512]{1,0:T(8,128)S(1)}, u32[]{:S(2)}, u32[]{:S(2)}) collective-permute-start(f32[512,512]{1,0:T(8,128)S(1)} %fusion), channel_id=1, source_target_pairs={{0,4},{4,0},{8,12},{12,8},{16,20},{20,16},{24,28},{28,24},{1,5},{5... | collective-permute-start | bytes 3145736 | tf_op jit(solution)/shard_map/ppermute | solution.py:10
  42.8 23.5 %collective-permute-start.1 = (f32[512,512]{1,0:T(8,128)S(1)}, f32[512,512]{1,0:T(8,128)S(1)}, u32[]{:S(2)}, u32[]{:S(2)}) collective-permute-start(f32[512,512]{1,0:T(8,128)S(1)} %add.23), channel_id=1, source_target_pairs={{0,8},{4,12},{8,0},{12,4},{16,24},{20,28},{24,16},{28,20},{1,9},{5... | collective-permute-start | bytes 3145736 | tf_op jit(solution)/shard_map/ppermute | solution.py:10
  66.5 47.8 %collective-permute-start.2 = (f32[512,512]{1,0:T(8,128)S(1)}, f32[512,512]{1,0:T(8,128)S(1)}, u32[]{:S(2)}, u32[]{:S(2)}) collective-permute-start(f32[512,512]{1,0:T(8,128)S(1)} %add.24), channel_id=1, source_target_pairs={{0,16},{4,20},{8,24},{12,28},{16,0},{20,4},{24,8},{28,12},{1,17},{... | collective-permute-start | bytes 3145736 | tf_op jit(solution)/shard_map/ppermute | solution.py:10
  114.5 3.5 %collective-permute-start.3 = (f32[512,512]{1,0:T(8,128)S(1)}, f32[512,512]{1,0:T(8,128)S(1)}, u32[]{:S(2)}, u32[]{:S(2)}) collective-permute-start(f32[512,512]{1,0:T(8,128)S(1)} %add.25), channel_id=1, source_target_pairs={{0,1},{1,0},{2,3},{3,2},{4,5},{5,4},{6,7},{7,6},{8,9},{9,8},{10,11... | collective-permute-start | bytes 3145736 | tf_op jit(solution)/shard_map/ppermute | solution.py:10
  118.2 24.4 %collective-permute-start.4 = (f32[512,512]{1,0:T(8,128)S(1)}, f32[512,512]{1,0:T(8,128)S(1)}, u32[]{:S(2)}, u32[]{:S(2)}) collective-permute-start(f32[512,512]{1,0:T(8,128)S(1)} %add.26), channel_id=1, source_target_pairs={{0,2},{1,3},{2,0},{3,1},{4,6},{5,7},{6,4},{7,5},{8,10},{9,11},{10,... | collective-permute-start | bytes 3145736 | tf_op jit(solution)/shard_map/ppermute | solution.py:10
where the time goes:
time: 294 us; the launch traced here: 290 us
  waiting for transfers between devices  117 us (40%)
  other arithmetic  93.1 us (32%)
  matrix products  37.8 us (13%)
  blocking collectives  28.3 us (10%)
  starting transfers between devices  7.54 us (3%)
  local copies, waits for them, and re-layouts  5.83 us (2%)
    ppermute x5, waiting for transfers between devices, partner(): lax.ppermute(value, axis, [(i, i ^ 1 << distance) for i in range(lax.axis...  117 us
    another operation x12, other arithmetic, orthonormal(): triangle = jnp.linalg.cholesky(square)  49.7 us
    another operation x8, other arithmetic, orthonormal(): lax.linalg.triangular_solve(triangle, block, left_side=False, lower=True,...  42.2 us
    all_to_all x1, blocking collectives, per_device(): lax.all_to_all(projected, 'slab', split_axis=2, concat_axis=1, tiled=True)  28.3 us
    dot_general x1, matrix products, per_device(): lax.dot_general(unfolded, unfolded, (((0,), (0,)), ((), ())), precision=l...  17.5 us
    dot_general x1, matrix products, per_device(): jnp.dot(unfolded, basis, precision=lax.Precision.HIGHEST, preferred_eleme...  12.3 us
    ppermute x5, starting transfers between devices, partner(): lax.ppermute(value, axis, [(i, i ^ 1 << distance) for i in range(lax.axis...  7.54 us
  transfers between devices with their start and end apart: 5, of which 5 were waited for; matrix products, arithmetic and copies ran while one was open for 0% of the time, Pallas kernels for 0%

commit v1 on v0

v1 whole, which is shorter than its diff:
```python
import functools

import jax
import jax.numpy as jnp
from jax import lax
from jax.experimental import pallas as pl
from jax.experimental.pallas import tpu as pltpu
from jax.sharding import PartitionSpec as P

SWEEPS = 4
AXES = ("wide", "slab")
MIB = 1 << 20
HIGHEST = lax.Precision.HIGHEST
NN = (((1,), (0,)), ((), ()))
NT = (((1,), (1,)), ((), ()))
TN = (((0,), (0,)), ((), ()))


def dot(a, b, dims, precision=None):
    return lax.dot_general(a, b, dims, precision=precision, preferred_element_type=jnp.float32)


def halves(x):
    high = x.astype(jnp.bfloat16)
    return high, (x - high.astype(jnp.float32)).astype(jnp.bfloat16)


def exchange(value, axes, mask):
    size = 1
    for axis in axes if isinstance(axes, tuple) else (axes,):
        size *= lax.axis_size(axis)
    return lax.ppermute(value, axes, [(i, i ^ mask) for i in range(size)])


def upper_blocks(blocks):
    return [(i, j) for i in range(blocks) for j in range(i, blocks)]


def gram_kernel(scale, place_ref, x_ref, keep_ref, give_ref, acc, whole):
    step = pl.program_id(0)
    n = x_ref.shape[1]
    half = n // 2
    high, low = halves(x_ref[...])
    left = dot(high[:, :half], jnp.concatenate([high, low], axis=1), TN)
    right = dot(high[:, half:], jnp.concatenate([high[:, half:], low], axis=1), TN)

    @pl.when(step == 0)
    def _():
        acc[:half, :] = left
        acc[half:, half:] = right

    @pl.when(step > 0)
    def _():
        acc[:half, :] += left
        acc[half:, half:] += right

    @pl.when(step == pl.num_programs(0) - 1)
    def _():
        edge = 128
        for number, (i, j) in enumerate(upper_blocks(n // edge)):
            rows, columns = slice(i * edge, (i + 1) * edge), slice(j * edge, (j + 1) * edge)
            cross = acc[rows, n + j * edge : n + (j + 1) * edge]
            other = acc[columns, n + i * edge : n + (i + 1) * edge]
            whole[number * edge : (number + 1) * edge, :] = (
                acc[rows, columns] + cross + other.T
            ) * scale
        place = place_ref[0]
        part = keep_ref.shape[0] // 4
        for k in range(4):
            quarter = ((place >> 1) & 3) ^ k
            mine = pl.multiple_of(((place & 1) * 4 + quarter) * part, 8)
            theirs = pl.multiple_of(((1 - (place & 1)) * 4 + quarter) * part, 8)
            keep_ref[k * part : (k + 1) * part, :] = whole[pl.ds(mine, part), :]
            give_ref[k * part : (k + 1) * part, :] = whole[pl.ds(theirs, part), :]


def local_gram(place, rows, count):
    n = rows.shape[1]
    tile = 512
    tall = len(upper_blocks(n // 128)) * 128
    shape = jax.ShapeDtypeStruct((tall // 2, 128), jnp.float32)
    return pl.pallas_call(
        functools.partial(gram_kernel, 1.0 / count),
        grid=(rows.shape[0] // tile,),
        in_specs=[
            pl.BlockSpec(memory_space=pltpu.SMEM),
            pl.BlockSpec((tile, n), lambda i: (i, 0)),
        ],
        out_specs=[pl.BlockSpec((tall // 2, 128), lambda i: (0, 0))] * 2,
        out_shape=[shape, shape],
        scratch_shapes=[
            pltpu.VMEM((n, 2 * n), jnp.float32),
            pltpu.VMEM((tall, 128), jnp.float32),
        ],
        compiler_params=pltpu.CompilerParams(vmem_limit_bytes=32 * MIB),
        name="local_gram",
    )(place, rows)


def sum_gram(keep, give):
    size = lax.axis_size("wide") * lax.axis_size("slab")
    held = keep + exchange(give, AXES, 1)
    part = held.shape[0] // 4
    pieces = [held[k * part : (k + 1) * part] for k in range(4)]
    total = pieces[0]
    arrived = [exchange(pieces[k], AXES, 2 * k) for k in range(1, 4)]
    for piece in arrived:
        total = total + piece
    mask = 8
    while mask < size:
        total = total + exchange(total, AXES, mask)
        mask *= 2
    mine = jnp.concatenate([total] + [exchange(total, AXES, 2 * k) for k in range(1, 4)])
    return mine, exchange(mine, AXES, 1)


def row_of(x, p):
    return jnp.broadcast_to(x[p : p + 1, :], x.shape)


def column_of(x, k):
    return jnp.broadcast_to(x[:, k : k + 1], x.shape)


def invert_factor(work, result):
    n = work.shape[0]
    lane = lax.broadcasted_iota(jnp.int32, (8, n), 1)
    sub = lax.broadcasted_iota(jnp.int32, (8, n), 0)
    for lo in range(0, n, 8):
        hi = lo + 8
        rows = work[lo:hi, :]
        columns = [column_of(rows, lo + k) for k in range(8)]
        rows = jnp.where((lane >= lo) & (lane < hi), (lane - lo == sub).astype(jnp.float32), rows)
        scaled = jnp.zeros((8, n), jnp.float32)
        for p in range(8):
            pivot = row_of(columns[p], p)
            inverse = 1.0 / pivot
            row = row_of(rows, p)
            here = sub == p
            scaled = jnp.where(here, row * lax.rsqrt(pivot), scaled)
            row = row * inverse
            rows = jnp.where(here, row, rows - columns[p] * row)
            for k in range(p + 1, 8):
                entry = row_of(columns[k], p) * inverse
                columns[k] = jnp.where(here, entry, columns[k] - columns[p] * entry)
        result[lo:hi, :] = jnp.where(lane <= sub + lo, scaled, 0.0)
        if hi < n:
            rest = work[hi:, :]
            lane_rest = lax.broadcasted_iota(jnp.int32, rest.shape, 1)
            update = jnp.where((lane_rest >= lo) & (lane_rest < hi), 0.0, rest)
            for k in range(8):
                update = update - column_of(rest, lo + k) * jnp.broadcast_to(
                    rows[k : k + 1, :], rest.shape
                )
            work[hi:, :] = update


def sweep_kernel(sweeps, place_ref, mine_ref, other_ref, start_ref, block_ref, blocks, gram, work, factor):
    place = place_ref[0]
    part = mine_ref.shape[0] // 4
    for k in range(4):
        quarter = ((place >> 1) & 3) ^ k
        mine = pl.multiple_of(((place & 1) * 4 + quarter) * part, 8)
        theirs = pl.multiple_of(((1 - (place & 1)) * 4 + quarter) * part, 8)
        blocks[pl.ds(mine, part), :] = mine_ref[k * part : (k + 1) * part, :]
        blocks[pl.ds(theirs, part), :] = other_ref[k * part : (k + 1) * part, :]
    edge = 128
    for number, (i, j) in enumerate(upper_blocks(gram.shape[0] // edge)):
        block = blocks[number * edge : (number + 1) * edge, :]
        gram[i * edge : (i + 1) * edge, j * edge : (j + 1) * edge] = block
        if i != j:
            gram[j * edge : (j + 1) * edge, i * edge : (i + 1) * edge] = block.T

    block_ref[...] = dot(start_ref[...].T, gram[...], NN, HIGHEST)

    def sweep(_, carry):
        block = block_ref[...]
        work[...] = dot(block, block, NT, HIGHEST)
        invert_factor(work, factor)
        basis = dot(factor[...], block, NN, HIGHEST)
        block_ref[...] = dot(basis, gram[...], NN, HIGHEST)
        return carry

    lax.fori_loop(0, sweeps - 1, sweep, 0)


def iterate(place, mine, other, start):
    n, rank = start.shape
    vmem = pl.BlockSpec(memory_space=pltpu.VMEM)
    return pl.pallas_call(
        functools.partial(sweep_kernel, SWEEPS),
        in_specs=[pl.BlockSpec(memory_space=pltpu.SMEM), vmem, vmem, vmem],
        out_specs=vmem,
        out_shape=jax.ShapeDtypeStruct((rank, n), jnp.float32),
        scratch_shapes=[
            pltpu.VMEM((2 * mine.shape[0], 128), jnp.float32),
            pltpu.VMEM((n, n), jnp.float32),
            pltpu.VMEM((rank, rank), jnp.float32),
            pltpu.VMEM((rank, rank), jnp.float32),
        ],
        compiler_params=pltpu.CompilerParams(vmem_limit_bytes=32 * MIB),
        name="iterate",
    )(place, mine, other, start)


def factor_kernel(block_ref, out_ref, work):
    block = block_ref[...]
    work[...] = dot(block, block, NT, HIGHEST)
    invert_factor(work, out_ref)


def last_factor(block):
    rank = block.shape[0]
    vmem = pl.BlockSpec(memory_space=pltpu.VMEM)
    return pl.pallas_call(
        factor_kernel,
        in_specs=[vmem],
        out_specs=vmem,
        out_shape=jax.ShapeDtypeStruct((rank, rank), jnp.float32),
        scratch_shapes=[pltpu.VMEM((rank, rank), jnp.float32)],
        compiler_params=pltpu.CompilerParams(vmem_limit_bytes=32 * MIB),
        name="last_factor",
    )(block)


def project_kernel(place_ref, x_ref, block_ref, *refs):
    outs, product = refs[:-1], refs[-1]
    per = 8 // len(outs)
    high, low = halves(x_ref[...])
    block_high, block_low = halves(block_ref[...])
    product[...] = (
        dot(high, block_high, NT) + dot(low, block_high, NT) + dot(high, block_low, NT)
    )
    fibres = x_ref.shape[0] // 8
    for k, out in enumerate(outs):
        to = place_ref[1] ^ k
        for j in range(per):
            out[pl.ds(j, fibres, stride=per), :] = product[pl.ds(to * per + j, fibres, stride=8), :]


def project(place, rows, block, slabs):
    n, rank = rows.shape[1], block.shape[0]
    tile = 512
    size = rows.shape[0] // slabs
    return pl.pallas_call(
        project_kernel,
        grid=(rows.shape[0] // tile,),
        in_specs=[
            pl.BlockSpec(memory_space=pltpu.SMEM),
            pl.BlockSpec((tile, n), lambda i: (i, 0)),
            pl.BlockSpec((rank, n), lambda i: (0, 0)),
        ],
        out_specs=[pl.BlockSpec((tile // slabs, rank), lambda i: (i, 0))] * slabs,
        out_shape=[jax.ShapeDtypeStruct((size, rank), jnp.float32)] * slabs,
        scratch_shapes=[pltpu.VMEM((tile, rank), jnp.float32)],
        compiler_params=pltpu.CompilerParams(vmem_limit_bytes=32 * MIB),
        name="project",
    )(place, rows, block)


def finish_kernel(place_ref, factor_ref, *refs):
    pieces, out = refs[:-1], refs[-1]
    factor = factor_ref[...]
    for k, piece in enumerate(pieces):
        out[0, place_ref[1] ^ k] = dot(piece[0], factor, NT, HIGHEST)


def finish(place, factor, pieces):
    slabs = len(pieces)
    nv, size, rank = pieces[0].shape
    return pl.pallas_call(
        finish_kernel,
        grid=(nv,),
        in_specs=[
            pl.BlockSpec(memory_space=pltpu.SMEM),
            pl.BlockSpec((rank, rank), lambda i: (0, 0)),
        ]
        + [pl.BlockSpec((1, size, rank), lambda i: (i, 0, 0))] * slabs,
        out_specs=pl.BlockSpec((1, slabs, size, rank), lambda i: (i, 0, 0, 0)),
        out_shape=jax.ShapeDtypeStruct((nv, slabs, size, rank), jnp.float32),
        compiler_params=pltpu.CompilerParams(vmem_limit_bytes=32 * MIB),
        name="finish",
    )(place, factor, *pieces)


def per_device(fields, start_basis):
    nv, n2, n3, n1 = fields.shape
    slabs = lax.axis_size("slab")
    slab = lax.axis_index("slab")
    place = jnp.stack([lax.axis_index("wide") * slabs + slab, slab]).astype(jnp.int32)
    rows = fields.reshape(-1, n1)
    count = float(rows.shape[0] * lax.axis_size("wide") * slabs)
    mine, other = sum_gram(*local_gram(place, rows, count))
    block = iterate(place, mine, other, start_basis)
    pieces = project(place, rows, block, slabs)
    pieces = [pieces[0]] + [exchange(pieces[k], "slab", k) for k in range(1, slabs)]
    factor = last_factor(block)
    out = finish(place, factor, [piece.reshape(nv, -1, piece.shape[1]) for piece in pieces])
    return out.reshape(nv, n2 * slabs, n3 // slabs, out.shape[-1])


def solution(mesh):
    in_specs = (P(None, "slab", "wide", None), P())
    out_specs = P(None, None, ("wide", "slab"), None)
    return jax.shard_map(
        per_device, mesh=mesh, in_specs=in_specs, out_specs=out_specs, check_vma=False
    )
```

time: 294 us -> 96.4 us (0.33); the launches traced: 290 us -> 96.2 us
  other arithmetic: 93.1 us -> 0.17 us
  waiting for transfers between devices: 117 us -> 31.8 us
  Pallas kernels: 0 us -> 42.5 us
  matrix products: 37.8 us -> 0 us
  blocking collectives: 28.3 us -> 0 us
  starting transfers between devices: 7.54 us -> 18.3 us
    another operation x20 -> x1, other arithmetic: 92 us -> 0.07 us  [per_device(): jnp.stack([lax.axis_index('wide') * slabs + slab, slab]).astype(jnp.int32)]
    ppermute x5 -> x13, waiting for transfers between devices: 117 us -> 31.8 us  [exchange(): return lax.ppermute(value, axes, [(i, i ^ mask) for i in range(size)])]
    pallas_call x0 -> x5, Pallas kernels: none -> 42.5 us  [the longest x1 19.9 us: iterate(): pl.pallas_call(functools.partial(sweep_kernel, SWEEPS), in_specs=[pl.Bloc...]
    dot_general x10 -> x0, matrix products: 36.1 us -> none  [the longest x1 17.5 us: per_device(): lax.dot_general(unfolded, unfolded, (((0,), (0,)), ((), ())), precision=l...]
    all_to_all x1 -> x0, blocking collectives: 28.3 us -> none  [per_device(): lax.all_to_all(projected, 'slab', split_axis=2, concat_axis=1, tiled=True)]
    ppermute x5 -> x13, starting transfers between devices: 7.54 us -> 18.3 us  [exchange(): return lax.ppermute(value, axes, [(i, i ^ mask) for i in range(size)])]
    unnamed x2 -> x6, local copies, waits for them, and re-layouts: 0.01 us -> 3.39 us
    all_to_all x2 -> x0, local copies, waits for them, and re-layouts: 3.16 us -> none  [per_device(): lax.all_to_all(projected, 'slab', split_axis=2, concat_axis=1, tiled=True)]
  transfers between devices with their start and end apart: 5 -> 13, of which waited for: 5 -> 12; matrix products, arithmetic and copies ran while one was open for 0% -> 0% of each run, Pallas kernels for 0% -> 5%
where the time goes in v1:
time: 96.4 us; the launch traced here: 96.2 us
  Pallas kernels  42.5 us (44%)
  waiting for transfers between devices  31.8 us (33%)
  starting transfers between devices  18.3 us (19%)
  local copies, waits for them, and re-layouts  3.41 us (4%)
    ppermute x13, waiting for transfers between devices, exchange(): return lax.ppermute(value, axes, [(i, i ^ mask) for i in range(size)])  31.8 us
    pallas_call x1, Pallas kernels, iterate(): pl.pallas_call(functools.partial(sweep_kernel, SWEEPS), in_specs=[pl.Bloc...  19.9 us
    ppermute x13, starting transfers between devices, exchange(): return lax.ppermute(value, axes, [(i, i ^ mask) for i in range(size)])  18.3 us
    pallas_call x1, Pallas kernels, local_gram(): pl.pallas_call(functools.partial(gram_kernel, 1.0 / count), grid=(rows.sh...  8.03 us
    pallas_call x1, Pallas kernels, project(): pl.pallas_call(project_kernel, grid=(rows.shape[0] // tile,), in_specs=[p...  5.82 us
    pallas_call x1, Pallas kernels, last_factor(): pl.pallas_call(factor_kernel, in_specs=[vmem], out_specs=vmem, out_shape=...  4.83 us
    pallas_call x1, Pallas kernels, finish(): pl.pallas_call(finish_kernel, grid=(nv,), in_specs=[pl.BlockSpec(memory_s...  3.93 us
    unnamed x6, local copies, waits for them, and re-layouts  3.39 us
  transfers between devices with their start and end apart: 13, of which 12 were waited for; matrix products, arithmetic and copies ran while one was open for 0% of the time, Pallas kernels for 5%

profile of v1, /device:TPU:1, one launch (start us, length us, event | category | flops | bytes accessed | tf_op | source)
XLA Modules:
  0.0 96.2 jit_solution(3899233162230698709)
XLA Ops:
  0.0 0.1 pad_add_fusion.place_ref
  0.1 0.0 copy-start
  0.1 3.4 %copy-done = f32[4,128,8,512]{3,2,1,0:T(8,128)S(1)} copy-done((f32[4,128,8,512]{3,2,1,0:T(8,128)S(1)}, f32[4,128,8,512]{3,2,1,0:T(8,128)}, u32[]{:S(2)}) %copy-start) | copy-done | bytes 8388632
  3.5 0.0 copy-start.2
  3.5 0.0 copy-start.1
  3.5 8.0 %local_gram.1 = (f32[640,128]{1,0:T(8,128)S(1)}, f32[640,128]{1,0:T(8,128)S(1)}) custom-call(s32[2]{0:T(128)S(1)} %pad_add_fusion.place_ref, f32[4096,512]{1,0:T(8,128)S(1)} %bitcast.8), custom_call_target="tpu_custom_call" | custom-call | tf_op jit(solution)/shard_map/local_gram/pallas_call | solution.py:82
  11.5 0.1 collective-permute-start
  11.6 1.6 %collective-permute-done = f32[640,128]{1,0:T(8,128)S(1)} collective-permute-done((f32[640,128]{1,0:T(8,128)S(1)}, f32[640,128]{1,0:T(8,128)S(1)}, u32[]{:S(2)}, u32[]{:S(2)}) %collective-permute-start) | collective-permute-done | bytes 327712 | tf_op jit(solution)/shard_map/ppermute | solution.py:32
  13.3 2.4 %collective-permute-start.1 = (f32[160,128]{1,0:T(8,128)S(1)}, f32[160,128]{1,0:T(8,128)S(1)}, u32[]{:S(2)}, u32[]{:S(2)}) collective-permute-start(f32[160,128]{1,0:T(8,128)S(1)} %get-tuple-element.17), channel_id=1, source_target_pairs={{0,2},{1,3},{2,0},{3,1},{4,6},{5,7},{6,4},{7,5},{8,10},{9,11},{10,... | collective-permute-start | bytes 245768 | tf_op jit(solution)/shard_map/ppermute | solution.py:32
  15.7 1.2 %collective-permute-start.3 = (f32[160,128]{1,0:T(8,128)S(1)}, f32[160,128]{1,0:T(8,128)S(1)}, u32[]{:S(2)}, u32[]{:S(2)}) collective-permute-start(f32[160,128]{1,0:T(8,128)S(1)} %get-tuple-element.18), channel_id=1, source_target_pairs={{0,6},{1,7},{2,4},{3,5},{4,2},{5,3},{6,0},{7,1},{8,14},{9,15},{10,... | collective-permute-start | bytes 245768 | tf_op jit(solution)/shard_map/ppermute | solution.py:32
  16.8 0.1 collective-permute-start.2
  17.0 1.3 %collective-permute-done.1 = f32[160,128]{1,0:T(8,128)S(1)} collective-permute-done((f32[160,128]{1,0:T(8,128)S(1)}, f32[160,128]{1,0:T(8,128)S(1)}, u32[]{:S(2)}, u32[]{:S(2)}) %collective-permute-start.1) | collective-permute-done | bytes 81952 | tf_op jit(solution)/shard_map/ppermute | solution.py:32
  18.2 1.7 %collective-permute-done.3 = f32[160,128]{1,0:T(8,128)S(1)} collective-permute-done((f32[160,128]{1,0:T(8,128)S(1)}, f32[160,128]{1,0:T(8,128)S(1)}, u32[]{:S(2)}, u32[]{:S(2)}) %collective-permute-start.3) | collective-permute-done | bytes 81952 | tf_op jit(solution)/shard_map/ppermute | solution.py:32
  19.9 1.0 %collective-permute-done.2 = f32[160,128]{1,0:T(8,128)S(1)} collective-permute-done((f32[160,128]{1,0:T(8,128)S(1)}, f32[160,128]{1,0:T(8,128)S(1)}, u32[]{:S(2)}, u32[]{:S(2)}) %collective-permute-start.2) | collective-permute-done | bytes 81952 | tf_op jit(solution)/shard_map/ppermute | solution.py:32
  20.9 1.8 %collective-permute-start.4 = (f32[160,128]{1,0:T(8,128)S(1)}, f32[160,128]{1,0:T(8,128)S(1)}, u32[]{:S(2)}, u32[]{:S(2)}) collective-permute-start(f32[160,128]{1,0:T(8,128)S(1)} %fusion.1), channel_id=1, source_target_pairs={{0,8},{1,9},{2,10},{3,11},{4,12},{5,13},{6,14},{7,15},{8,0},{9,1},... | collective-permute-start | bytes 245768 | tf_op jit(solution)/shard_map/ppermute | solution.py:32
  22.7 1.8 %collective-permute-done.4 = f32[160,128]{1,0:T(8,128)S(1)} collective-permute-done((f32[160,128]{1,0:T(8,128)S(1)}, f32[160,128]{1,0:T(8,128)S(1)}, u32[]{:S(2)}, u32[]{:S(2)}) %collective-permute-start.4) | collective-permute-done | bytes 81952 | tf_op jit(solution)/shard_map/ppermute | solution.py:32
  24.5 2.5 %collective-permute-start.5 = (f32[160,128]{1,0:T(8,128)S(1)}, f32[160,128]{1,0:T(8,128)S(1)}, u32[]{:S(2)}, u32[]{:S(2)}) collective-permute-start(f32[160,128]{1,0:T(8,128)S(1)} %add.26), channel_id=1, source_target_pairs={{0,16},{1,17},{2,18},{3,19},{4,20},{5,21},{6,22},{7,23},{8,24},{9,... | collective-permute-start | bytes 245768 | tf_op jit(solution)/shard_map/ppermute | solution.py:32
  27.1 1.8 %collective-permute-done.5 = f32[160,128]{1,0:T(8,128)S(1)} collective-permute-done((f32[160,128]{1,0:T(8,128)S(1)}, f32[160,128]{1,0:T(8,128)S(1)}, u32[]{:S(2)}, u32[]{:S(2)}) %collective-permute-start.5) | collective-permute-done | bytes 81952 | tf_op jit(solution)/shard_map/ppermute | solution.py:32
  28.9 1.7 %collective-permute-start.8 = (f32[160,128]{1,0:T(8,128)S(1)}, f32[160,128]{1,0:T(8,128)S(1)}, u32[]{:S(2)}, u32[]{:S(2)}) collective-permute-start(f32[160,128]{1,0:T(8,128)S(1)} %add.27), channel_id=1, source_target_pairs={{0,6},{1,7},{2,4},{3,5},{4,2},{5,3},{6,0},{7,1},{8,14},{9,15},{10,... | collective-permute-start | bytes 245768 | tf_op jit(solution)/shard_map/ppermute | solution.py:32
  30.6 0.8 collective-permute-start.7
  31.5 0.2 collective-permute-start.6
  31.6 1.5 %collective-permute-done.8 = f32[160,128]{1,0:T(8,128)S(1)} collective-permute-done((f32[160,128]{1,0:T(8,128)S(1)}, f32[160,128]{1,0:T(8,128)S(1)}, u32[]{:S(2)}, u32[]{:S(2)}) %collective-permute-start.8) | collective-permute-done | bytes 81952 | tf_op jit(solution)/shard_map/ppermute | solution.py:32
  33.2 1.0 %collective-permute-done.7 = f32[160,128]{1,0:T(8,128)S(1)} collective-permute-done((f32[160,128]{1,0:T(8,128)S(1)}, f32[160,128]{1,0:T(8,128)S(1)}, u32[]{:S(2)}, u32[]{:S(2)}) %collective-permute-start.7) | collective-permute-done | bytes 81952 | tf_op jit(solution)/shard_map/ppermute | solution.py:32
  34.2 0.6 collective-permute-done.6
  34.8 5.2 %collective-permute-start.9 = (f32[640,128]{1,0:T(8,128)S(1)}, f32[640,128]{1,0:T(8,128)S(1)}, u32[]{:S(2)}, u32[]{:S(2)}) collective-permute-start(f32[640,128]{1,0:T(8,128)S(1)} %pad_maximum_fusion.mine_ref), channel_id=1, source_target_pairs={{0,1},{1,0},{2,3},{3,2},{4,5},{5,4},{6,7},{7,6},{8,9},{9,8},{10,11... | collective-permute-start | bytes 983048 | tf_op jit(solution)/shard_map/ppermute | solution.py:32
  40.0 1.3 %collective-permute-done.9.other_ref = f32[640,128]{1,0:T(8,128)S(1)} collective-permute-done((f32[640,128]{1,0:T(8,128)S(1)}, f32[640,128]{1,0:T(8,128)S(1)}, u32[]{:S(2)}, u32[]{:S(2)}) %collective-permute-start.9) | collective-permute-done | bytes 327712 | tf_op jit(solution)/shard_map/ppermute | solution.py:32
  41.3 0.0 copy-done.2
  41.3 19.9 %iterate.1.block_ref = f32[128,512]{1,0:T(8,128)S(1)} custom-call(s32[2]{0:T(128)S(1)} %pad_add_fusion.place_ref, f32[640,128]{1,0:T(8,128)S(1)} %pad_maximum_fusion.mine_ref, f32[640,128]{1,0:T(8,128)S(1)} %collective-permute-done.9.other_ref, f32[512,128]{1,0:T(8,128)S(1)} %copy-done.2), custom_call_target="tpu_custom_call" | custom-call | tf_op jit(solution)/shard_map/iterate/pallas_call | solution.py:190
  61.2 0.0 copy-done.1
  61.2 5.8 %project.1 = (f32[1024,128]{1,0:T(8,128)S(1)}, f32[1024,128]{1,0:T(8,128)S(1)}, f32[1024,128]{1,0:T(8,128)S(1)}, f32[1024,128]{1,0:T(8,128)S(1)}) custom-call(s32[2]{0:T(128)S(1)} %pad_add_fusion.place_ref, f32[4096,512]{1,0:T(8,128)S(1)} %bitcast.9, f32[128,512]{1,0:T(8,128)S(1)} %iterate.1.block_ref), custom_call_target="tpu_custom_call" | custom-call | tf_op jit(solution)/shard_map/project/pallas_call | solution.py:245
  67.0 0.4 collective-permute-start.10
  67.4 0.2 collective-permute-start.11
  67.6 1.6 %collective-permute-start.12 = (f32[1024,128]{1,0:T(8,128)S(1)}, f32[1024,128]{1,0:T(8,128)S(1)}, u32[]{:S(2)}, u32[]{:S(2)}) collective-permute-start(f32[1024,128]{1,0:T(8,128)S(1)} %get-tuple-element.16), channel_id=1, source_target_pairs={{0,3},{1,2},{2,1},{3,0},{4,7},{5,6},{6,5},{7,4},{8,11},{9,10},{10,... | collective-permute-start | bytes 1572872 | tf_op jit(solution)/shard_map/ppermute | solution.py:32
  69.2 4.8 %last_factor.1.factor_ref = f32[128,128]{1,0:T(8,128)S(1)} custom-call(f32[128,512]{1,0:T(8,128)S(1)} %iterate.1.block_ref), custom_call_target="tpu_custom_call" | custom-call | tf_op jit(solution)/shard_map/last_factor/pallas_call | solution.py:215
  74.1 0.0 collective-permute-done.10
  74.1 6.7 %collective-permute-done.11 = f32[1024,128]{1,0:T(8,128)S(1)} collective-permute-done((f32[1024,128]{1,0:T(8,128)S(1)}, f32[1024,128]{1,0:T(8,128)S(1)}, u32[]{:S(2)}, u32[]{:S(2)}) %collective-permute-start.11) | collective-permute-done | bytes 524320 | tf_op jit(solution)/shard_map/ppermute | solution.py:32
  80.8 11.5 %collective-permute-done.12 = f32[1024,128]{1,0:T(8,128)S(1)} collective-permute-done((f32[1024,128]{1,0:T(8,128)S(1)}, f32[1024,128]{1,0:T(8,128)S(1)}, u32[]{:S(2)}, u32[]{:S(2)}) %collective-permute-start.12) | collective-permute-done | bytes 524320 | tf_op jit(solution)/shard_map/ppermute | solution.py:32
  92.3 3.9 %finish.1 = f32[4,4,256,128]{3,2,1,0:T(8,128)} custom-call(s32[2]{0:T(128)S(1)} %pad_add_fusion.place_ref, f32[128,128]{1,0:T(8,128)S(1)} %last_factor.1.factor_ref, f32[4,256,128]{2,1,0:T(8,128)S(1)} %bitcast.10, f32[4,256,128]{2,1,0:T(8,128)S(1)} %bitcast.11, f32[4,256,128]{2,1,0:T(8,128)S(1)} %bitcast.12, f32[4,256,128]{2,1,0:T(8,128)S(1)} %bitcast.13), custom_call_target="tpu_custom_call" | custom-call | tf_op jit(solution)/shard_map/finish/pallas_call | solution.py:271
  (6 shorter events, 0.1 us)
Async XLA Ops:
  0.1 3.4 %copy-start = (f32[4,128,8,512]{3,2,1,0:T(8,128)S(1)}, f32[4,128,8,512]{3,2,1,0:T(8,128)}, u32[]{:S(2)}) copy-start(f32[4,128,8,512]{3,2,1,0:T(8,128)} %param.2) | copy-start | bytes 25165828
  3.5 37.8 %copy-start.2 = (f32[512,128]{1,0:T(8,128)S(1)}, f32[512,128]{1,0:T(8,128)}, u32[]{:S(2)}) copy-start(f32[512,128]{1,0:T(8,128)} %start_ref.1) | copy-start | bytes 786436
  3.5 57.7 %copy-start.1 = (f32[4,128,8,512]{3,2,1,0:T(8,128)S(1)}, f32[4,128,8,512]{3,2,1,0:T(8,128)}, u32[]{:S(2)}) copy-start(f32[4,128,8,512]{3,2,1,0:T(8,128)} %param.2) | copy-start | bytes 25165828
  11.5 1.7 %collective-permute-start = (f32[640,128]{1,0:T(8,128)S(1)}, f32[640,128]{1,0:T(8,128)S(1)}, u32[]{:S(2)}, u32[]{:S(2)}) collective-permute-start(f32[640,128]{1,0:T(8,128)S(1)} %get-tuple-element.12), channel_id=1, source_target_pairs={{0,1},{1,0},{2,3},{3,2},{4,5},{5,4},{6,7},{7,6},{8,9},{9,8},{10,11... | collective-permute-start | bytes 983048 | tf_op jit(solution)/shard_map/ppermute | solution.py:32
  13.3 5.0 %collective-permute-start.1 = (f32[160,128]{1,0:T(8,128)S(1)}, f32[160,128]{1,0:T(8,128)S(1)}, u32[]{:S(2)}, u32[]{:S(2)}) collective-permute-start(f32[160,128]{1,0:T(8,128)S(1)} %get-tuple-element.17), channel_id=1, source_target_pairs={{0,2},{1,3},{2,0},{3,1},{4,6},{5,7},{6,4},{7,5},{8,10},{9,11},{10,... | collective-permute-start | bytes 245768 | tf_op jit(solution)/shard_map/ppermute | solution.py:32
  15.7 4.2 %collective-permute-start.3 = (f32[160,128]{1,0:T(8,128)S(1)}, f32[160,128]{1,0:T(8,128)S(1)}, u32[]{:S(2)}, u32[]{:S(2)}) collective-permute-start(f32[160,128]{1,0:T(8,128)S(1)} %get-tuple-element.18), channel_id=1, source_target_pairs={{0,6},{1,7},{2,4},{3,5},{4,2},{5,3},{6,0},{7,1},{8,14},{9,15},{10,... | collective-permute-start | bytes 245768 | tf_op jit(solution)/shard_map/ppermute | solution.py:32
  16.8 4.0 %collective-permute-start.2 = (f32[160,128]{1,0:T(8,128)S(1)}, f32[160,128]{1,0:T(8,128)S(1)}, u32[]{:S(2)}, u32[]{:S(2)}) collective-permute-start(f32[160,128]{1,0:T(8,128)S(1)} %get-tuple-element.19), channel_id=1, source_target_pairs={{0,4},{1,5},{2,6},{3,7},{4,0},{5,1},{6,2},{7,3},{8,12},{9,13},{10,... | collective-permute-start | bytes 245768 | tf_op jit(solution)/shard_map/ppermute | solution.py:32
  20.9 3.6 %collective-permute-start.4 = (f32[160,128]{1,0:T(8,128)S(1)}, f32[160,128]{1,0:T(8,128)S(1)}, u32[]{:S(2)}, u32[]{:S(2)}) collective-permute-start(f32[160,128]{1,0:T(8,128)S(1)} %fusion.1), channel_id=1, source_target_pairs={{0,8},{1,9},{2,10},{3,11},{4,12},{5,13},{6,14},{7,15},{8,0},{9,1},... | collective-permute-start | bytes 245768 | tf_op jit(solution)/shard_map/ppermute | solution.py:32
  24.5 4.4 %collective-permute-start.5 = (f32[160,128]{1,0:T(8,128)S(1)}, f32[160,128]{1,0:T(8,128)S(1)}, u32[]{:S(2)}, u32[]{:S(2)}) collective-permute-start(f32[160,128]{1,0:T(8,128)S(1)} %add.26), channel_id=1, source_target_pairs={{0,16},{1,17},{2,18},{3,19},{4,20},{5,21},{6,22},{7,23},{8,24},{9,... | collective-permute-start | bytes 245768 | tf_op jit(solution)/shard_map/ppermute | solution.py:32
  28.9 4.3 %collective-permute-start.8 = (f32[160,128]{1,0:T(8,128)S(1)}, f32[160,128]{1,0:T(8,128)S(1)}, u32[]{:S(2)}, u32[]{:S(2)}) collective-permute-start(f32[160,128]{1,0:T(8,128)S(1)} %add.27), channel_id=1, source_target_pairs={{0,6},{1,7},{2,4},{3,5},{4,2},{5,3},{6,0},{7,1},{8,14},{9,15},{10,... | collective-permute-start | bytes 245768 | tf_op jit(solution)/shard_map/ppermute | solution.py:32
  30.6 3.5 %collective-permute-start.7 = (f32[160,128]{1,0:T(8,128)S(1)}, f32[160,128]{1,0:T(8,128)S(1)}, u32[]{:S(2)}, u32[]{:S(2)}) collective-permute-start(f32[160,128]{1,0:T(8,128)S(1)} %add.27), channel_id=1, source_target_pairs={{0,4},{1,5},{2,6},{3,7},{4,0},{5,1},{6,2},{7,3},{8,12},{9,13},{10,... | collective-permute-start | bytes 245768 | tf_op jit(solution)/shard_map/ppermute | solution.py:32
  31.5 3.3 %collective-permute-start.6 = (f32[160,128]{1,0:T(8,128)S(1)}, f32[160,128]{1,0:T(8,128)S(1)}, u32[]{:S(2)}, u32[]{:S(2)}) collective-permute-start(f32[160,128]{1,0:T(8,128)S(1)} %add.27), channel_id=1, source_target_pairs={{0,2},{1,3},{2,0},{3,1},{4,6},{5,7},{6,4},{7,5},{8,10},{9,11},{10,... | collective-permute-start | bytes 245768 | tf_op jit(solution)/shard_map/ppermute | solution.py:32
  34.8 6.5 %collective-permute-start.9 = (f32[640,128]{1,0:T(8,128)S(1)}, f32[640,128]{1,0:T(8,128)S(1)}, u32[]{:S(2)}, u32[]{:S(2)}) collective-permute-start(f32[640,128]{1,0:T(8,128)S(1)} %pad_maximum_fusion.mine_ref), channel_id=1, source_target_pairs={{0,1},{1,0},{2,3},{3,2},{4,5},{5,4},{6,7},{7,6},{8,9},{9,8},{10,11... | collective-permute-start | bytes 983048 | tf_op jit(solution)/shard_map/ppermute | solution.py:32
  67.0 7.1 %collective-permute-start.10 = (f32[1024,128]{1,0:T(8,128)S(1)}, f32[1024,128]{1,0:T(8,128)S(1)}, u32[]{:S(2)}, u32[]{:S(2)}) collective-permute-start(f32[1024,128]{1,0:T(8,128)S(1)} %get-tuple-element.14), channel_id=1, source_target_pairs={{0,1},{1,0},{2,3},{3,2},{4,5},{5,4},{6,7},{7,6},{8,9},{9,8},{10,11... | collective-permute-start | bytes 1572872 | tf_op jit(solution)/shard_map/ppermute | solution.py:32
  67.4 13.4 %collective-permute-start.11 = (f32[1024,128]{1,0:T(8,128)S(1)}, f32[1024,128]{1,0:T(8,128)S(1)}, u32[]{:S(2)}, u32[]{:S(2)}) collective-permute-start(f32[1024,128]{1,0:T(8,128)S(1)} %get-tuple-element.15), channel_id=1, source_target_pairs={{0,2},{1,3},{2,0},{3,1},{4,6},{5,7},{6,4},{7,5},{8,10},{9,11},{10,... | collective-permute-start | bytes 1572872 | tf_op jit(solution)/shard_map/ppermute | solution.py:32
  67.6 24.7 %collective-permute-start.12 = (f32[1024,128]{1,0:T(8,128)S(1)}, f32[1024,128]{1,0:T(8,128)S(1)}, u32[]{:S(2)}, u32[]{:S(2)}) collective-permute-start(f32[1024,128]{1,0:T(8,128)S(1)} %get-tuple-element.16), channel_id=1, source_target_pairs={{0,3},{1,2},{2,1},{3,0},{4,7},{5,6},{6,5},{7,4},{8,11},{9,10},{10,... | collective-permute-start | bytes 1572872 | tf_op jit(solution)/shard_map/ppermute | solution.py:32

commit v2 on v1

v2 whole, which is shorter than its diff:
```python
import functools

import jax
import jax.numpy as jnp
from jax import lax
from jax.experimental import pallas as pl
from jax.experimental.pallas import tpu as pltpu
from jax.sharding import PartitionSpec as P

SWEEPS = 4
SLABS = 4
CHUNKS = 8
EARLY = (1, 2)
TILES = (1, 1, 2, 2, 2)
AXES = ("wide", "slab")
MIB = 1 << 20
HIGHEST = lax.Precision.HIGHEST
NN = (((1,), (0,)), ((), ()))
NT = (((1,), (1,)), ((), ()))
TN = (((0,), (0,)), ((), ()))
BRIEF = pl.CostEstimate(flops=1, bytes_accessed=1, transcendentals=0)


def dot(a, b, dims, precision=None):
    return lax.dot_general(a, b, dims, precision=precision, preferred_element_type=jnp.float32)


def halves(x):
    high = x.astype(jnp.bfloat16)
    return high, (x - high.astype(jnp.float32)).astype(jnp.bfloat16)


def exchange(value, axes, mask):
    size = 1
    for axis in axes if isinstance(axes, tuple) else (axes,):
        size *= lax.axis_size(axis)
    return lax.ppermute(value, axes, [(i, i ^ mask) for i in range(size)])


def upper_blocks(blocks):
    return [(i, j) for i in range(blocks) for j in range(i, blocks)]


def copies(x_ref, held, sems):
    tile = held.shape[1] // sems.shape[0]
    return [
        [
            pltpu.make_async_copy(
                x_ref.at[pl.ds(i * tile, tile), pl.ds(c * 128, 128)],
                held.at[c, pl.ds(i * tile, tile)],
                sems.at[i, c],
            )
            for c in range(held.shape[0])
        ]
        for i in range(sems.shape[0])
    ]


def side_by_side(ref, span):
    return jnp.concatenate([ref[c, span, :] for c in range(ref.shape[0])], axis=1)


def gram_kernel(scale, place_ref, x_ref, *refs):
    keep_ref, give_ref, held = refs[:3]
    early_refs = refs[3:-3]
    acc, whole, sems = refs[-3:]
    n = held.shape[0] * held.shape[2]
    half = n // 2
    arrivals = copies(x_ref, held, sems)
    for arrival in arrivals:
        for copy in arrival:
            copy.start()
    tile = held.shape[1] // len(arrivals)
    first = 0
    for count in TILES:
        for arrival in arrivals[first : first + count]:
            for copy in arrival:
                copy.wait()
        high, low = halves(side_by_side(held, pl.ds(first * tile, count * tile)))
        left = dot(high[:, :half], jnp.concatenate([high, low], axis=1), TN)
        right = dot(high[:, half:], jnp.concatenate([high[:, half:], low], axis=1), TN)
        if first == 0:
            acc[:half, :] = left
            acc[half:, half:] = right
        else:
            acc[:half, :] += left
            acc[half:, half:] += right
        first += count

    per = 8 // SLABS
    begin = 0
    for number, out in enumerate(early_refs):
        to = place_ref[1] ^ (number % 2 + 2)
        fibres = out.shape[1] // per
        for c in range(out.shape[0]):
            for j in range(per):
                out[c, pl.ds(j, fibres, stride=per), :] = held[
                    c, pl.ds(begin + to * per + j, fibres, stride=8), :
                ]
        begin += number % 2 * fibres * 8

    edge = 128
    for number, (i, j) in enumerate(upper_blocks(n // edge)):
        rows, columns = slice(i * edge, (i + 1) * edge), slice(j * edge, (j + 1) * edge)
        cross = acc[rows, n + j * edge : n + (j + 1) * edge]
        other = acc[columns, n + i * edge : n + (i + 1) * edge]
        whole[number * edge : (number + 1) * edge, :] = (
            acc[rows, columns] + cross + other.T
        ) * scale
    place = place_ref[0]
    part = keep_ref.shape[0] // 4
    for k in range(4):
        quarter = ((place >> 2) & 3) ^ k
        mine = pl.multiple_of(((place & 1) * 4 + quarter) * part, 8)
        theirs = pl.multiple_of(((1 - (place & 1)) * 4 + quarter) * part, 8)
        keep_ref[k * part : (k + 1) * part, :] = whole[pl.ds(mine, part), :]
        give_ref[k * part : (k + 1) * part, :] = whole[pl.ds(theirs, part), :]


def local_gram(place, rows, count, early):
    n = rows.shape[1]
    tall = len(upper_blocks(n // 128)) * 128
    half = jax.ShapeDtypeStruct((tall // 2, 128), jnp.float32)
    held = jax.ShapeDtypeStruct((n // 128, rows.shape[0], 128), jnp.float32)
    sent = [
        jax.ShapeDtypeStruct((n // 128, size // SLABS, 128), jnp.float32)
        for size in early
        for _ in range(2)
    ]
    vmem = pl.BlockSpec(memory_space=pltpu.VMEM)
    return pl.pallas_call(
        functools.partial(gram_kernel, 1.0 / count),
        in_specs=[pl.BlockSpec(memory_space=pltpu.SMEM), pl.BlockSpec(memory_space=pl.ANY)],
        out_specs=[vmem] * (3 + len(sent)),
        out_shape=[half, half, held, *sent],
        scratch_shapes=[
            pltpu.VMEM((n, 2 * n), jnp.float32),
            pltpu.VMEM((tall, 128), jnp.float32),
            pltpu.SemaphoreType.DMA((sum(TILES), n // 128)),
        ],
        cost_estimate=BRIEF,
        compiler_params=pltpu.CompilerParams(vmem_limit_bytes=40 * MIB),
        name="local_gram",
    )(place, rows)


def sum_gram(keep, give, send_back):
    size = lax.axis_size("wide") * lax.axis_size("slab")
    held = keep + exchange(give, AXES, 1)
    part = held.shape[0] // 4
    pieces = [held[k * part : (k + 1) * part] for k in range(4)]
    total = pieces[0]
    arrived = [exchange(pieces[k], AXES, 4 * k) for k in range(1, 4)]
    for piece in arrived:
        total = total + piece
    total = total + exchange(total, AXES, 2)
    total, extra = send_back(total)
    mask = 16
    while mask < size:
        total = total + exchange(total, AXES, mask)
        mask *= 2
    mine = jnp.concatenate([total] + [exchange(total, AXES, 4 * k) for k in range(1, 4)])
    mine, extra = lax.optimization_barrier((mine, extra))
    return mine, exchange(mine, AXES, 1), extra


def row_of(x, p):
    return jnp.broadcast_to(x[p : p + 1, :], x.shape)


def column_of(x, k):
    return jnp.broadcast_to(x[:, k : k + 1], x.shape)


def invert_factor(work, result):
    n = work.shape[0]
    lane = lax.broadcasted_iota(jnp.int32, (8, n), 1)
    sub = lax.broadcasted_iota(jnp.int32, (8, n), 0)
    for lo in range(0, n, 8):
        hi = lo + 8
        rows = work[lo:hi, :]
        columns = [column_of(rows, lo + k) for k in range(8)]
        rows = jnp.where((lane >= lo) & (lane < hi), (lane - lo == sub).astype(jnp.float32), rows)
        scaled = jnp.zeros((8, n), jnp.float32)
        for p in range(8):
            pivot = row_of(columns[p], p)
            inverse = 1.0 / pivot
            row = row_of(rows, p)
            here = sub == p
            scaled = jnp.where(here, row * lax.rsqrt(pivot), scaled)
            row = row * inverse
            rows = jnp.where(here, row, rows - columns[p] * row)
            for k in range(p + 1, 8):
                entry = row_of(columns[k], p) * inverse
                columns[k] = jnp.where(here, entry, columns[k] - columns[p] * entry)
        result[lo:hi, :] = jnp.where(lane <= sub + lo, scaled, 0.0)
        if hi < n:
            rest = work[hi:, :]
            lane_rest = lax.broadcasted_iota(jnp.int32, rest.shape, 1)
            update = jnp.where((lane_rest >= lo) & (lane_rest < hi), 0.0, rest)
            for k in range(8):
                update = update - column_of(rest, lo + k) * jnp.broadcast_to(
                    rows[k : k + 1, :], rest.shape
                )
            work[hi:, :] = update


def sweep_kernel(sweeps, place_ref, mine_ref, other_ref, start_ref, block_ref, blocks, gram, work, factor):
    place = place_ref[0]
    part = mine_ref.shape[0] // 4
    for k in range(4):
        quarter = ((place >> 2) & 3) ^ k
        mine = pl.multiple_of(((place & 1) * 4 + quarter) * part, 8)
        theirs = pl.multiple_of(((1 - (place & 1)) * 4 + quarter) * part, 8)
        blocks[pl.ds(mine, part), :] = mine_ref[k * part : (k + 1) * part, :]
        blocks[pl.ds(theirs, part), :] = other_ref[k * part : (k + 1) * part, :]
    edge = 128
    for number, (i, j) in enumerate(upper_blocks(gram.shape[0] // edge)):
        block = blocks[number * edge : (number + 1) * edge, :]
        gram[i * edge : (i + 1) * edge, j * edge : (j + 1) * edge] = block
        if i != j:
            gram[j * edge : (j + 1) * edge, i * edge : (i + 1) * edge] = block.T

    block_ref[...] = dot(start_ref[...].T, gram[...], NN, HIGHEST)

    def sweep(_, carry):
        block = block_ref[...]
        work[...] = dot(block, block, NT, HIGHEST)
        invert_factor(work, factor)
        basis = dot(factor[...], block, NN, HIGHEST)
        block_ref[...] = dot(basis, gram[...], NN, HIGHEST)
        return carry

    lax.fori_loop(0, sweeps - 1, sweep, 0)


def iterate(place, mine, other, start):
    n, rank = start.shape
    vmem = pl.BlockSpec(memory_space=pltpu.VMEM)
    return pl.pallas_call(
        functools.partial(sweep_kernel, SWEEPS),
        in_specs=[pl.BlockSpec(memory_space=pltpu.SMEM), vmem, vmem, vmem],
        out_specs=vmem,
        out_shape=jax.ShapeDtypeStruct((rank, n), jnp.float32),
        scratch_shapes=[
            pltpu.VMEM((2 * mine.shape[0], 128), jnp.float32),
            pltpu.VMEM((n, n), jnp.float32),
            pltpu.VMEM((rank, rank), jnp.float32),
            pltpu.VMEM((rank, rank), jnp.float32),
        ],
        cost_estimate=BRIEF,
        compiler_params=pltpu.CompilerParams(vmem_limit_bytes=16 * MIB),
        name="iterate",
    )(place, mine, other, start)


def factor_kernel(block_ref, out_ref, work):
    block = block_ref[...]
    work[...] = dot(block, block, NT, HIGHEST)
    invert_factor(work, out_ref)


def last_factor(block):
    rank = block.shape[0]
    vmem = pl.BlockSpec(memory_space=pltpu.VMEM)
    return pl.pallas_call(
        factor_kernel,
        in_specs=[vmem],
        out_specs=vmem,
        out_shape=jax.ShapeDtypeStruct((rank, rank), jnp.float32),
        scratch_shapes=[pltpu.VMEM((rank, rank), jnp.float32)],
        cost_estimate=BRIEF,
        compiler_params=pltpu.CompilerParams(vmem_limit_bytes=16 * MIB),
        name="last_factor",
    )(block)


def weights(block_ref):
    return jnp.concatenate(halves(block_ref[...]), axis=0)


def halved_product(x, both):
    high, low = halves(x)
    rank = both.shape[0] // 2
    product = dot(high, both, NT)
    return product[:, :rank] + product[:, rank:] + dot(low, both[:rank], NT)


def project_kernel(ranks, begins, place_ref, held, block_ref, *outs):
    per = 8 // SLABS
    both = weights(block_ref)
    for begin in sorted(set(begins)):
        some = [(k, out) for k, b, out in zip(ranks, begins, outs, strict=True) if b == begin]
        total = some[0][1].shape[0] // per
        fibres = total // pl.cdiv(total * len(some), 512)
        for first in range(0, total, fibres):
            picks = [
                pl.ds(begin + first * 8 + (place_ref[1] ^ k) * per + j, fibres, stride=8)
                for k, _ in some
                for j in range(per)
            ]
            x = jnp.concatenate([side_by_side(held, pick) for pick in picks], axis=0)
            product = halved_product(x, both)
            for number in range(len(picks)):
                out = some[number // per][1]
                place = pl.ds(first * per + number % per, fibres, stride=per)
                out[place, :] = product[number * fibres : (number + 1) * fibres]


def project(place, held, block, ranks, begins, name):
    rows, rank = held.shape[1], block.shape[0]
    vmem = pl.BlockSpec(memory_space=pltpu.VMEM)
    return pl.pallas_call(
        functools.partial(project_kernel, ranks, begins),
        in_specs=[pl.BlockSpec(memory_space=pltpu.SMEM), vmem, vmem],
        out_specs=[vmem] * len(ranks),
        out_shape=[
            jax.ShapeDtypeStruct(((rows - begin) // SLABS, rank), jnp.float32) for begin in begins
        ],
        cost_estimate=BRIEF,
        compiler_params=pltpu.CompilerParams(vmem_limit_bytes=16 * MIB),
        name=name,
    )(place, held, block)


def arrived_kernel(block_ref, *refs):
    outs = refs[-2:]
    each = (len(refs) - 2) // 2
    both = weights(block_ref)
    for k, out in enumerate(outs):
        begin = 0
        for x_ref in refs[k * each : (k + 1) * each]:
            size = x_ref.shape[1]
            x = side_by_side(x_ref, slice(None))
            out[begin : begin + size, :] = halved_product(x, both)
            begin += size


def project_arrived(block, arrived):
    vmem = pl.BlockSpec(memory_space=pltpu.VMEM)
    rows = sum(x.shape[1] for x in arrived) // 2
    return pl.pallas_call(
        arrived_kernel,
        in_specs=[vmem] * (1 + len(arrived)),
        out_specs=[vmem] * 2,
        out_shape=[jax.ShapeDtypeStruct((rows, block.shape[0]), jnp.float32)] * 2,
        cost_estimate=BRIEF,
        compiler_params=pltpu.CompilerParams(vmem_limit_bytes=16 * MIB),
        name="project_arrived",
    )(block, *arrived)


def finish_kernel(pair, first, place_ref, factor_ref, *refs):
    pieces = refs[:2]
    out, results, sems = refs[-3:]
    factor = factor_ref[...]
    per, size = out.shape[2], out.shape[3]
    count = results.shape[1]
    runs = []
    while sum(length for _, length in runs) < count:
        begin = first + sum(length for _, length in runs)
        runs.append((begin, min(per - begin % per, first + count - begin)))
    sends = []
    for k, piece in enumerate(pieces):
        results[k] = dot(piece[...], factor, NT, HIGHEST).reshape(results.shape[1:])
        for number, (begin, length) in enumerate(runs):
            send = pltpu.make_async_copy(
                results.at[k, pl.ds(begin - first, length)],
                out.at[begin // per, place_ref[1] ^ (2 * pair + k), pl.ds(begin % per, length)],
                sems.at[k, number],
            )
            send.start()
            sends.append(send)
    for send in sends:
        send.wait()


def finish(place, factor, pieces, pair, first, into, name):
    shape = into if isinstance(into, tuple) else into.shape
    size, rank = shape[3:]
    count = pieces[0].shape[0] // size
    vmem = pl.BlockSpec(memory_space=pltpu.VMEM)
    in_specs = [pl.BlockSpec(memory_space=pltpu.SMEM)] + [vmem] * 3
    operands = [place, factor, *pieces]
    aliases = {}
    if not isinstance(into, tuple):
        aliases = {len(operands): 0}
        in_specs.append(pl.BlockSpec(memory_space=pl.ANY))
        operands.append(into)
    return pl.pallas_call(
        functools.partial(finish_kernel, pair, first),
        in_specs=in_specs,
        out_specs=pl.BlockSpec(memory_space=pl.ANY),
        out_shape=jax.ShapeDtypeStruct(shape, jnp.float32),
        scratch_shapes=[
            pltpu.VMEM((2, count, size, rank), jnp.float32),
            pltpu.SemaphoreType.DMA((2, shape[0])),
        ],
        input_output_aliases=aliases,
        cost_estimate=BRIEF,
        compiler_params=pltpu.CompilerParams(vmem_limit_bytes=16 * MIB),
        name=name,
    )(*operands)


def per_device(fields, start_basis):
    nv, n2, n3, n1 = fields.shape
    slabs = lax.axis_size("slab")
    slab = lax.axis_index("slab")
    place = jnp.stack([lax.axis_index("wide") * slabs + slab, slab]).astype(jnp.int32)
    rows = fields.reshape(-1, n1)
    count = float(rows.shape[0] * lax.axis_size("wide") * slabs)
    early = [some * rows.shape[0] // CHUNKS for some in EARLY]

    keep, give, held, *sent = local_gram(place, rows, count, early)

    def first_early(total):
        total, *some = lax.optimization_barrier((total, *sent[:2]))
        return total, [exchange(x, "slab", 2 + k) for k, x in enumerate(some)]

    mine, other, arrived = sum_gram(keep, give, first_early)
    more, arrived = lax.optimization_barrier((sent[2:], arrived))
    more = [exchange(x, "slab", 2 + k) for k, x in enumerate(more)]
    arrived = [x for pair in zip(arrived, more, strict=True) for x in pair]
    block = iterate(place, mine, other, start_basis)

    late = sum(early)
    near, *far = project(place, held, block, (1, 2, 3), (0, late, late), "project_sent")
    block, near, *far = lax.optimization_barrier((block, near, *far))
    far = [exchange(x, "slab", 2 + k) for k, x in enumerate(far)]
    near = [*project(place, held, block, (0,), (0,), "project_own"), exchange(near, "slab", 1)]
    arrived = project_arrived(block, arrived)
    factor = last_factor(block)

    per = CHUNKS // nv
    out = (nv, slabs, per, n2 * n3 // slabs // per, block.shape[0])
    out = finish(place, factor, near, 0, 0, out, "finish_near")
    out = finish(place, factor, arrived, 1, 0, out, "finish_arrived")
    out = finish(place, factor, far, 1, sum(EARLY), out, "finish_far")
    return out.reshape(nv, n2 * slabs, n3 // slabs, out.shape[-1])


def solution(mesh):
    in_specs = (P(None, "slab", "wide", None), P())
    out_specs = P(None, None, ("wide", "slab"), None)
    return jax.shard_map(
        per_device, mesh=mesh, in_specs=in_specs, out_specs=out_specs, check_vma=False
    )
```

time: 96.4 us -> 80.9 us (0.84)
  waiting for transfers between devices: 31.8 us -> 17.3 us
  local copies, waits for them, and re-layouts: 3.41 us -> 0.02 us
  starting transfers between devices: 18.3 us -> 19.4 us
  Pallas kernels: 42.5 us -> 43.5 us
    ppermute x13 -> x17, waiting for transfers between devices: 31.8 us -> 17.3 us  [exchange(): return lax.ppermute(value, axes, [(i, i ^ mask) for i in range(size)])]
    unnamed x6 -> x2, local copies, waits for them, and re-layouts: 3.39 us -> 0.01 us
    ppermute x13 -> x17, starting transfers between devices: 18.3 us -> 19.4 us  [exchange(): return lax.ppermute(value, axes, [(i, i ^ mask) for i in range(size)])]
    pallas_call x3 -> x7, Pallas kernels: 17.8 us -> 18.6 us  [the longest x1 8.07 us: local_gram(): pl.pallas_call(functools.partial(gram_kernel, 1.0 / count), in_specs=[pl....]
  transfers between devices with their start and end apart: 13 -> 17, of which waited for: 12 -> 10; matrix products, arithmetic and copies ran while one was open for 0% -> 0% of each run, Pallas kernels for 5% -> 41%
where the time goes in v2:
time: 80.9 us; the launch traced here: 80.8 us
  Pallas kernels  43.5 us (54%)
  starting transfers between devices  19.4 us (24%)
  waiting for transfers between devices  17.3 us (21%)
    pallas_call x1, Pallas kernels, iterate(): pl.pallas_call(functools.partial(sweep_kernel, SWEEPS), in_specs=[pl.Bloc...  20 us
    ppermute x17, starting transfers between devices, exchange(): return lax.ppermute(value, axes, [(i, i ^ mask) for i in range(size)])  19.4 us
    ppermute x17, waiting for transfers between devices, exchange(): return lax.ppermute(value, axes, [(i, i ^ mask) for i in range(size)])  17.3 us
    pallas_call x1, Pallas kernels, local_gram(): pl.pallas_call(functools.partial(gram_kernel, 1.0 / count), in_specs=[pl....  8.07 us
    pallas_call x3, Pallas kernels, finish(): pl.pallas_call(functools.partial(finish_kernel, pair, first), in_specs=in...  6.52 us
    pallas_call x1, Pallas kernels, last_factor(): pl.pallas_call(factor_kernel, in_specs=[vmem], out_specs=vmem, out_shape=...  4.83 us
    pallas_call x2, Pallas kernels, project(): pl.pallas_call(functools.partial(project_kernel, ranks, begins), in_specs...  3.34 us
  transfers between devices with their start and end apart: 17, of which 10 were waited for; matrix products, arithmetic and copies ran while one was open for 0% of the time, Pallas kernels for 41%

profile of v2, /device:TPU:1, one launch (start us, length us, event | category | flops | bytes accessed | tf_op | source)
XLA Modules:
  0.0 80.8 jit_solution(16020084237601762319)
XLA Ops:
  0.0 0.1 pad_add_fusion.place_ref
  0.1 8.1 %local_gram.1 = (f32[640,128]{1,0:T(8,128)S(1)}, f32[640,128]{1,0:T(8,128)S(1)}, f32[4,4096,128]{2,1,0:T(8,128)S(1)}, f32[4,128,128]{2,1,0:T(8,128)S(1)}, f32[4,...) custom-call(s32[2]{0:T(128)S(1)} %pad_add_fusion.place_ref, f32[4096,512]{1,0:T(8,128)} %bitcast.4), custom_call_target="tpu_custom_call" | custom-call | flops 1 | bytes 1 | tf_op jit(solution)/shard_map/local_gram/pallas_call | solution.py:131
  8.2 0.0 copy-start
  8.2 0.1 collective-permute-start
  8.3 1.6 %collective-permute-done = f32[640,128]{1,0:T(8,128)S(1)} collective-permute-done((f32[640,128]{1,0:T(8,128)S(1)}, f32[640,128]{1,0:T(8,128)S(1)}, u32[]{:S(2)}, u32[]{:S(2)}) %collective-permute-start) | collective-permute-done | bytes 327712 | tf_op jit(solution)/shard_map/ppermute | solution.py:37
  9.9 2.4 %collective-permute-start.1 = (f32[160,128]{1,0:T(8,128)S(1)}, f32[160,128]{1,0:T(8,128)S(1)}, u32[]{:S(2)}, u32[]{:S(2)}) collective-permute-start(f32[160,128]{1,0:T(8,128)S(1)} %get-tuple-element.57), channel_id=1, source_target_pairs={{0,4},{1,5},{2,6},{3,7},{4,0},{5,1},{6,2},{7,3},{8,12},{9,13},{10,... | collective-permute-start | bytes 245768 | tf_op jit(solution)/shard_map/ppermute | solution.py:37
  12.3 1.3 %collective-permute-start.3 = (f32[160,128]{1,0:T(8,128)S(1)}, f32[160,128]{1,0:T(8,128)S(1)}, u32[]{:S(2)}, u32[]{:S(2)}) collective-permute-start(f32[160,128]{1,0:T(8,128)S(1)} %get-tuple-element.58), channel_id=1, source_target_pairs={{0,12},{1,13},{2,14},{3,15},{4,8},{5,9},{6,10},{7,11},{8,4},{9,5},... | collective-permute-start | bytes 245768 | tf_op jit(solution)/shard_map/ppermute | solution.py:37
  13.6 0.0 collective-permute-start.2
  13.6 1.2 %collective-permute-done.1 = f32[160,128]{1,0:T(8,128)S(1)} collective-permute-done((f32[160,128]{1,0:T(8,128)S(1)}, f32[160,128]{1,0:T(8,128)S(1)}, u32[]{:S(2)}, u32[]{:S(2)}) %collective-permute-start.1) | collective-permute-done | bytes 81952 | tf_op jit(solution)/shard_map/ppermute | solution.py:37
  14.9 1.7 %collective-permute-done.3 = f32[160,128]{1,0:T(8,128)S(1)} collective-permute-done((f32[160,128]{1,0:T(8,128)S(1)}, f32[160,128]{1,0:T(8,128)S(1)}, u32[]{:S(2)}, u32[]{:S(2)}) %collective-permute-start.3) | collective-permute-done | bytes 81952 | tf_op jit(solution)/shard_map/ppermute | solution.py:37
  16.5 1.0 %collective-permute-done.2 = f32[160,128]{1,0:T(8,128)S(1)} collective-permute-done((f32[160,128]{1,0:T(8,128)S(1)}, f32[160,128]{1,0:T(8,128)S(1)}, u32[]{:S(2)}, u32[]{:S(2)}) %collective-permute-start.2) | collective-permute-done | bytes 81952 | tf_op jit(solution)/shard_map/ppermute | solution.py:37
  17.6 1.7 %collective-permute-start.4 = (f32[160,128]{1,0:T(8,128)S(1)}, f32[160,128]{1,0:T(8,128)S(1)}, u32[]{:S(2)}, u32[]{:S(2)}) collective-permute-start(f32[160,128]{1,0:T(8,128)S(1)} %fusion.1), channel_id=1, source_target_pairs={{0,2},{1,3},{2,0},{3,1},{4,6},{5,7},{6,4},{7,5},{8,10},{9,11},{10,... | collective-permute-start | bytes 245768 | tf_op jit(solution)/shard_map/ppermute | solution.py:37
  19.3 1.8 %collective-permute-done.4 = f32[160,128]{1,0:T(8,128)S(1)} collective-permute-done((f32[160,128]{1,0:T(8,128)S(1)}, f32[160,128]{1,0:T(8,128)S(1)}, u32[]{:S(2)}, u32[]{:S(2)}) %collective-permute-start.4) | collective-permute-done | bytes 81952 | tf_op jit(solution)/shard_map/ppermute | solution.py:37
  21.2 2.6 %collective-permute-start.5 = (f32[160,128]{1,0:T(8,128)S(1)}, f32[160,128]{1,0:T(8,128)S(1)}, u32[]{:S(2)}, u32[]{:S(2)}) collective-permute-start(f32[160,128]{1,0:T(8,128)S(1)} %add.26), channel_id=1, source_target_pairs={{0,16},{1,17},{2,18},{3,19},{4,20},{5,21},{6,22},{7,23},{8,24},{9,... | collective-permute-start | bytes 245768 | tf_op jit(solution)/shard_map/ppermute | solution.py:37
  23.8 1.3 %collective-permute-start.9 = (f32[4,128,128]{2,1,0:T(8,128)S(1)}, f32[4,128,128]{2,1,0:T(8,128)S(1)}, u32[]{:S(2)}, u32[]{:S(2)}) collective-permute-start(f32[4,128,128]{2,1,0:T(8,128)S(1)} %get-tuple-element.36), channel_id=1, source_target_pairs={{0,2},{1,3},{2,0},{3,1},{4,6},{5,7},{6,4},{7,5},{8,10},{9,11},{10,... | collective-permute-start | bytes 786440 | tf_op jit(solution)/shard_map/ppermute | solution.py:37
  25.1 2.9 %collective-permute-start.10 = (f32[4,128,128]{2,1,0:T(8,128)S(1)}, f32[4,128,128]{2,1,0:T(8,128)S(1)}, u32[]{:S(2)}, u32[]{:S(2)}) collective-permute-start(f32[4,128,128]{2,1,0:T(8,128)S(1)} %get-tuple-element.37), channel_id=1, source_target_pairs={{0,3},{1,2},{2,1},{3,0},{4,7},{5,6},{6,5},{7,4},{8,11},{9,10},{10,... | collective-permute-start | bytes 786440 | tf_op jit(solution)/shard_map/ppermute | solution.py:37
  28.0 0.0 collective-permute-done.5
  28.0 2.1 %collective-permute-start.8 = (f32[160,128]{1,0:T(8,128)S(1)}, f32[160,128]{1,0:T(8,128)S(1)}, u32[]{:S(2)}, u32[]{:S(2)}) collective-permute-start(f32[160,128]{1,0:T(8,128)S(1)} %add.27), channel_id=1, source_target_pairs={{0,12},{1,13},{2,14},{3,15},{4,8},{5,9},{6,10},{7,11},{8,4},{9,5},... | collective-permute-start | bytes 245768 | tf_op jit(solution)/shard_map/ppermute | solution.py:37
  30.1 0.4 collective-permute-start.7
  30.4 0.3 collective-permute-start.6
  30.7 1.5 %collective-permute-done.8 = f32[160,128]{1,0:T(8,128)S(1)} collective-permute-done((f32[160,128]{1,0:T(8,128)S(1)}, f32[160,128]{1,0:T(8,128)S(1)}, u32[]{:S(2)}, u32[]{:S(2)}) %collective-permute-start.8) | collective-permute-done | bytes 81952 | tf_op jit(solution)/shard_map/ppermute | solution.py:37
  32.2 1.4 %collective-permute-done.7 = f32[160,128]{1,0:T(8,128)S(1)} collective-permute-done((f32[160,128]{1,0:T(8,128)S(1)}, f32[160,128]{1,0:T(8,128)S(1)}, u32[]{:S(2)}, u32[]{:S(2)}) %collective-permute-start.7) | collective-permute-done | bytes 81952 | tf_op jit(solution)/shard_map/ppermute | solution.py:37
  33.7 1.2 %collective-permute-done.6 = f32[160,128]{1,0:T(8,128)S(1)} collective-permute-done((f32[160,128]{1,0:T(8,128)S(1)}, f32[160,128]{1,0:T(8,128)S(1)}, u32[]{:S(2)}, u32[]{:S(2)}) %collective-permute-start.6) | collective-permute-done | bytes 81952 | tf_op jit(solution)/shard_map/ppermute | solution.py:37
  34.9 0.0 collective-permute-done.9.refs_0_
  34.9 2.7 %collective-permute-done.10.refs_2_ = f32[4,128,128]{2,1,0:T(8,128)S(1)} collective-permute-done((f32[4,128,128]{2,1,0:T(8,128)S(1)}, f32[4,128,128]{2,1,0:T(8,128)S(1)}, u32[]{:S(2)}, u32[]{:S(2)}) %collective-permute-start.10) | collective-permute-done | bytes 262176 | tf_op jit(solution)/shard_map/ppermute | solution.py:37
  37.6 0.0 collective-permute-start.11
  37.6 1.2 %collective-permute-start.14 = (f32[4,256,128]{2,1,0:T(8,128)S(1)}, f32[4,256,128]{2,1,0:T(8,128)S(1)}, u32[]{:S(2)}, u32[]{:S(2)}) collective-permute-start(f32[4,256,128]{2,1,0:T(8,128)S(1)} %get-tuple-element.51), channel_id=1, source_target_pairs={{0,2},{1,3},{2,0},{3,1},{4,6},{5,7},{6,4},{7,5},{8,10},{9,11},{10,... | collective-permute-start | bytes 1572872 | tf_op jit(solution)/shard_map/ppermute | solution.py:37
  38.8 1.0 %collective-permute-start.15 = (f32[4,256,128]{2,1,0:T(8,128)S(1)}, f32[4,256,128]{2,1,0:T(8,128)S(1)}, u32[]{:S(2)}, u32[]{:S(2)}) collective-permute-start(f32[4,256,128]{2,1,0:T(8,128)S(1)} %get-tuple-element.53), channel_id=1, source_target_pairs={{0,3},{1,2},{2,1},{3,0},{4,7},{5,6},{6,5},{7,4},{8,11},{9,10},{10,... | collective-permute-start | bytes 1572872 | tf_op jit(solution)/shard_map/ppermute | solution.py:37
  39.8 0.0 collective-permute-done.11.other_ref
  39.8 0.0 copy-done
  39.8 20.0 %iterate.1.block_ref = f32[128,512]{1,0:T(8,128)S(1)} custom-call(s32[2]{0:T(128)S(1)} %pad_add_fusion.place_ref, f32[640,128]{1,0:T(8,128)S(1)} %pad_maximum_fusion.mine_ref, f32[640,128]{1,0:T(8,128)S(1)} %collective-permute-done.11.other_ref, f32[512,128]{1,0:T(8,128)S(1)} %copy-done), custom_call_target="tpu_custom_call" | custom-call | flops 1 | bytes 1 | tf_op jit(solution)/shard_map/iterate/pallas_call | solution.py:240
  59.8 2.0 %project_sent.1 = (f32[1024,128]{1,0:T(8,128)S(1)}, f32[640,128]{1,0:T(8,128)S(1)}, f32[640,128]{1,0:T(8,128)S(1)}) custom-call(s32[2]{0:T(128)S(1)} %pad_add_fusion.place_ref, f32[4,4096,128]{2,1,0:T(8,128)S(1)} %get-tuple-element.39.held, f32[128,512]{1,0:T(8,128)S(1)} %iterate.1.block_ref), custom_call_target="tpu_custom_call" | custom-call | flops 1 | bytes 1 | tf_op jit(solution)/shard_map/project_sent/pallas_call | solution.py:313
  61.9 0.1 collective-permute-start.16
  61.9 1.2 %collective-permute-start.12 = (f32[640,128]{1,0:T(8,128)S(1)}, f32[640,128]{1,0:T(8,128)S(1)}, u32[]{:S(2)}, u32[]{:S(2)}) collective-permute-start(f32[640,128]{1,0:T(8,128)S(1)} %get-tuple-element.44), channel_id=1, source_target_pairs={{0,2},{1,3},{2,0},{3,1},{4,6},{5,7},{6,4},{7,5},{8,10},{9,11},{10,... | collective-permute-start | bytes 983048 | tf_op jit(solution)/shard_map/ppermute | solution.py:37
  63.2 0.9 %collective-permute-start.13 = (f32[640,128]{1,0:T(8,128)S(1)}, f32[640,128]{1,0:T(8,128)S(1)}, u32[]{:S(2)}, u32[]{:S(2)}) collective-permute-start(f32[640,128]{1,0:T(8,128)S(1)} %get-tuple-element.45), channel_id=1, source_target_pairs={{0,3},{1,2},{2,1},{3,0},{4,7},{5,6},{6,5},{7,4},{8,11},{9,10},{10,... | collective-permute-start | bytes 983048 | tf_op jit(solution)/shard_map/ppermute | solution.py:37
  64.1 1.3 %project_own.1.refs_0_ = f32[1024,128]{1,0:T(8,128)S(1)} custom-call(s32[2]{0:T(128)S(1)} %pad_add_fusion.place_ref, f32[4,4096,128]{2,1,0:T(8,128)S(1)} %get-tuple-element.39.held, f32[128,512]{1,0:T(8,128)S(1)} %iterate.1.block_ref), custom_call_target="tpu_custom_call" | custom-call | flops 1 | bytes 1 | tf_op jit(solution)/shard_map/project_own/pallas_call | solution.py:313
  65.4 4.8 %last_factor.1.factor_ref = f32[128,128]{1,0:T(8,128)S(1)} custom-call(f32[128,512]{1,0:T(8,128)S(1)} %iterate.1.block_ref), custom_call_target="tpu_custom_call" | custom-call | flops 1 | bytes 1 | tf_op jit(solution)/shard_map/last_factor/pallas_call | solution.py:266
  70.2 0.0 collective-permute-done.14.refs_1_
  70.2 0.0 collective-permute-done.15.refs_3_
  70.2 0.7 project_arrived.1
  71.0 0.0 collective-permute-done.16.refs_1_
  71.0 2.6 %finish_near.1.refs_2_ = f32[4,4,2,128,128]{4,3,2,1,0:T(8,128)} custom-call(s32[2]{0:T(128)S(1)} %pad_add_fusion.place_ref, f32[128,128]{1,0:T(8,128)S(1)} %last_factor.1.factor_ref, f32[1024,128]{1,0:T(8,128)S(1)} %project_own.1.refs_0_, f32[1024,128]{1,0:T(8,128)S(1)} %collective-permute-done.16.refs_1_), custom_call_target="tpu_custom_call" | custom-call | flops 1 | bytes 1 | tf_op jit(solution)/shard_map/finish_near/pallas_call | solution.py:390
  73.5 1.8 %finish_arrived.1.refs_2_ = f32[4,4,2,128,128]{4,3,2,1,0:T(8,128)} custom-call(s32[2]{0:T(128)S(1)} %pad_add_fusion.place_ref, f32[128,128]{1,0:T(8,128)S(1)} %last_factor.1.factor_ref, f32[384,128]{1,0:T(8,128)S(1)} %get-tuple-element.54.refs_0_, f32[384,128]{1,0:T(8,128)S(1)} %get-tuple-element.55.refs_1_, ...), custom_call_target="tpu_custom_call", output_to_operand_aliasing={{}: (4, {})} | custom-call | flops 1 | bytes 1 | tf_op jit(solution)/shard_map/finish_arrived/pallas_call | solution.py:390
  75.4 0.0 collective-permute-done.12.refs_0_
  75.4 3.1 %collective-permute-done.13.refs_1_ = f32[640,128]{1,0:T(8,128)S(1)} collective-permute-done((f32[640,128]{1,0:T(8,128)S(1)}, f32[640,128]{1,0:T(8,128)S(1)}, u32[]{:S(2)}, u32[]{:S(2)}) %collective-permute-start.13) | collective-permute-done | bytes 327712 | tf_op jit(solution)/shard_map/ppermute | solution.py:37
  78.5 2.1 %finish_far.1 = f32[4,4,2,128,128]{4,3,2,1,0:T(8,128)} custom-call(s32[2]{0:T(128)S(1)} %pad_add_fusion.place_ref, f32[128,128]{1,0:T(8,128)S(1)} %last_factor.1.factor_ref, f32[640,128]{1,0:T(8,128)S(1)} %collective-permute-done.12.refs_0_, f32[640,128]{1,0:T(8,128)S(1)} %collective-permute-done.13.refs_1_, ...), custom_call_target="tpu_custom_call", output_to_operand_aliasing={{}: (4, {})} | custom-call | flops 1 | bytes 1 | tf_op jit(solution)/shard_map/finish_far/pallas_call | solution.py:390
  (6 shorter events, 0.1 us)
Async XLA Ops:
  8.2 31.6 %copy-start = (f32[512,128]{1,0:T(8,128)S(1)}, f32[512,128]{1,0:T(8,128)}, u32[]{:S(2)}) copy-start(f32[512,128]{1,0:T(8,128)} %start_ref.1) | copy-start | bytes 786436
  8.2 1.7 %collective-permute-start = (f32[640,128]{1,0:T(8,128)S(1)}, f32[640,128]{1,0:T(8,128)S(1)}, u32[]{:S(2)}, u32[]{:S(2)}) collective-permute-start(f32[640,128]{1,0:T(8,128)S(1)} %get-tuple-element.32), channel_id=1, source_target_pairs={{0,1},{1,0},{2,3},{3,2},{4,5},{5,4},{6,7},{7,6},{8,9},{9,8},{10,11... | collective-permute-start | bytes 983048 | tf_op jit(solution)/shard_map/ppermute | solution.py:37
  9.9 4.9 %collective-permute-start.1 = (f32[160,128]{1,0:T(8,128)S(1)}, f32[160,128]{1,0:T(8,128)S(1)}, u32[]{:S(2)}, u32[]{:S(2)}) collective-permute-start(f32[160,128]{1,0:T(8,128)S(1)} %get-tuple-element.57), channel_id=1, source_target_pairs={{0,4},{1,5},{2,6},{3,7},{4,0},{5,1},{6,2},{7,3},{8,12},{9,13},{10,... | collective-permute-start | bytes 245768 | tf_op jit(solution)/shard_map/ppermute | solution.py:37
  12.3 4.2 %collective-permute-start.3 = (f32[160,128]{1,0:T(8,128)S(1)}, f32[160,128]{1,0:T(8,128)S(1)}, u32[]{:S(2)}, u32[]{:S(2)}) collective-permute-start(f32[160,128]{1,0:T(8,128)S(1)} %get-tuple-element.58), channel_id=1, source_target_pairs={{0,12},{1,13},{2,14},{3,15},{4,8},{5,9},{6,10},{7,11},{8,4},{9,5},... | collective-permute-start | bytes 245768 | tf_op jit(solution)/shard_map/ppermute | solution.py:37
  13.6 3.9 %collective-permute-start.2 = (f32[160,128]{1,0:T(8,128)S(1)}, f32[160,128]{1,0:T(8,128)S(1)}, u32[]{:S(2)}, u32[]{:S(2)}) collective-permute-start(f32[160,128]{1,0:T(8,128)S(1)} %get-tuple-element.59), channel_id=1, source_target_pairs={{0,8},{1,9},{2,10},{3,11},{4,12},{5,13},{6,14},{7,15},{8,0},{9,1},... | collective-permute-start | bytes 245768 | tf_op jit(solution)/shard_map/ppermute | solution.py:37
  17.6 3.6 %collective-permute-start.4 = (f32[160,128]{1,0:T(8,128)S(1)}, f32[160,128]{1,0:T(8,128)S(1)}, u32[]{:S(2)}, u32[]{:S(2)}) collective-permute-start(f32[160,128]{1,0:T(8,128)S(1)} %fusion.1), channel_id=1, source_target_pairs={{0,2},{1,3},{2,0},{3,1},{4,6},{5,7},{6,4},{7,5},{8,10},{9,11},{10,... | collective-permute-start | bytes 245768 | tf_op jit(solution)/shard_map/ppermute | solution.py:37
  21.2 6.8 %collective-permute-start.5 = (f32[160,128]{1,0:T(8,128)S(1)}, f32[160,128]{1,0:T(8,128)S(1)}, u32[]{:S(2)}, u32[]{:S(2)}) collective-permute-start(f32[160,128]{1,0:T(8,128)S(1)} %add.26), channel_id=1, source_target_pairs={{0,16},{1,17},{2,18},{3,19},{4,20},{5,21},{6,22},{7,23},{8,24},{9,... | collective-permute-start | bytes 245768 | tf_op jit(solution)/shard_map/ppermute | solution.py:37
  23.8 11.2 %collective-permute-start.9 = (f32[4,128,128]{2,1,0:T(8,128)S(1)}, f32[4,128,128]{2,1,0:T(8,128)S(1)}, u32[]{:S(2)}, u32[]{:S(2)}) collective-permute-start(f32[4,128,128]{2,1,0:T(8,128)S(1)} %get-tuple-element.36), channel_id=1, source_target_pairs={{0,2},{1,3},{2,0},{3,1},{4,6},{5,7},{6,4},{7,5},{8,10},{9,11},{10,... | collective-permute-start | bytes 786440 | tf_op jit(solution)/shard_map/ppermute | solution.py:37
  25.1 12.6 %collective-permute-start.10 = (f32[4,128,128]{2,1,0:T(8,128)S(1)}, f32[4,128,128]{2,1,0:T(8,128)S(1)}, u32[]{:S(2)}, u32[]{:S(2)}) collective-permute-start(f32[4,128,128]{2,1,0:T(8,128)S(1)} %get-tuple-element.37), channel_id=1, source_target_pairs={{0,3},{1,2},{2,1},{3,0},{4,7},{5,6},{6,5},{7,4},{8,11},{9,10},{10,... | collective-permute-start | bytes 786440 | tf_op jit(solution)/shard_map/ppermute | solution.py:37
  28.0 4.3 %collective-permute-start.8 = (f32[160,128]{1,0:T(8,128)S(1)}, f32[160,128]{1,0:T(8,128)S(1)}, u32[]{:S(2)}, u32[]{:S(2)}) collective-permute-start(f32[160,128]{1,0:T(8,128)S(1)} %add.27), channel_id=1, source_target_pairs={{0,12},{1,13},{2,14},{3,15},{4,8},{5,9},{6,10},{7,11},{8,4},{9,5},... | collective-permute-start | bytes 245768 | tf_op jit(solution)/shard_map/ppermute | solution.py:37
  30.1 3.6 %collective-permute-start.7 = (f32[160,128]{1,0:T(8,128)S(1)}, f32[160,128]{1,0:T(8,128)S(1)}, u32[]{:S(2)}, u32[]{:S(2)}) collective-permute-start(f32[160,128]{1,0:T(8,128)S(1)} %add.27), channel_id=1, source_target_pairs={{0,8},{1,9},{2,10},{3,11},{4,12},{5,13},{6,14},{7,15},{8,0},{9,1},... | collective-permute-start | bytes 245768 | tf_op jit(solution)/shard_map/ppermute | solution.py:37
  30.4 4.5 %collective-permute-start.6 = (f32[160,128]{1,0:T(8,128)S(1)}, f32[160,128]{1,0:T(8,128)S(1)}, u32[]{:S(2)}, u32[]{:S(2)}) collective-permute-start(f32[160,128]{1,0:T(8,128)S(1)} %add.27), channel_id=1, source_target_pairs={{0,4},{1,5},{2,6},{3,7},{4,0},{5,1},{6,2},{7,3},{8,12},{9,13},{10,... | collective-permute-start | bytes 245768 | tf_op jit(solution)/shard_map/ppermute | solution.py:37
  37.6 2.1 %collective-permute-start.11 = (f32[640,128]{1,0:T(8,128)S(1)}, f32[640,128]{1,0:T(8,128)S(1)}, u32[]{:S(2)}, u32[]{:S(2)}) collective-permute-start(f32[640,128]{1,0:T(8,128)S(1)} %pad_maximum_fusion.mine_ref), channel_id=1, source_target_pairs={{0,1},{1,0},{2,3},{3,2},{4,5},{5,4},{6,7},{7,6},{8,9},{9,8},{10,11... | collective-permute-start | bytes 983048 | tf_op jit(solution)/shard_map/ppermute | solution.py:37
  37.6 32.6 %collective-permute-start.14 = (f32[4,256,128]{2,1,0:T(8,128)S(1)}, f32[4,256,128]{2,1,0:T(8,128)S(1)}, u32[]{:S(2)}, u32[]{:S(2)}) collective-permute-start(f32[4,256,128]{2,1,0:T(8,128)S(1)} %get-tuple-element.51), channel_id=1, source_target_pairs={{0,2},{1,3},{2,0},{3,1},{4,6},{5,7},{6,4},{7,5},{8,10},{9,11},{10,... | collective-permute-start | bytes 1572872 | tf_op jit(solution)/shard_map/ppermute | solution.py:37
  38.8 31.4 %collective-permute-start.15 = (f32[4,256,128]{2,1,0:T(8,128)S(1)}, f32[4,256,128]{2,1,0:T(8,128)S(1)}, u32[]{:S(2)}, u32[]{:S(2)}) collective-permute-start(f32[4,256,128]{2,1,0:T(8,128)S(1)} %get-tuple-element.53), channel_id=1, source_target_pairs={{0,3},{1,2},{2,1},{3,0},{4,7},{5,6},{6,5},{7,4},{8,11},{9,10},{10,... | collective-permute-start | bytes 1572872 | tf_op jit(solution)/shard_map/ppermute | solution.py:37
  61.9 9.1 %collective-permute-start.16 = (f32[1024,128]{1,0:T(8,128)S(1)}, f32[1024,128]{1,0:T(8,128)S(1)}, u32[]{:S(2)}, u32[]{:S(2)}) collective-permute-start(f32[1024,128]{1,0:T(8,128)S(1)} %get-tuple-element.56), channel_id=1, source_target_pairs={{0,1},{1,0},{2,3},{3,2},{4,5},{5,4},{6,7},{7,6},{8,9},{9,8},{10,11... | collective-permute-start | bytes 1572872 | tf_op jit(solution)/shard_map/ppermute | solution.py:37
  61.9 13.4 %collective-permute-start.12 = (f32[640,128]{1,0:T(8,128)S(1)}, f32[640,128]{1,0:T(8,128)S(1)}, u32[]{:S(2)}, u32[]{:S(2)}) collective-permute-start(f32[640,128]{1,0:T(8,128)S(1)} %get-tuple-element.44), channel_id=1, source_target_pairs={{0,2},{1,3},{2,0},{3,1},{4,6},{5,7},{6,4},{7,5},{8,10},{9,11},{10,... | collective-permute-start | bytes 983048 | tf_op jit(solution)/shard_map/ppermute | solution.py:37
  63.2 15.3 %collective-permute-start.13 = (f32[640,128]{1,0:T(8,128)S(1)}, f32[640,128]{1,0:T(8,128)S(1)}, u32[]{:S(2)}, u32[]{:S(2)}) collective-permute-start(f32[640,128]{1,0:T(8,128)S(1)} %get-tuple-element.45), channel_id=1, source_target_pairs={{0,3},{1,2},{2,1},{3,0},{4,7},{5,6},{6,5},{7,4},{8,11},{9,10},{10,... | collective-permute-start | bytes 983048 | tf_op jit(solution)/shard_map/ppermute | solution.py:37

commit v3 on v2

--- a/solution.py
+++ b/solution.py
@@ -9,8 +9,8 @@
 
 SWEEPS = 4
 SLABS = 4
-CHUNKS = 8
-EARLY = (1, 2)
+CHUNKS = 16
+EARLY = 4
 TILES = (1, 1, 2, 2, 2)
 AXES = ("wide", "slab")
 MIB = 1 << 20
@@ -88,16 +88,14 @@
         first += count
 
     per = 8 // SLABS
-    begin = 0
     for number, out in enumerate(early_refs):
-        to = place_ref[1] ^ (number % 2 + 2)
+        to = place_ref[1] ^ (number + 2)
         fibres = out.shape[1] // per
         for c in range(out.shape[0]):
             for j in range(per):
                 out[c, pl.ds(j, fibres, stride=per), :] = held[
-                    c, pl.ds(begin + to * per + j, fibres, stride=8), :
+                    c, pl.ds(to * per + j, fibres, stride=8), :
                 ]
-        begin += number % 2 * fibres * 8
 
     edge = 128
     for number, (i, j) in enumerate(upper_blocks(n // edge)):
@@ -122,17 +120,13 @@
     tall = len(upper_blocks(n // 128)) * 128
     half = jax.ShapeDtypeStruct((tall // 2, 128), jnp.float32)
     held = jax.ShapeDtypeStruct((n // 128, rows.shape[0], 128), jnp.float32)
-    sent = [
-        jax.ShapeDtypeStruct((n // 128, size // SLABS, 128), jnp.float32)
-        for size in early
-        for _ in range(2)
-    ]
+    sent = jax.ShapeDtypeStruct((n // 128, early // SLABS, 128), jnp.float32)
     vmem = pl.BlockSpec(memory_space=pltpu.VMEM)
     return pl.pallas_call(
         functools.partial(gram_kernel, 1.0 / count),
         in_specs=[pl.BlockSpec(memory_space=pltpu.SMEM), pl.BlockSpec(memory_space=pl.ANY)],
-        out_specs=[vmem] * (3 + len(sent)),
-        out_shape=[half, half, held, *sent],
+        out_specs=[vmem] * 5,
+        out_shape=[half, half, held, sent, sent],
         scratch_shapes=[
             pltpu.VMEM((n, 2 * n), jnp.float32),
             pltpu.VMEM((tall, 128), jnp.float32),
@@ -144,7 +138,7 @@
     )(place, rows)
 
 
-def sum_gram(keep, give, send_back):
+def sum_gram(keep, give, sent):
     size = lax.axis_size("wide") * lax.axis_size("slab")
     held = keep + exchange(give, AXES, 1)
     part = held.shape[0] // 4
@@ -154,14 +148,13 @@
     for piece in arrived:
         total = total + piece
     total = total + exchange(total, AXES, 2)
-    total, extra = send_back(total)
+    total, *sent = lax.optimization_barrier((total, *sent))
     mask = 16
     while mask < size:
         total = total + exchange(total, AXES, mask)
         mask *= 2
     mine = jnp.concatenate([total] + [exchange(total, AXES, 4 * k) for k in range(1, 4)])
-    mine, extra = lax.optimization_barrier((mine, extra))
-    return mine, exchange(mine, AXES, 1), extra
+    return mine, exchange(mine, AXES, 1), sent
 
 
 def row_of(x, p):
@@ -170,42 +163,74 @@
 
 def column_of(x, k):
     return jnp.broadcast_to(x[:, k : k + 1], x.shape)
+
+
+def total(terms):
+    while len(terms) > 1:
+        odd = terms[len(terms) & ~1 :]
+        terms = [x + y for x, y in zip(terms[::2], terms[1::2], strict=False)] + odd
+    return terms[0]
 
 
 def invert_factor(work, result):
     n = work.shape[0]
     lane = lax.broadcasted_iota(jnp.int32, (8, n), 1)
     sub = lax.broadcasted_iota(jnp.int32, (8, n), 0)
+    columns = [column_of(work[:8, :], k) for k in range(8)]
     for lo in range(0, n, 8):
         hi = lo + 8
         rows = work[lo:hi, :]
-        columns = [column_of(rows, lo + k) for k in range(8)]
+        if hi < n:
+            rest = work[hi:, :]
+            factors = [column_of(rest, lo + k) for k in range(8)]
+            across = [column_of(rows, hi + k) for k in range(8)]
+            later = [column_of(rest[:8], hi + k) for k in range(8)]
+            under = [x[:8] for x in factors]
         rows = jnp.where((lane >= lo) & (lane < hi), (lane - lo == sub).astype(jnp.float32), rows)
         scaled = jnp.zeros((8, n), jnp.float32)
         for p in range(8):
-            pivot = row_of(columns[p], p)
+            here = sub == p
+            column = columns[p]
+            pivot = row_of(column, p)
             inverse = 1.0 / pivot
             row = row_of(rows, p)
-            here = sub == p
             scaled = jnp.where(here, row * lax.rsqrt(pivot), scaled)
             row = row * inverse
-            rows = jnp.where(here, row, rows - columns[p] * row)
-            for k in range(p + 1, 8):
-                entry = row_of(columns[k], p) * inverse
-                columns[k] = jnp.where(here, entry, columns[k] - columns[p] * entry)
+            rows = jnp.where(here, row, rows - column * row)
+            for k in range(8 if hi < n else 0):
+                if k == p:
+                    continue
+                entry = row_of(columns[k], p)
+                if k == p + 1:
+                    kept = jnp.where(here, 0.0, columns[k])
+                    columns[k] = kept - jnp.where(here, -entry, column * entry) * inverse
+                else:
+                    columns[k] = jnp.where(here, entry * inverse, columns[k] - column * (entry * inverse))
+                under[k] = under[k] - under[p] * (entry * inverse)
+            if hi < n:
+                columns[p] = jnp.where(here, inverse, -column * inverse)
+                under[p] = -under[p] * inverse
+            else:
+                for k in range(p + 1, 8):
+                    entry = row_of(columns[k], p) * inverse
+                    columns[k] = jnp.where(here, entry, columns[k] - column * entry)
         result[lo:hi, :] = jnp.where(lane <= sub + lo, scaled, 0.0)
         if hi < n:
-            rest = work[hi:, :]
+            columns = [
+                later[k] + total([under[p] * row_of(across[k], p) for p in range(8)])
+                for k in range(8)
+            ]
             lane_rest = lax.broadcasted_iota(jnp.int32, rest.shape, 1)
-            update = jnp.where((lane_rest >= lo) & (lane_rest < hi), 0.0, rest)
-            for k in range(8):
-                update = update - column_of(rest, lo + k) * jnp.broadcast_to(
-                    rows[k : k + 1, :], rest.shape
-                )
-            work[hi:, :] = update
-
-
-def sweep_kernel(sweeps, place_ref, mine_ref, other_ref, start_ref, block_ref, blocks, gram, work, factor):
+            kept = jnp.where((lane_rest >= lo) & (lane_rest < hi), 0.0, rest)
+            work[hi:, :] = kept - total(
+                [factors[k] * jnp.broadcast_to(rows[k : k + 1, :], rest.shape) for k in range(8)]
+            )
+
+
+def sweep_kernel(
+    sweeps, place_ref, mine_ref, other_ref, start_ref, block_ref, blocks, gram, gram_high, gram_low,
+    ahead, work, factor,
+):
     place = place_ref[0]
     part = mine_ref.shape[0] // 4
     for k in range(4):
@@ -221,14 +246,22 @@
         if i != j:
             gram[j * edge : (j + 1) * edge, i * edge : (i + 1) * edge] = block.T
 
-    block_ref[...] = dot(start_ref[...].T, gram[...], NN, HIGHEST)
+    gram_high[...], gram_low[...] = halves(gram[...])
+
+    def by_gram(block):
+        high, low = halves(block)
+        both = dot(jnp.concatenate([high, low], axis=0), gram_high[...], NN)
+        rank = block.shape[0]
+        return both[:rank] + both[rank:] + dot(high, gram_low[...], NN)
+
+    block_ref[...] = by_gram(start_ref[...].T)
 
     def sweep(_, carry):
         block = block_ref[...]
         work[...] = dot(block, block, NT, HIGHEST)
+        ahead[...] = by_gram(block)
         invert_factor(work, factor)
-        basis = dot(factor[...], block, NN, HIGHEST)
-        block_ref[...] = dot(basis, gram[...], NN, HIGHEST)
+        block_ref[...] = dot(factor[...], ahead[...], NN, HIGHEST)
         return carry
 
     lax.fori_loop(0, sweeps - 1, sweep, 0)
@@ -245,6 +278,9 @@
         scratch_shapes=[
             pltpu.VMEM((2 * mine.shape[0], 128), jnp.float32),
             pltpu.VMEM((n, n), jnp.float32),
+            pltpu.VMEM((n, n), jnp.bfloat16),
+            pltpu.VMEM((n, n), jnp.bfloat16),
+            pltpu.VMEM((rank, n), jnp.float32),
             pltpu.VMEM((rank, rank), jnp.float32),
             pltpu.VMEM((rank, rank), jnp.float32),
         ],
@@ -324,34 +360,27 @@
 
 
 def arrived_kernel(block_ref, *refs):
-    outs = refs[-2:]
-    each = (len(refs) - 2) // 2
     both = weights(block_ref)
-    for k, out in enumerate(outs):
-        begin = 0
-        for x_ref in refs[k * each : (k + 1) * each]:
-            size = x_ref.shape[1]
-            x = side_by_side(x_ref, slice(None))
-            out[begin : begin + size, :] = halved_product(x, both)
-            begin += size
+    half = len(refs) // 2
+    for x_ref, out in zip(refs[:half], refs[half:], strict=True):
+        out[...] = halved_product(side_by_side(x_ref, slice(None)), both)
 
 
 def project_arrived(block, arrived):
     vmem = pl.BlockSpec(memory_space=pltpu.VMEM)
-    rows = sum(x.shape[1] for x in arrived) // 2
     return pl.pallas_call(
         arrived_kernel,
         in_specs=[vmem] * (1 + len(arrived)),
-        out_specs=[vmem] * 2,
-        out_shape=[jax.ShapeDtypeStruct((rows, block.shape[0]), jnp.float32)] * 2,
+        out_specs=[vmem] * len(arrived),
+        out_shape=[jax.ShapeDtypeStruct((x.shape[1], block.shape[0]), jnp.float32) for x in arrived],
         cost_estimate=BRIEF,
         compiler_params=pltpu.CompilerParams(vmem_limit_bytes=16 * MIB),
         name="project_arrived",
     )(block, *arrived)
 
 
-def finish_kernel(pair, first, place_ref, factor_ref, *refs):
-    pieces = refs[:2]
+def finish_kernel(ranks, first, place_ref, factor_ref, *refs):
+    pieces = refs[: len(ranks)]
     out, results, sems = refs[-3:]
     factor = factor_ref[...]
     per, size = out.shape[2], out.shape[3]
@@ -361,12 +390,14 @@
         begin = first + sum(length for _, length in runs)
         runs.append((begin, min(per - begin % per, first + count - begin)))
     sends = []
-    for k, piece in enumerate(pieces):
-        results[k] = dot(piece[...], factor, NT, HIGHEST).reshape(results.shape[1:])
+    for k, (rank, piece) in enumerate(zip(ranks, pieces, strict=True)):
         for number, (begin, length) in enumerate(runs):
+            span = pl.ds(begin - first, length)
+            rows = piece[(begin - first) * size : (begin - first + length) * size, :]
+            results[k, span] = dot(rows, factor, NT, HIGHEST).reshape(length, size, -1)
             send = pltpu.make_async_copy(
-                results.at[k, pl.ds(begin - first, length)],
-                out.at[begin // per, place_ref[1] ^ (2 * pair + k), pl.ds(begin % per, length)],
+                results.at[k, span],
+                out.at[begin // per, place_ref[1] ^ rank, pl.ds(begin % per, length)],
                 sems.at[k, number],
             )
             send.start()
@@ -375,12 +406,12 @@
         send.wait()
 
 
-def finish(place, factor, pieces, pair, first, into, name):
+def finish(place, factor, pieces, ranks, first, into, name):
     shape = into if isinstance(into, tuple) else into.shape
     size, rank = shape[3:]
     count = pieces[0].shape[0] // size
     vmem = pl.BlockSpec(memory_space=pltpu.VMEM)
-    in_specs = [pl.BlockSpec(memory_space=pltpu.SMEM)] + [vmem] * 3
+    in_specs = [pl.BlockSpec(memory_space=pltpu.SMEM)] + [vmem] * (1 + len(pieces))
     operands = [place, factor, *pieces]
     aliases = {}
     if not isinstance(into, tuple):
@@ -388,13 +419,13 @@
         in_specs.append(pl.BlockSpec(memory_space=pl.ANY))
         operands.append(into)
     return pl.pallas_call(
-        functools.partial(finish_kernel, pair, first),
+        functools.partial(finish_kernel, ranks, first),
         in_specs=in_specs,
         out_specs=pl.BlockSpec(memory_space=pl.ANY),
         out_shape=jax.ShapeDtypeStruct(shape, jnp.float32),
         scratch_shapes=[
-            pltpu.VMEM((2, count, size, rank), jnp.float32),
-            pltpu.SemaphoreType.DMA((2, shape[0])),
+            pltpu.VMEM((len(pieces), count, size, rank), jnp.float32),
+            pltpu.SemaphoreType.DMA((len(pieces), shape[0])),
         ],
         input_output_aliases=aliases,
         cost_estimate=BRIEF,
@@ -410,33 +441,31 @@
     place = jnp.stack([lax.axis_index("wide") * slabs + slab, slab]).astype(jnp.int32)
     rows = fields.reshape(-1, n1)
     count = float(rows.shape[0] * lax.axis_size("wide") * slabs)
-    early = [some * rows.shape[0] // CHUNKS for some in EARLY]
+    early = EARLY * rows.shape[0] // CHUNKS
+
+    def to_far(some):
+        return [exchange(x, "slab", 2 + k) for k, x in enumerate(some)]
 
     keep, give, held, *sent = local_gram(place, rows, count, early)
-
-    def first_early(total):
-        total, *some = lax.optimization_barrier((total, *sent[:2]))
-        return total, [exchange(x, "slab", 2 + k) for k, x in enumerate(some)]
-
-    mine, other, arrived = sum_gram(keep, give, first_early)
-    more, arrived = lax.optimization_barrier((sent[2:], arrived))
-    more = [exchange(x, "slab", 2 + k) for k, x in enumerate(more)]
-    arrived = [x for pair in zip(arrived, more, strict=True) for x in pair]
+    mine, other, sent = sum_gram(keep, give, sent)
+    arrived = to_far(sent)
     block = iterate(place, mine, other, start_basis)
 
-    late = sum(early)
-    near, *far = project(place, held, block, (1, 2, 3), (0, late, late), "project_sent")
+    block, *arrived = lax.optimization_barrier((block, *arrived))
+    near, *far = project(place, held, block, (1, 2, 3), (0, early, early), "project_sent")
     block, near, *far = lax.optimization_barrier((block, near, *far))
-    far = [exchange(x, "slab", 2 + k) for k, x in enumerate(far)]
-    near = [*project(place, held, block, (0,), (0,), "project_own"), exchange(near, "slab", 1)]
+    far = to_far(far)
+    near = exchange(near, "slab", 1)
+    (own,) = project(place, held, block, (0,), (0,), "project_own")
     arrived = project_arrived(block, arrived)
     factor = last_factor(block)
 
     per = CHUNKS // nv
     out = (nv, slabs, per, n2 * n3 // slabs // per, block.shape[0])
-    out = finish(place, factor, near, 0, 0, out, "finish_near")
-    out = finish(place, factor, arrived, 1, 0, out, "finish_arrived")
-    out = finish(place, factor, far, 1, sum(EARLY), out, "finish_far")
+    out = finish(place, factor, arrived, (2, 3), 0, out, "finish_arrived")
+    out = finish(place, factor, far[:1], (2,), EARLY, out, "finish_first_far")
+    out = finish(place, factor, [own, near], (0, 1), 0, out, "finish_near")
+    out = finish(place, factor, far[1:], (3,), EARLY, out, "finish_last_far")
     return out.reshape(nv, n2 * slabs, n3 // slabs, out.shape[-1])
 
 

time: 80.9 us -> 77.6 us (0.959)
  Pallas kernels: 43.5 us -> 37.7 us
  waiting for transfers between devices: 17.3 us -> 18.8 us
  starting transfers between devices: 19.4 us -> 20.5 us
    pallas_call x1, Pallas kernels: 20 us -> 14.6 us  [iterate(): pl.pallas_call(functools.partial(sweep_kernel, SWEEPS), in_specs=[pl.Bloc...]
    ppermute x17 -> x15, waiting for transfers between devices: 17.3 us -> 18.8 us  [exchange(): return lax.ppermute(value, axes, [(i, i ^ mask) for i in range(size)])]
    pallas_call x1, Pallas kernels: 4.83 us -> 3.67 us  [last_factor(): pl.pallas_call(factor_kernel, in_specs=[vmem], out_specs=vmem, out_shape=...]
    ppermute x17 -> x15, starting transfers between devices: 19.4 us -> 20.5 us  [exchange(): return lax.ppermute(value, axes, [(i, i ^ mask) for i in range(size)])]
    pallas_call x3 -> x4, Pallas kernels: 6.52 us -> 7.51 us  [finish(): pl.pallas_call(functools.partial(finish_kernel, ranks, first), in_specs=i...]
  transfers between devices with their start and end apart: 17 -> 15, of which waited for: 10 -> 10; matrix products, arithmetic and copies ran while one was open for 0% -> 0% of each run, Pallas kernels for 41% -> 33%
where the time goes in v3:
time: 77.6 us; the launch traced here: 77.5 us
  Pallas kernels  37.7 us (49%)
  starting transfers between devices  20.5 us (26%)
  waiting for transfers between devices  18.8 us (24%)
    ppermute x15, starting transfers between devices, exchange(): return lax.ppermute(value, axes, [(i, i ^ mask) for i in range(size)])  20.5 us
    ppermute x15, waiting for transfers between devices, exchange(): return lax.ppermute(value, axes, [(i, i ^ mask) for i in range(size)])  18.8 us
    pallas_call x1, Pallas kernels, iterate(): pl.pallas_call(functools.partial(sweep_kernel, SWEEPS), in_specs=[pl.Bloc...  14.6 us
    pallas_call x1, Pallas kernels, local_gram(): pl.pallas_call(functools.partial(gram_kernel, 1.0 / count), in_specs=[pl....  7.94 us
    pallas_call x4, Pallas kernels, finish(): pl.pallas_call(functools.partial(finish_kernel, ranks, first), in_specs=i...  7.51 us
    pallas_call x1, Pallas kernels, last_factor(): pl.pallas_call(factor_kernel, in_specs=[vmem], out_specs=vmem, out_shape=...  3.67 us
    pallas_call x2, Pallas kernels, project(): pl.pallas_call(functools.partial(project_kernel, ranks, begins), in_specs...  3.49 us
  transfers between devices with their start and end apart: 15, of which 10 were waited for; matrix products, arithmetic and copies ran while one was open for 0% of the time, Pallas kernels for 33%

profile of v3, /device:TPU:1, one launch (start us, length us, event | category | flops | bytes accessed | tf_op | source)
XLA Modules:
  0.0 77.5 jit_solution(8031233726968014576)
XLA Ops:
  0.0 0.1 pad_add_fusion.place_ref
  0.1 7.9 %local_gram.1 = (f32[640,128]{1,0:T(8,128)S(1)}, f32[640,128]{1,0:T(8,128)S(1)}, f32[4,4096,128]{2,1,0:T(8,128)S(1)}, f32[4,256,128]{2,1,0:T(8,128)S(1)}, f32[4,256,128]{2,1,0:T(8,128)S(1)}) custom-call(s32[2]{0:T(128)S(1)} %pad_add_fusion.place_ref, f32[4096,512]{1,0:T(8,128)} %bitcast.4), custom_call_target="tpu_custom_call" | custom-call | flops 1 | bytes 1 | tf_op jit(solution)/shard_map/local_gram/pallas_call | solution.py:125
  8.0 0.0 copy-start
  8.0 0.1 collective-permute-start
  8.2 1.6 %collective-permute-done = f32[640,128]{1,0:T(8,128)S(1)} collective-permute-done((f32[640,128]{1,0:T(8,128)S(1)}, f32[640,128]{1,0:T(8,128)S(1)}, u32[]{:S(2)}, u32[]{:S(2)}) %collective-permute-start) | collective-permute-done | bytes 327712 | tf_op jit(solution)/shard_map/ppermute | solution.py:37
  9.8 2.4 %collective-permute-start.1 = (f32[160,128]{1,0:T(8,128)S(1)}, f32[160,128]{1,0:T(8,128)S(1)}, u32[]{:S(2)}, u32[]{:S(2)}) collective-permute-start(f32[160,128]{1,0:T(8,128)S(1)} %get-tuple-element.45), channel_id=1, source_target_pairs={{0,4},{1,5},{2,6},{3,7},{4,0},{5,1},{6,2},{7,3},{8,12},{9,13},{10,... | collective-permute-start | bytes 245768 | tf_op jit(solution)/shard_map/ppermute | solution.py:37
  12.2 1.3 %collective-permute-start.3 = (f32[160,128]{1,0:T(8,128)S(1)}, f32[160,128]{1,0:T(8,128)S(1)}, u32[]{:S(2)}, u32[]{:S(2)}) collective-permute-start(f32[160,128]{1,0:T(8,128)S(1)} %get-tuple-element.46), channel_id=1, source_target_pairs={{0,12},{1,13},{2,14},{3,15},{4,8},{5,9},{6,10},{7,11},{8,4},{9,5},... | collective-permute-start | bytes 245768 | tf_op jit(solution)/shard_map/ppermute | solution.py:37
  13.5 0.0 collective-permute-start.2
  13.5 1.2 %collective-permute-done.1 = f32[160,128]{1,0:T(8,128)S(1)} collective-permute-done((f32[160,128]{1,0:T(8,128)S(1)}, f32[160,128]{1,0:T(8,128)S(1)}, u32[]{:S(2)}, u32[]{:S(2)}) %collective-permute-start.1) | collective-permute-done | bytes 81952 | tf_op jit(solution)/shard_map/ppermute | solution.py:37
  14.7 1.7 %collective-permute-done.3 = f32[160,128]{1,0:T(8,128)S(1)} collective-permute-done((f32[160,128]{1,0:T(8,128)S(1)}, f32[160,128]{1,0:T(8,128)S(1)}, u32[]{:S(2)}, u32[]{:S(2)}) %collective-permute-start.3) | collective-permute-done | bytes 81952 | tf_op jit(solution)/shard_map/ppermute | solution.py:37
  16.4 1.0 %collective-permute-done.2 = f32[160,128]{1,0:T(8,128)S(1)} collective-permute-done((f32[160,128]{1,0:T(8,128)S(1)}, f32[160,128]{1,0:T(8,128)S(1)}, u32[]{:S(2)}, u32[]{:S(2)}) %collective-permute-start.2) | collective-permute-done | bytes 81952 | tf_op jit(solution)/shard_map/ppermute | solution.py:37
  17.5 1.7 %collective-permute-start.4 = (f32[160,128]{1,0:T(8,128)S(1)}, f32[160,128]{1,0:T(8,128)S(1)}, u32[]{:S(2)}, u32[]{:S(2)}) collective-permute-start(f32[160,128]{1,0:T(8,128)S(1)} %fusion.1), channel_id=1, source_target_pairs={{0,2},{1,3},{2,0},{3,1},{4,6},{5,7},{6,4},{7,5},{8,10},{9,11},{10,... | collective-permute-start | bytes 245768 | tf_op jit(solution)/shard_map/ppermute | solution.py:37
  19.2 1.8 %collective-permute-done.4 = f32[160,128]{1,0:T(8,128)S(1)} collective-permute-done((f32[160,128]{1,0:T(8,128)S(1)}, f32[160,128]{1,0:T(8,128)S(1)}, u32[]{:S(2)}, u32[]{:S(2)}) %collective-permute-start.4) | collective-permute-done | bytes 81952 | tf_op jit(solution)/shard_map/ppermute | solution.py:37
  21.0 2.6 %collective-permute-start.5 = (f32[160,128]{1,0:T(8,128)S(1)}, f32[160,128]{1,0:T(8,128)S(1)}, u32[]{:S(2)}, u32[]{:S(2)}) collective-permute-start(f32[160,128]{1,0:T(8,128)S(1)} %add.26), channel_id=1, source_target_pairs={{0,16},{1,17},{2,18},{3,19},{4,20},{5,21},{6,22},{7,23},{8,24},{9,... | collective-permute-start | bytes 245768 | tf_op jit(solution)/shard_map/ppermute | solution.py:37
  23.6 2.7 %collective-permute-done.5 = f32[160,128]{1,0:T(8,128)S(1)} collective-permute-done((f32[160,128]{1,0:T(8,128)S(1)}, f32[160,128]{1,0:T(8,128)S(1)}, u32[]{:S(2)}, u32[]{:S(2)}) %collective-permute-start.5) | collective-permute-done | bytes 81952 | tf_op jit(solution)/shard_map/ppermute | solution.py:37
  26.4 1.2 %collective-permute-start.8 = (f32[160,128]{1,0:T(8,128)S(1)}, f32[160,128]{1,0:T(8,128)S(1)}, u32[]{:S(2)}, u32[]{:S(2)}) collective-permute-start(f32[160,128]{1,0:T(8,128)S(1)} %add.27), channel_id=1, source_target_pairs={{0,12},{1,13},{2,14},{3,15},{4,8},{5,9},{6,10},{7,11},{8,4},{9,5},... | collective-permute-start | bytes 245768 | tf_op jit(solution)/shard_map/ppermute | solution.py:37
  27.6 1.3 %collective-permute-start.7 = (f32[160,128]{1,0:T(8,128)S(1)}, f32[160,128]{1,0:T(8,128)S(1)}, u32[]{:S(2)}, u32[]{:S(2)}) collective-permute-start(f32[160,128]{1,0:T(8,128)S(1)} %add.27), channel_id=1, source_target_pairs={{0,8},{1,9},{2,10},{3,11},{4,12},{5,13},{6,14},{7,15},{8,0},{9,1},... | collective-permute-start | bytes 245768 | tf_op jit(solution)/shard_map/ppermute | solution.py:37
  28.9 0.2 collective-permute-start.6
  29.1 1.3 %collective-permute-start.10 = (f32[4,256,128]{2,1,0:T(8,128)S(1)}, f32[4,256,128]{2,1,0:T(8,128)S(1)}, u32[]{:S(2)}, u32[]{:S(2)}) collective-permute-start(f32[4,256,128]{2,1,0:T(8,128)S(1)} %get-tuple-element.30), channel_id=1, source_target_pairs={{0,2},{1,3},{2,0},{3,1},{4,6},{5,7},{6,4},{7,5},{8,10},{9,11},{10,... | collective-permute-start | bytes 1572872 | tf_op jit(solution)/shard_map/ppermute | solution.py:37
  30.4 3.7 %collective-permute-start.11 = (f32[4,256,128]{2,1,0:T(8,128)S(1)}, f32[4,256,128]{2,1,0:T(8,128)S(1)}, u32[]{:S(2)}, u32[]{:S(2)}) collective-permute-start(f32[4,256,128]{2,1,0:T(8,128)S(1)} %get-tuple-element.31), channel_id=1, source_target_pairs={{0,3},{1,2},{2,1},{3,0},{4,7},{5,6},{6,5},{7,4},{8,11},{9,10},{10,... | collective-permute-start | bytes 1572872 | tf_op jit(solution)/shard_map/ppermute | solution.py:37
  34.0 0.0 collective-permute-done.8
  34.0 0.0 collective-permute-done.7
  34.0 0.0 collective-permute-done.6
  34.1 2.5 %collective-permute-start.9 = (f32[640,128]{1,0:T(8,128)S(1)}, f32[640,128]{1,0:T(8,128)S(1)}, u32[]{:S(2)}, u32[]{:S(2)}) collective-permute-start(f32[640,128]{1,0:T(8,128)S(1)} %pad_maximum_fusion.mine_ref), channel_id=1, source_target_pairs={{0,1},{1,0},{2,3},{3,2},{4,5},{5,4},{6,7},{7,6},{8,9},{9,8},{10,11... | collective-permute-start | bytes 983048 | tf_op jit(solution)/shard_map/ppermute | solution.py:37
  36.5 1.3 %collective-permute-done.9.other_ref = f32[640,128]{1,0:T(8,128)S(1)} collective-permute-done((f32[640,128]{1,0:T(8,128)S(1)}, f32[640,128]{1,0:T(8,128)S(1)}, u32[]{:S(2)}, u32[]{:S(2)}) %collective-permute-start.9) | collective-permute-done | bytes 327712 | tf_op jit(solution)/shard_map/ppermute | solution.py:37
  37.8 0.0 copy-done
  37.8 14.6 %iterate.1.block_ref = f32[128,512]{1,0:T(8,128)S(1)} custom-call(s32[2]{0:T(128)S(1)} %pad_add_fusion.place_ref, f32[640,128]{1,0:T(8,128)S(1)} %pad_maximum_fusion.mine_ref, f32[640,128]{1,0:T(8,128)S(1)} %collective-permute-done.9.other_ref, f32[512,128]{1,0:T(8,128)S(1)} %copy-done), custom_call_target="tpu_custom_call" | custom-call | flops 1 | bytes 1 | tf_op jit(solution)/shard_map/iterate/pallas_call | solution.py:273
  52.4 0.0 collective-permute-done.10.refs_0_
  52.4 1.5 %collective-permute-done.11.refs_1_ = f32[4,256,128]{2,1,0:T(8,128)S(1)} collective-permute-done((f32[4,256,128]{2,1,0:T(8,128)S(1)}, f32[4,256,128]{2,1,0:T(8,128)S(1)}, u32[]{:S(2)}, u32[]{:S(2)}) %collective-permute-start.11) | collective-permute-done | bytes 524320 | tf_op jit(solution)/shard_map/ppermute | solution.py:37
  54.0 2.2 %project_sent.1 = (f32[1024,128]{1,0:T(8,128)S(1)}, f32[768,128]{1,0:T(8,128)S(1)}, f32[768,128]{1,0:T(8,128)S(1)}) custom-call(s32[2]{0:T(128)S(1)} %pad_add_fusion.place_ref, f32[4,4096,128]{2,1,0:T(8,128)S(1)} %get-tuple-element.33.held, f32[128,512]{1,0:T(8,128)S(1)} %iterate.1.block_ref), custom_call_target="tpu_custom_call" | custom-call | flops 1 | bytes 1 | tf_op jit(solution)/shard_map/project_sent/pallas_call | solution.py:349
  56.2 0.1 collective-permute-start.13
  56.2 1.4 %collective-permute-start.14 = (f32[768,128]{1,0:T(8,128)S(1)}, f32[768,128]{1,0:T(8,128)S(1)}, u32[]{:S(2)}, u32[]{:S(2)}) collective-permute-start(f32[768,128]{1,0:T(8,128)S(1)} %get-tuple-element.40), channel_id=1, source_target_pairs={{0,2},{1,3},{2,0},{3,1},{4,6},{5,7},{6,4},{7,5},{8,10},{9,11},{10,... | collective-permute-start | bytes 1179656 | tf_op jit(solution)/shard_map/ppermute | solution.py:37
  57.6 0.8 collective-permute-start.12
  58.4 1.3 %project_own.1.refs_0_ = f32[1024,128]{1,0:T(8,128)S(1)} custom-call(s32[2]{0:T(128)S(1)} %pad_add_fusion.place_ref, f32[4,4096,128]{2,1,0:T(8,128)S(1)} %get-tuple-element.33.held, f32[128,512]{1,0:T(8,128)S(1)} %iterate.1.block_ref), custom_call_target="tpu_custom_call" | custom-call | flops 1 | bytes 1 | tf_op jit(solution)/shard_map/project_own/pallas_call | solution.py:349
  59.7 3.7 %last_factor.1.factor_ref = f32[128,128]{1,0:T(8,128)S(1)} custom-call(f32[128,512]{1,0:T(8,128)S(1)} %iterate.1.block_ref), custom_call_target="tpu_custom_call" | custom-call | flops 1 | bytes 1 | tf_op jit(solution)/shard_map/last_factor/pallas_call | solution.py:302
  63.3 0.5 project_arrived.1
  63.8 1.7 %finish_arrived.1.refs_1_ = f32[4,4,4,64,128]{4,3,2,1,0:T(8,128)} custom-call(s32[2]{0:T(128)S(1)} %pad_add_fusion.place_ref, f32[128,128]{1,0:T(8,128)S(1)} %last_factor.1.factor_ref, f32[256,128]{1,0:T(8,128)S(1)} %get-tuple-element.43.refs_0_, f32[256,128]{1,0:T(8,128)S(1)} %get-tuple-element.44.refs_1_), custom_call_target="tpu_custom_call" | custom-call | flops 1 | bytes 1 | tf_op jit(solution)/shard_map/finish_arrived/pallas_call | solution.py:421
  65.5 1.1 %collective-permute-done.14.refs_0_ = f32[768,128]{1,0:T(8,128)S(1)} collective-permute-done((f32[768,128]{1,0:T(8,128)S(1)}, f32[768,128]{1,0:T(8,128)S(1)}, u32[]{:S(2)}, u32[]{:S(2)}) %collective-permute-start.14) | collective-permute-done | bytes 393248 | tf_op jit(solution)/shard_map/ppermute | solution.py:37
  66.6 1.8 %finish_first_far.1.refs_2_ = f32[4,4,4,64,128]{4,3,2,1,0:T(8,128)} custom-call(s32[2]{0:T(128)S(1)} %pad_add_fusion.place_ref, f32[128,128]{1,0:T(8,128)S(1)} %last_factor.1.factor_ref, f32[768,128]{1,0:T(8,128)S(1)} %collective-permute-done.14.refs_0_, f32[4,4,4,64,128]{4,3,2,1,0:T(8,128)} %finish_arrived.1.refs_1_), custom_call_target="tpu_custom_call", output_to_operand_aliasing={{}: (3, {})} | custom-call | flops 1 | bytes 1 | tf_op jit(solution)/shard_map/finish_first_far/pallas_call | solution.py:421
  68.3 0.0 collective-permute-done.13.refs_1_
  68.3 2.3 %finish_near.1.refs_1_ = f32[4,4,4,64,128]{4,3,2,1,0:T(8,128)} custom-call(s32[2]{0:T(128)S(1)} %pad_add_fusion.place_ref, f32[128,128]{1,0:T(8,128)S(1)} %last_factor.1.factor_ref, f32[1024,128]{1,0:T(8,128)S(1)} %project_own.1.refs_0_, f32[1024,128]{1,0:T(8,128)S(1)} %collective-permute-done.13.refs_1_, ...), custom_call_target="tpu_custom_call", output_to_operand_aliasing={{}: (4, {})} | custom-call | flops 1 | bytes 1 | tf_op jit(solution)/shard_map/finish_near/pallas_call | solution.py:421
  70.6 4.9 %collective-permute-done.12.refs_0_ = f32[768,128]{1,0:T(8,128)S(1)} collective-permute-done((f32[768,128]{1,0:T(8,128)S(1)}, f32[768,128]{1,0:T(8,128)S(1)}, u32[]{:S(2)}, u32[]{:S(2)}) %collective-permute-start.12) | collective-permute-done | bytes 393248 | tf_op jit(solution)/shard_map/ppermute | solution.py:37
  75.6 1.8 %finish_last_far.1 = f32[4,4,4,64,128]{4,3,2,1,0:T(8,128)} custom-call(s32[2]{0:T(128)S(1)} %pad_add_fusion.place_ref, f32[128,128]{1,0:T(8,128)S(1)} %last_factor.1.factor_ref, f32[768,128]{1,0:T(8,128)S(1)} %collective-permute-done.12.refs_0_, f32[4,4,4,64,128]{4,3,2,1,0:T(8,128)} %finish_near.1.refs_1_), custom_call_target="tpu_custom_call", output_to_operand_aliasing={{}: (3, {})} | custom-call | flops 1 | bytes 1 | tf_op jit(solution)/shard_map/finish_last_far/pallas_call | solution.py:421
  (6 shorter events, 0.1 us)
Async XLA Ops:
  8.0 29.8 %copy-start = (f32[512,128]{1,0:T(8,128)S(1)}, f32[512,128]{1,0:T(8,128)}, u32[]{:S(2)}) copy-start(f32[512,128]{1,0:T(8,128)} %start_ref.1) | copy-start | bytes 786436
  8.0 1.7 %collective-permute-start = (f32[640,128]{1,0:T(8,128)S(1)}, f32[640,128]{1,0:T(8,128)S(1)}, u32[]{:S(2)}, u32[]{:S(2)}) collective-permute-start(f32[640,128]{1,0:T(8,128)S(1)} %get-tuple-element.26), channel_id=1, source_target_pairs={{0,1},{1,0},{2,3},{3,2},{4,5},{5,4},{6,7},{7,6},{8,9},{9,8},{10,11... | collective-permute-start | bytes 983048 | tf_op jit(solution)/shard_map/ppermute | solution.py:37
  9.8 4.9 %collective-permute-start.1 = (f32[160,128]{1,0:T(8,128)S(1)}, f32[160,128]{1,0:T(8,128)S(1)}, u32[]{:S(2)}, u32[]{:S(2)}) collective-permute-start(f32[160,128]{1,0:T(8,128)S(1)} %get-tuple-element.45), channel_id=1, source_target_pairs={{0,4},{1,5},{2,6},{3,7},{4,0},{5,1},{6,2},{7,3},{8,12},{9,13},{10,... | collective-permute-start | bytes 245768 | tf_op jit(solution)/shard_map/ppermute | solution.py:37
  12.2 4.2 %collective-permute-start.3 = (f32[160,128]{1,0:T(8,128)S(1)}, f32[160,128]{1,0:T(8,128)S(1)}, u32[]{:S(2)}, u32[]{:S(2)}) collective-permute-start(f32[160,128]{1,0:T(8,128)S(1)} %get-tuple-element.46), channel_id=1, source_target_pairs={{0,12},{1,13},{2,14},{3,15},{4,8},{5,9},{6,10},{7,11},{8,4},{9,5},... | collective-permute-start | bytes 245768 | tf_op jit(solution)/shard_map/ppermute | solution.py:37
  13.5 4.0 %collective-permute-start.2 = (f32[160,128]{1,0:T(8,128)S(1)}, f32[160,128]{1,0:T(8,128)S(1)}, u32[]{:S(2)}, u32[]{:S(2)}) collective-permute-start(f32[160,128]{1,0:T(8,128)S(1)} %get-tuple-element.47), channel_id=1, source_target_pairs={{0,8},{1,9},{2,10},{3,11},{4,12},{5,13},{6,14},{7,15},{8,0},{9,1},... | collective-permute-start | bytes 245768 | tf_op jit(solution)/shard_map/ppermute | solution.py:37
  17.5 3.6 %collective-permute-start.4 = (f32[160,128]{1,0:T(8,128)S(1)}, f32[160,128]{1,0:T(8,128)S(1)}, u32[]{:S(2)}, u32[]{:S(2)}) collective-permute-start(f32[160,128]{1,0:T(8,128)S(1)} %fusion.1), channel_id=1, source_target_pairs={{0,2},{1,3},{2,0},{3,1},{4,6},{5,7},{6,4},{7,5},{8,10},{9,11},{10,... | collective-permute-start | bytes 245768 | tf_op jit(solution)/shard_map/ppermute | solution.py:37
  21.0 5.3 %collective-permute-start.5 = (f32[160,128]{1,0:T(8,128)S(1)}, f32[160,128]{1,0:T(8,128)S(1)}, u32[]{:S(2)}, u32[]{:S(2)}) collective-permute-start(f32[160,128]{1,0:T(8,128)S(1)} %add.26), channel_id=1, source_target_pairs={{0,16},{1,17},{2,18},{3,19},{4,20},{5,21},{6,22},{7,23},{8,24},{9,... | collective-permute-start | bytes 245768 | tf_op jit(solution)/shard_map/ppermute | solution.py:37
  26.4 7.7 %collective-permute-start.8 = (f32[160,128]{1,0:T(8,128)S(1)}, f32[160,128]{1,0:T(8,128)S(1)}, u32[]{:S(2)}, u32[]{:S(2)}) collective-permute-start(f32[160,128]{1,0:T(8,128)S(1)} %add.27), channel_id=1, source_target_pairs={{0,12},{1,13},{2,14},{3,15},{4,8},{5,9},{6,10},{7,11},{8,4},{9,5},... | collective-permute-start | bytes 245768 | tf_op jit(solution)/shard_map/ppermute | solution.py:37
  27.6 6.4 %collective-permute-start.7 = (f32[160,128]{1,0:T(8,128)S(1)}, f32[160,128]{1,0:T(8,128)S(1)}, u32[]{:S(2)}, u32[]{:S(2)}) collective-permute-start(f32[160,128]{1,0:T(8,128)S(1)} %add.27), channel_id=1, source_target_pairs={{0,8},{1,9},{2,10},{3,11},{4,12},{5,13},{6,14},{7,15},{8,0},{9,1},... | collective-permute-start | bytes 245768 | tf_op jit(solution)/shard_map/ppermute | solution.py:37
  28.9 5.2 %collective-permute-start.6 = (f32[160,128]{1,0:T(8,128)S(1)}, f32[160,128]{1,0:T(8,128)S(1)}, u32[]{:S(2)}, u32[]{:S(2)}) collective-permute-start(f32[160,128]{1,0:T(8,128)S(1)} %add.27), channel_id=1, source_target_pairs={{0,4},{1,5},{2,6},{3,7},{4,0},{5,1},{6,2},{7,3},{8,12},{9,13},{10,... | collective-permute-start | bytes 245768 | tf_op jit(solution)/shard_map/ppermute | solution.py:37
  29.1 23.3 %collective-permute-start.10 = (f32[4,256,128]{2,1,0:T(8,128)S(1)}, f32[4,256,128]{2,1,0:T(8,128)S(1)}, u32[]{:S(2)}, u32[]{:S(2)}) collective-permute-start(f32[4,256,128]{2,1,0:T(8,128)S(1)} %get-tuple-element.30), channel_id=1, source_target_pairs={{0,2},{1,3},{2,0},{3,1},{4,6},{5,7},{6,4},{7,5},{8,10},{9,11},{10,... | collective-permute-start | bytes 1572872 | tf_op jit(solution)/shard_map/ppermute | solution.py:37
  30.4 23.6 %collective-permute-start.11 = (f32[4,256,128]{2,1,0:T(8,128)S(1)}, f32[4,256,128]{2,1,0:T(8,128)S(1)}, u32[]{:S(2)}, u32[]{:S(2)}) collective-permute-start(f32[4,256,128]{2,1,0:T(8,128)S(1)} %get-tuple-element.31), channel_id=1, source_target_pairs={{0,3},{1,2},{2,1},{3,0},{4,7},{5,6},{6,5},{7,4},{8,11},{9,10},{10,... | collective-permute-start | bytes 1572872 | tf_op jit(solution)/shard_map/ppermute | solution.py:37
  34.1 3.7 %collective-permute-start.9 = (f32[640,128]{1,0:T(8,128)S(1)}, f32[640,128]{1,0:T(8,128)S(1)}, u32[]{:S(2)}, u32[]{:S(2)}) collective-permute-start(f32[640,128]{1,0:T(8,128)S(1)} %pad_maximum_fusion.mine_ref), channel_id=1, source_target_pairs={{0,1},{1,0},{2,3},{3,2},{4,5},{5,4},{6,7},{7,6},{8,9},{9,8},{10,11... | collective-permute-start | bytes 983048 | tf_op jit(solution)/shard_map/ppermute | solution.py:37
  56.2 12.2 %collective-permute-start.13 = (f32[1024,128]{1,0:T(8,128)S(1)}, f32[1024,128]{1,0:T(8,128)S(1)}, u32[]{:S(2)}, u32[]{:S(2)}) collective-permute-start(f32[1024,128]{1,0:T(8,128)S(1)} %get-tuple-element.39), channel_id=1, source_target_pairs={{0,1},{1,0},{2,3},{3,2},{4,5},{5,4},{6,7},{7,6},{8,9},{9,8},{10,11... | collective-permute-start | bytes 1572872 | tf_op jit(solution)/shard_map/ppermute | solution.py:37
  56.2 10.3 %collective-permute-start.14 = (f32[768,128]{1,0:T(8,128)S(1)}, f32[768,128]{1,0:T(8,128)S(1)}, u32[]{:S(2)}, u32[]{:S(2)}) collective-permute-start(f32[768,128]{1,0:T(8,128)S(1)} %get-tuple-element.40), channel_id=1, source_target_pairs={{0,2},{1,3},{2,0},{3,1},{4,6},{5,7},{6,4},{7,5},{8,10},{9,11},{10,... | collective-permute-start | bytes 1179656 | tf_op jit(solution)/shard_map/ppermute | solution.py:37
  57.6 18.0 %collective-permute-start.12 = (f32[768,128]{1,0:T(8,128)S(1)}, f32[768,128]{1,0:T(8,128)S(1)}, u32[]{:S(2)}, u32[]{:S(2)}) collective-permute-start(f32[768,128]{1,0:T(8,128)S(1)} %get-tuple-element.38), channel_id=1, source_target_pairs={{0,3},{1,2},{2,1},{3,0},{4,7},{5,6},{6,5},{7,4},{8,11},{9,10},{10,... | collective-permute-start | bytes 1179656 | tf_op jit(solution)/shard_map/ppermute | solution.py:37

commit v4 on v3

--- a/solution.py
+++ b/solution.py
@@ -10,7 +10,8 @@
 SWEEPS = 4
 SLABS = 4
 CHUNKS = 16
-EARLY = 4
+EARLY = ((3, 0, 2), (2, 0, 3), (3, 2, 3))
+FAR = (2, 3)
 TILES = (1, 1, 2, 2, 2)
 AXES = ("wide", "slab")
 MIB = 1 << 20
@@ -61,9 +62,7 @@
 
 
 def gram_kernel(scale, place_ref, x_ref, *refs):
-    keep_ref, give_ref, held = refs[:3]
-    early_refs = refs[3:-3]
-    acc, whole, sems = refs[-3:]
+    keep_ref, give_ref, held, acc, whole, sems = refs
     n = held.shape[0] * held.shape[2]
     half = n // 2
     arrivals = copies(x_ref, held, sems)
@@ -87,16 +86,6 @@
             acc[half:, half:] += right
         first += count
 
-    per = 8 // SLABS
-    for number, out in enumerate(early_refs):
-        to = place_ref[1] ^ (number + 2)
-        fibres = out.shape[1] // per
-        for c in range(out.shape[0]):
-            for j in range(per):
-                out[c, pl.ds(j, fibres, stride=per), :] = held[
-                    c, pl.ds(to * per + j, fibres, stride=8), :
-                ]
-
     edge = 128
     for number, (i, j) in enumerate(upper_blocks(n // edge)):
         rows, columns = slice(i * edge, (i + 1) * edge), slice(j * edge, (j + 1) * edge)
@@ -115,18 +104,17 @@
         give_ref[k * part : (k + 1) * part, :] = whole[pl.ds(theirs, part), :]
 
 
-def local_gram(place, rows, count, early):
+def local_gram(place, rows, count):
     n = rows.shape[1]
     tall = len(upper_blocks(n // 128)) * 128
     half = jax.ShapeDtypeStruct((tall // 2, 128), jnp.float32)
     held = jax.ShapeDtypeStruct((n // 128, rows.shape[0], 128), jnp.float32)
-    sent = jax.ShapeDtypeStruct((n // 128, early // SLABS, 128), jnp.float32)
     vmem = pl.BlockSpec(memory_space=pltpu.VMEM)
     return pl.pallas_call(
         functools.partial(gram_kernel, 1.0 / count),
         in_specs=[pl.BlockSpec(memory_space=pltpu.SMEM), pl.BlockSpec(memory_space=pl.ANY)],
-        out_specs=[vmem] * 5,
-        out_shape=[half, half, held, sent, sent],
+        out_specs=[vmem] * 3,
+        out_shape=[half, half, held],
         scratch_shapes=[
             pltpu.VMEM((n, 2 * n), jnp.float32),
             pltpu.VMEM((tall, 128), jnp.float32),
@@ -138,7 +126,7 @@
     )(place, rows)
 
 
-def sum_gram(keep, give, sent):
+def sum_gram(keep, give, prepared, send):
     size = lax.axis_size("wide") * lax.axis_size("slab")
     held = keep + exchange(give, AXES, 1)
     part = held.shape[0] // 4
@@ -148,13 +136,15 @@
     for piece in arrived:
         total = total + piece
     total = total + exchange(total, AXES, 2)
-    total, *sent = lax.optimization_barrier((total, *sent))
+    total, prepared = lax.optimization_barrier((total, prepared))
+    soon, more = send(prepared)
     mask = 16
     while mask < size:
         total = total + exchange(total, AXES, mask)
         mask *= 2
     mine = jnp.concatenate([total] + [exchange(total, AXES, 4 * k) for k in range(1, 4)])
-    return mine, exchange(mine, AXES, 1), sent
+    mine, soon = lax.optimization_barrier((mine, soon))
+    return mine, exchange(mine, AXES, 1), soon, more
 
 
 def row_of(x, p):
@@ -315,101 +305,174 @@
     return jnp.concatenate(halves(block_ref[...]), axis=0)
 
 
-def halved_product(x, both):
-    high, low = halves(x)
+def split_product(high, low, both):
     rank = both.shape[0] // 2
     product = dot(high, both, NT)
     return product[:, :rank] + product[:, rank:] + dot(low, both[:rank], NT)
 
 
-def project_kernel(ranks, begins, place_ref, held, block_ref, *outs):
+def halved_product(x, both):
+    return split_product(*halves(x), both)
+
+
+def pick(held, place_ref, rank, first, fibres, j):
+    start = first * 8 + (place_ref[1] ^ rank) * (8 // SLABS) + j
+    return side_by_side(held, pl.ds(start, fibres, stride=8))
+
+
+def chunks_of(rank):
+    return sum(count for to, _, count in EARLY if to == rank)
+
+
+def prepare_kernel(place_ref, held, *refs):
+    per = 8 // SLABS
+    high_ref, low_ref = refs[-2:]
+    chunk = held.shape[1] // 8 // CHUNKS
+    for (rank, first, count), out in zip(EARLY, refs[:-2], strict=True):
+        for j in range(per):
+            rows = pick(held, place_ref, rank, first * chunk, count * chunk, j)
+            for c in range(out.shape[0]):
+                out[c, pl.ds(j, count * chunk, stride=per), :] = rows[:, c * 128 : (c + 1) * 128]
+    begin = 0
+    for rank in (1, *FAR):
+        first = chunks_of(rank) * chunk
+        fibres = CHUNKS * chunk - first
+        for j in range(per):
+            high, low = halves(pick(held, place_ref, rank, first, fibres, j))
+            high_ref[begin : begin + fibres, :] = high
+            low_ref[begin : begin + fibres, :] = low
+            begin += fibres
+
+
+def prepare(place, held):
+    columns, rows, lanes = held.shape
+    chunk = rows // SLABS // CHUNKS
+    count = sum(CHUNKS - chunks_of(rank) for rank in (1, *FAR)) * chunk
+    split = jax.ShapeDtypeStruct((count, columns * lanes), jnp.bfloat16)
+    sent = [
+        jax.ShapeDtypeStruct((columns, some * chunk, lanes), jnp.float32) for _, _, some in EARLY
+    ]
+    vmem = pl.BlockSpec(memory_space=pltpu.VMEM)
+    return pl.pallas_call(
+        prepare_kernel,
+        in_specs=[pl.BlockSpec(memory_space=pltpu.SMEM), vmem],
+        out_specs=[vmem] * (len(sent) + 2),
+        out_shape=[*sent, split, split],
+        cost_estimate=BRIEF,
+        compiler_params=pltpu.CompilerParams(vmem_limit_bytes=16 * MIB),
+        name="prepare",
+    )(place, held)
+
+
+def sent_kernel(high_ref, low_ref, block_ref, *outs):
     per = 8 // SLABS
     both = weights(block_ref)
-    for begin in sorted(set(begins)):
-        some = [(k, out) for k, b, out in zip(ranks, begins, outs, strict=True) if b == begin]
-        total = some[0][1].shape[0] // per
-        fibres = total // pl.cdiv(total * len(some), 512)
-        for first in range(0, total, fibres):
-            picks = [
-                pl.ds(begin + first * 8 + (place_ref[1] ^ k) * per + j, fibres, stride=8)
-                for k, _ in some
-                for j in range(per)
-            ]
-            x = jnp.concatenate([side_by_side(held, pick) for pick in picks], axis=0)
-            product = halved_product(x, both)
-            for number in range(len(picks)):
-                out = some[number // per][1]
-                place = pl.ds(first * per + number % per, fibres, stride=per)
-                out[place, :] = product[number * fibres : (number + 1) * fibres]
-
-
-def project(place, held, block, ranks, begins, name):
-    rows, rank = held.shape[1], block.shape[0]
-    vmem = pl.BlockSpec(memory_space=pltpu.VMEM)
-    return pl.pallas_call(
-        functools.partial(project_kernel, ranks, begins),
+    begin = 0
+    for out in outs:
+        fibres = out.shape[0] // per
+        span = slice(begin, begin + fibres * per)
+        product = split_product(high_ref[span, :], low_ref[span, :], both)
+        for j in range(per):
+            out[pl.ds(j, fibres, stride=per), :] = product[j * fibres : (j + 1) * fibres]
+        begin += fibres * per
+
+
+def project_sent(high, low, block):
+    rank = block.shape[0]
+    parts = [CHUNKS - chunks_of(to) for to in (1, *FAR)]
+    sizes = [part * high.shape[0] // sum(parts) for part in parts]
+    vmem = pl.BlockSpec(memory_space=pltpu.VMEM)
+    return pl.pallas_call(
+        sent_kernel,
+        in_specs=[vmem] * 3,
+        out_specs=[vmem] * 3,
+        out_shape=[jax.ShapeDtypeStruct((size, rank), jnp.float32) for size in sizes],
+        cost_estimate=BRIEF,
+        compiler_params=pltpu.CompilerParams(vmem_limit_bytes=16 * MIB),
+        name="project_sent",
+    )(high, low, block)
+
+
+def own_kernel(place_ref, held, block_ref, out):
+    per = 8 // SLABS
+    both = weights(block_ref)
+    fibres = held.shape[1] // 8
+    x = jnp.concatenate([pick(held, place_ref, 0, 0, fibres, j) for j in range(per)], axis=0)
+    product = halved_product(x, both)
+    for j in range(per):
+        out[pl.ds(j, fibres, stride=per), :] = product[j * fibres : (j + 1) * fibres]
+
+
+def project_own(place, held, block):
+    vmem = pl.BlockSpec(memory_space=pltpu.VMEM)
+    return pl.pallas_call(
+        own_kernel,
         in_specs=[pl.BlockSpec(memory_space=pltpu.SMEM), vmem, vmem],
-        out_specs=[vmem] * len(ranks),
-        out_shape=[
-            jax.ShapeDtypeStruct(((rows - begin) // SLABS, rank), jnp.float32) for begin in begins
-        ],
-        cost_estimate=BRIEF,
-        compiler_params=pltpu.CompilerParams(vmem_limit_bytes=16 * MIB),
-        name=name,
+        out_specs=vmem,
+        out_shape=jax.ShapeDtypeStruct((held.shape[1] // SLABS, block.shape[0]), jnp.float32),
+        cost_estimate=BRIEF,
+        compiler_params=pltpu.CompilerParams(vmem_limit_bytes=16 * MIB),
+        name="project_own",
     )(place, held, block)
 
 
 def arrived_kernel(block_ref, *refs):
+    outs = refs[-len(FAR) :]
     both = weights(block_ref)
-    half = len(refs) // 2
-    for x_ref, out in zip(refs[:half], refs[half:], strict=True):
-        out[...] = halved_product(side_by_side(x_ref, slice(None)), both)
+    begins = [0] * len(FAR)
+    for (rank, _, _), x_ref in zip(EARLY, refs[: len(EARLY)], strict=True):
+        k, size = FAR.index(rank), x_ref.shape[1]
+        x = side_by_side(x_ref, slice(None))
+        outs[k][begins[k] : begins[k] + size, :] = halved_product(x, both)
+        begins[k] += size
 
 
 def project_arrived(block, arrived):
     vmem = pl.BlockSpec(memory_space=pltpu.VMEM)
+    chunk = arrived[0].shape[1] // EARLY[0][2]
     return pl.pallas_call(
         arrived_kernel,
         in_specs=[vmem] * (1 + len(arrived)),
-        out_specs=[vmem] * len(arrived),
-        out_shape=[jax.ShapeDtypeStruct((x.shape[1], block.shape[0]), jnp.float32) for x in arrived],
+        out_specs=[vmem] * len(FAR),
+        out_shape=[
+            jax.ShapeDtypeStruct((chunks_of(rank) * chunk, block.shape[0]), jnp.float32)
+            for rank in FAR
+        ],
         cost_estimate=BRIEF,
         compiler_params=pltpu.CompilerParams(vmem_limit_bytes=16 * MIB),
         name="project_arrived",
     )(block, *arrived)
 
 
-def finish_kernel(ranks, first, place_ref, factor_ref, *refs):
+def finish_kernel(ranks, firsts, place_ref, factor_ref, *refs):
     pieces = refs[: len(ranks)]
-    out, results, sems = refs[-3:]
+    out, *results, sems = refs[-2 - len(ranks) :]
     factor = factor_ref[...]
     per, size = out.shape[2], out.shape[3]
-    count = results.shape[1]
-    runs = []
-    while sum(length for _, length in runs) < count:
-        begin = first + sum(length for _, length in runs)
-        runs.append((begin, min(per - begin % per, first + count - begin)))
     sends = []
-    for k, (rank, piece) in enumerate(zip(ranks, pieces, strict=True)):
-        for number, (begin, length) in enumerate(runs):
+    for k, (rank, first, piece) in enumerate(zip(ranks, firsts, pieces, strict=True)):
+        last = first + results[k].shape[0]
+        begin = first
+        while begin < last:
+            length = min(per - begin % per, last - begin)
             span = pl.ds(begin - first, length)
             rows = piece[(begin - first) * size : (begin - first + length) * size, :]
-            results[k, span] = dot(rows, factor, NT, HIGHEST).reshape(length, size, -1)
+            results[k][span] = dot(rows, factor, NT, HIGHEST).reshape(length, size, -1)
             send = pltpu.make_async_copy(
-                results.at[k, span],
+                results[k].at[span],
                 out.at[begin // per, place_ref[1] ^ rank, pl.ds(begin % per, length)],
-                sems.at[k, number],
+                sems.at[k, begin // per],
             )
             send.start()
             sends.append(send)
+            begin += length
     for send in sends:
         send.wait()
 
 
-def finish(place, factor, pieces, ranks, first, into, name):
+def finish(place, factor, pieces, ranks, firsts, into, name):
     shape = into if isinstance(into, tuple) else into.shape
     size, rank = shape[3:]
-    count = pieces[0].shape[0] // size
     vmem = pl.BlockSpec(memory_space=pltpu.VMEM)
     in_specs = [pl.BlockSpec(memory_space=pltpu.SMEM)] + [vmem] * (1 + len(pieces))
     operands = [place, factor, *pieces]
@@ -419,14 +482,14 @@
         in_specs.append(pl.BlockSpec(memory_space=pl.ANY))
         operands.append(into)
     return pl.pallas_call(
-        functools.partial(finish_kernel, ranks, first),
+        functools.partial(finish_kernel, ranks, firsts),
         in_specs=in_specs,
         out_specs=pl.BlockSpec(memory_space=pl.ANY),
         out_shape=jax.ShapeDtypeStruct(shape, jnp.float32),
         scratch_shapes=[
-            pltpu.VMEM((len(pieces), count, size, rank), jnp.float32),
-            pltpu.SemaphoreType.DMA((len(pieces), shape[0])),
-        ],
+            pltpu.VMEM((piece.shape[0] // size, size, rank), jnp.float32) for piece in pieces
+        ]
+        + [pltpu.SemaphoreType.DMA((len(pieces), shape[0]))],
         input_output_aliases=aliases,
         cost_estimate=BRIEF,
         compiler_params=pltpu.CompilerParams(vmem_limit_bytes=16 * MIB),
@@ -441,31 +504,35 @@
     place = jnp.stack([lax.axis_index("wide") * slabs + slab, slab]).astype(jnp.int32)
     rows = fields.reshape(-1, n1)
     count = float(rows.shape[0] * lax.axis_size("wide") * slabs)
-    early = EARLY * rows.shape[0] // CHUNKS
-
-    def to_far(some):
-        return [exchange(x, "slab", 2 + k) for k, x in enumerate(some)]
-
-    keep, give, held, *sent = local_gram(place, rows, count, early)
-    mine, other, sent = sum_gram(keep, give, sent)
-    arrived = to_far(sent)
+    def to_far(some, ranks):
+        return [exchange(x, "slab", rank) for x, rank in zip(some, ranks, strict=True)]
+
+    def send(prepared):
+        *sent, high, low = prepared
+        ranks = [rank for rank, _, _ in EARLY]
+        return [*to_far(sent[:1], ranks[:1]), high, low], to_far(sent[1:], ranks[1:])
+
+    keep, give, held = local_gram(place, rows, count)
+    prepared = prepare(place, held)
+    mine, other, (soon, high, low), later = sum_gram(keep, give, prepared, send)
     block = iterate(place, mine, other, start_basis)
 
-    block, *arrived = lax.optimization_barrier((block, *arrived))
-    near, *far = project(place, held, block, (1, 2, 3), (0, early, early), "project_sent")
+    block, *arrived = lax.optimization_barrier((block, soon, *later))
+    near, *far = project_sent(high, low, block)
     block, near, *far = lax.optimization_barrier((block, near, *far))
-    far = to_far(far)
+    far = to_far(far, FAR)
     near = exchange(near, "slab", 1)
-    (own,) = project(place, held, block, (0,), (0,), "project_own")
+    own = project_own(place, held, block)
     arrived = project_arrived(block, arrived)
     factor = last_factor(block)
 
     per = CHUNKS // nv
     out = (nv, slabs, per, n2 * n3 // slabs // per, block.shape[0])
-    out = finish(place, factor, arrived, (2, 3), 0, out, "finish_arrived")
-    out = finish(place, factor, far[:1], (2,), EARLY, out, "finish_first_far")
-    out = finish(place, factor, [own, near], (0, 1), 0, out, "finish_near")
-    out = finish(place, factor, far[1:], (3,), EARLY, out, "finish_last_far")
+    late = [chunks_of(rank) for rank in FAR]
+    out = finish(place, factor, arrived, FAR, (0, 0), out, "finish_arrived")
+    out = finish(place, factor, far[:1], FAR[:1], late[:1], out, "finish_first_far")
+    out = finish(place, factor, [own, near], (0, 1), (0, 0), out, "finish_near")
+    out = finish(place, factor, far[1:], FAR[1:], late[1:], out, "finish_last_far")
     return out.reshape(nv, n2 * slabs, n3 // slabs, out.shape[-1])
 
 

time: 77.6 us -> 75.7 us (0.976)
  waiting for transfers between devices: 18.8 us -> 14.1 us
  Pallas kernels: 37.7 us -> 39.6 us
  starting transfers between devices: 20.5 us -> 21.3 us
    ppermute x15 -> x16, waiting for transfers between devices: 18.8 us -> 14.1 us  [exchange(): return lax.ppermute(value, axes, [(i, i ^ mask) for i in range(size)])]
    pallas_call x6 -> x7, Pallas kernels: 11 us -> 13 us  [the longest x4 7.6 us: finish(): pl.pallas_call(functools.partial(finish_kernel, ranks, firsts), in_specs=...]
    ppermute x15 -> x16, starting transfers between devices: 20.5 us -> 21.3 us  [exchange(): return lax.ppermute(value, axes, [(i, i ^ mask) for i in range(size)])]
  transfers between devices with their start and end apart: 15 -> 16, of which waited for: 10 -> 8; matrix products, arithmetic and copies ran while one was open for 0% -> 0% of each run, Pallas kernels for 33% -> 38%
where the time goes in v4:
time: 75.7 us; the launch traced here: 75.5 us
  Pallas kernels  39.6 us (52%)
  starting transfers between devices  21.3 us (28%)
  waiting for transfers between devices  14.1 us (19%)
    ppermute x16, starting transfers between devices, exchange(): return lax.ppermute(value, axes, [(i, i ^ mask) for i in range(size)])  21.3 us
    pallas_call x1, Pallas kernels, iterate(): pl.pallas_call(functools.partial(sweep_kernel, SWEEPS), in_specs=[pl.Bloc...  14.6 us
    ppermute x16, waiting for transfers between devices, exchange(): return lax.ppermute(value, axes, [(i, i ^ mask) for i in range(size)])  14.1 us
    pallas_call x1, Pallas kernels, local_gram(): pl.pallas_call(functools.partial(gram_kernel, 1.0 / count), in_specs=[pl....  7.77 us
    pallas_call x4, Pallas kernels, finish(): pl.pallas_call(functools.partial(finish_kernel, ranks, firsts), in_specs=...  7.6 us
    pallas_call x1, Pallas kernels, last_factor(): pl.pallas_call(factor_kernel, in_specs=[vmem], out_specs=vmem, out_shape=...  3.67 us
    pallas_call x1, Pallas kernels, prepare(): pl.pallas_call(prepare_kernel, in_specs=[pl.BlockSpec(memory_space=pltpu....  2.54 us
    pallas_call x1, Pallas kernels, project_sent(): pl.pallas_call(sent_kernel, in_specs=[vmem] * 3, out_specs=[vmem] * 3, ou...  1.56 us
  transfers between devices with their start and end apart: 16, of which 8 were waited for; matrix products, arithmetic and copies ran while one was open for 0% of the time, Pallas kernels for 38%

profile of v4, /device:TPU:1, one launch (start us, length us, event | category | flops | bytes accessed | tf_op | source)
XLA Modules:
  0.0 75.5 jit_solution(16881158107958945713)
XLA Ops:
  0.0 0.1 pad_add_fusion.place_ref
  0.1 7.8 %local_gram.1 = (f32[640,128]{1,0:T(8,128)S(1)}, f32[640,128]{1,0:T(8,128)S(1)}, f32[4,4096,128]{2,1,0:T(8,128)S(1)}) custom-call(s32[2]{0:T(128)S(1)} %pad_add_fusion.place_ref, f32[4096,512]{1,0:T(8,128)} %bitcast.4), custom_call_target="tpu_custom_call" | custom-call | flops 1 | bytes 1 | tf_op jit(solution)/shard_map/local_gram/pallas_call | solution.py:113
  7.9 0.1 collective-permute-start
  8.0 1.6 %collective-permute-done = f32[640,128]{1,0:T(8,128)S(1)} collective-permute-done((f32[640,128]{1,0:T(8,128)S(1)}, f32[640,128]{1,0:T(8,128)S(1)}, u32[]{:S(2)}, u32[]{:S(2)}) %collective-permute-start) | collective-permute-done | bytes 327712 | tf_op jit(solution)/shard_map/ppermute | solution.py:38
  9.6 2.4 %collective-permute-start.1 = (f32[160,128]{1,0:T(8,128)S(1)}, f32[160,128]{1,0:T(8,128)S(1)}, u32[]{:S(2)}, u32[]{:S(2)}) collective-permute-start(f32[160,128]{1,0:T(8,128)S(1)} %get-tuple-element.67), channel_id=1, source_target_pairs={{0,4},{1,5},{2,6},{3,7},{4,0},{5,1},{6,2},{7,3},{8,12},{9,13},{10,... | collective-permute-start | bytes 245768 | tf_op jit(solution)/shard_map/ppermute | solution.py:38
  12.0 1.3 %collective-permute-start.3 = (f32[160,128]{1,0:T(8,128)S(1)}, f32[160,128]{1,0:T(8,128)S(1)}, u32[]{:S(2)}, u32[]{:S(2)}) collective-permute-start(f32[160,128]{1,0:T(8,128)S(1)} %get-tuple-element.68), channel_id=1, source_target_pairs={{0,12},{1,13},{2,14},{3,15},{4,8},{5,9},{6,10},{7,11},{8,4},{9,5},... | collective-permute-start | bytes 245768 | tf_op jit(solution)/shard_map/ppermute | solution.py:38
  13.3 0.0 collective-permute-start.2
  13.3 1.2 %collective-permute-done.1 = f32[160,128]{1,0:T(8,128)S(1)} collective-permute-done((f32[160,128]{1,0:T(8,128)S(1)}, f32[160,128]{1,0:T(8,128)S(1)}, u32[]{:S(2)}, u32[]{:S(2)}) %collective-permute-start.1) | collective-permute-done | bytes 81952 | tf_op jit(solution)/shard_map/ppermute | solution.py:38
  14.5 1.7 %collective-permute-done.3 = f32[160,128]{1,0:T(8,128)S(1)} collective-permute-done((f32[160,128]{1,0:T(8,128)S(1)}, f32[160,128]{1,0:T(8,128)S(1)}, u32[]{:S(2)}, u32[]{:S(2)}) %collective-permute-start.3) | collective-permute-done | bytes 81952 | tf_op jit(solution)/shard_map/ppermute | solution.py:38
  16.2 1.0 %collective-permute-done.2 = f32[160,128]{1,0:T(8,128)S(1)} collective-permute-done((f32[160,128]{1,0:T(8,128)S(1)}, f32[160,128]{1,0:T(8,128)S(1)}, u32[]{:S(2)}, u32[]{:S(2)}) %collective-permute-start.2) | collective-permute-done | bytes 81952 | tf_op jit(solution)/shard_map/ppermute | solution.py:38
  17.3 1.7 %collective-permute-start.4 = (f32[160,128]{1,0:T(8,128)S(1)}, f32[160,128]{1,0:T(8,128)S(1)}, u32[]{:S(2)}, u32[]{:S(2)}) collective-permute-start(f32[160,128]{1,0:T(8,128)S(1)} %fusion.1), channel_id=1, source_target_pairs={{0,2},{1,3},{2,0},{3,1},{4,6},{5,7},{6,4},{7,5},{8,10},{9,11},{10,... | collective-permute-start | bytes 245768 | tf_op jit(solution)/shard_map/ppermute | solution.py:38
  19.0 0.0 copy-start
  19.0 2.5 %prepare.1 = (f32[4,128,128]{2,1,0:T(8,128)S(1)}, f32[4,192,128]{2,1,0:T(8,128)S(1)}, f32[4,192,128]{2,1,0:T(8,128)S(1)}, bf16[2560,512]{1,0:T(8,128)(2,1)S(1)}, bf16[2560,512]{1,0:T(8,128)(2,1)S(1)}) custom-call(s32[2]{0:T(128)S(1)} %pad_add_fusion.place_ref, f32[4,4096,128]{2,1,0:T(8,128)S(1)} %get-tuple-element.38.held), custom_call_target="tpu_custom_call" | custom-call | flops 1 | bytes 1 | tf_op jit(solution)/shard_map/prepare/pallas_call | solution.py:356
  21.6 0.0 collective-permute-done.4
  21.6 2.4 %collective-permute-start.5 = (f32[160,128]{1,0:T(8,128)S(1)}, f32[160,128]{1,0:T(8,128)S(1)}, u32[]{:S(2)}, u32[]{:S(2)}) collective-permute-start(f32[160,128]{1,0:T(8,128)S(1)} %add.26), channel_id=1, source_target_pairs={{0,16},{1,17},{2,18},{3,19},{4,20},{5,21},{6,22},{7,23},{8,24},{9,... | collective-permute-start | bytes 245768 | tf_op jit(solution)/shard_map/ppermute | solution.py:38
  24.0 3.2 %collective-permute-start.9 = (f32[4,128,128]{2,1,0:T(8,128)S(1)}, f32[4,128,128]{2,1,0:T(8,128)S(1)}, u32[]{:S(2)}, u32[]{:S(2)}) collective-permute-start(f32[4,128,128]{2,1,0:T(8,128)S(1)} %get-tuple-element.45), channel_id=1, source_target_pairs={{0,3},{1,2},{2,1},{3,0},{4,7},{5,6},{6,5},{7,4},{8,11},{9,10},{10,... | collective-permute-start | bytes 786440 | tf_op jit(solution)/shard_map/ppermute | solution.py:38
  27.2 0.0 collective-permute-done.5
  27.2 2.1 %collective-permute-start.8 = (f32[160,128]{1,0:T(8,128)S(1)}, f32[160,128]{1,0:T(8,128)S(1)}, u32[]{:S(2)}, u32[]{:S(2)}) collective-permute-start(f32[160,128]{1,0:T(8,128)S(1)} %add.27), channel_id=1, source_target_pairs={{0,12},{1,13},{2,14},{3,15},{4,8},{5,9},{6,10},{7,11},{8,4},{9,5},... | collective-permute-start | bytes 245768 | tf_op jit(solution)/shard_map/ppermute | solution.py:38
  29.2 0.4 collective-permute-start.7
  29.6 0.3 collective-permute-start.6
  29.9 0.3 collective-permute-start.11
  30.2 1.3 %collective-permute-done.8 = f32[160,128]{1,0:T(8,128)S(1)} collective-permute-done((f32[160,128]{1,0:T(8,128)S(1)}, f32[160,128]{1,0:T(8,128)S(1)}, u32[]{:S(2)}, u32[]{:S(2)}) %collective-permute-start.8) | collective-permute-done | bytes 81952 | tf_op jit(solution)/shard_map/ppermute | solution.py:38
  31.4 3.9 %collective-permute-start.12 = (f32[4,192,128]{2,1,0:T(8,128)S(1)}, f32[4,192,128]{2,1,0:T(8,128)S(1)}, u32[]{:S(2)}, u32[]{:S(2)}) collective-permute-start(f32[4,192,128]{2,1,0:T(8,128)S(1)} %get-tuple-element.51), channel_id=1, source_target_pairs={{0,3},{1,2},{2,1},{3,0},{4,7},{5,6},{6,5},{7,4},{8,11},{9,10},{10,... | collective-permute-start | bytes 1179656 | tf_op jit(solution)/shard_map/ppermute | solution.py:38
  35.3 0.0 collective-permute-done.7
  35.3 0.0 collective-permute-done.6
  35.4 0.0 collective-permute-done.9.refs_0_
  35.4 1.0 %collective-permute-start.10 = (f32[640,128]{1,0:T(8,128)S(1)}, f32[640,128]{1,0:T(8,128)S(1)}, u32[]{:S(2)}, u32[]{:S(2)}) collective-permute-start(f32[640,128]{1,0:T(8,128)S(1)} %pad_maximum_fusion.mine_ref), channel_id=1, source_target_pairs={{0,1},{1,0},{2,3},{3,2},{4,5},{5,4},{6,7},{7,6},{8,9},{9,8},{10,11... | collective-permute-start | bytes 983048 | tf_op jit(solution)/shard_map/ppermute | solution.py:38
  36.4 1.3 %collective-permute-done.10.other_ref = f32[640,128]{1,0:T(8,128)S(1)} collective-permute-done((f32[640,128]{1,0:T(8,128)S(1)}, f32[640,128]{1,0:T(8,128)S(1)}, u32[]{:S(2)}, u32[]{:S(2)}) %collective-permute-start.10) | collective-permute-done | bytes 327712 | tf_op jit(solution)/shard_map/ppermute | solution.py:38
  37.6 0.0 copy-done
  37.6 14.6 %iterate.1.block_ref = f32[128,512]{1,0:T(8,128)S(1)} custom-call(s32[2]{0:T(128)S(1)} %pad_add_fusion.place_ref, f32[640,128]{1,0:T(8,128)S(1)} %pad_maximum_fusion.mine_ref, f32[640,128]{1,0:T(8,128)S(1)} %collective-permute-done.10.other_ref, f32[512,128]{1,0:T(8,128)S(1)} %copy-done), custom_call_target="tpu_custom_call" | custom-call | flops 1 | bytes 1 | tf_op jit(solution)/shard_map/iterate/pallas_call | solution.py:263
  52.2 0.0 collective-permute-done.11.refs_1_
  52.3 0.0 collective-permute-done.12.refs_2_
  52.3 1.6 %project_sent.1 = (f32[1024,128]{1,0:T(8,128)S(1)}, f32[832,128]{1,0:T(8,128)S(1)}, f32[704,128]{1,0:T(8,128)S(1)}) custom-call(bf16[2560,512]{1,0:T(8,128)(2,1)S(1)} %get-tuple-element.53.high_ref, bf16[2560,512]{1,0:T(8,128)(2,1)S(1)} %get-tuple-element.54.low_ref, f32[128,512]{1,0:T(8,128)S(1)} %iterate.1.block_ref), custom_call_target="tpu_custom_call" | custom-call | flops 1 | bytes 1 | tf_op jit(solution)/shard_map/project_sent/pallas_call | solution.py:385
  53.8 0.4 collective-permute-start.14
  54.3 1.2 %collective-permute-start.15 = (f32[832,128]{1,0:T(8,128)S(1)}, f32[832,128]{1,0:T(8,128)S(1)}, u32[]{:S(2)}, u32[]{:S(2)}) collective-permute-start(f32[832,128]{1,0:T(8,128)S(1)} %get-tuple-element.61), channel_id=1, source_target_pairs={{0,2},{1,3},{2,0},{3,1},{4,6},{5,7},{6,4},{7,5},{8,10},{9,11},{10,... | collective-permute-start | bytes 1277960 | tf_op jit(solution)/shard_map/ppermute | solution.py:38
  55.5 0.5 collective-permute-start.13
  56.1 1.3 %project_own.1.refs_0_ = f32[1024,128]{1,0:T(8,128)S(1)} custom-call(s32[2]{0:T(128)S(1)} %pad_add_fusion.place_ref, f32[4,4096,128]{2,1,0:T(8,128)S(1)} %get-tuple-element.38.held, f32[128,512]{1,0:T(8,128)S(1)} %iterate.1.block_ref), custom_call_target="tpu_custom_call" | custom-call | flops 1 | bytes 1 | tf_op jit(solution)/shard_map/project_own/pallas_call | solution.py:408
  57.4 3.7 %last_factor.1.factor_ref = f32[128,128]{1,0:T(8,128)S(1)} custom-call(f32[128,512]{1,0:T(8,128)S(1)} %iterate.1.block_ref), custom_call_target="tpu_custom_call" | custom-call | flops 1 | bytes 1 | tf_op jit(solution)/shard_map/last_factor/pallas_call | solution.py:292
  61.0 0.6 project_arrived.1
  61.6 1.7 %finish_arrived.1.refs_1_ = f32[4,4,4,64,128]{4,3,2,1,0:T(8,128)} custom-call(s32[2]{0:T(128)S(1)} %pad_add_fusion.place_ref, f32[128,128]{1,0:T(8,128)S(1)} %last_factor.1.factor_ref, f32[192,128]{1,0:T(8,128)S(1)} %get-tuple-element.65.refs_0_, f32[320,128]{1,0:T(8,128)S(1)} %get-tuple-element.66.refs_1_), custom_call_target="tpu_custom_call" | custom-call | flops 1 | bytes 1 | tf_op jit(solution)/shard_map/finish_arrived/pallas_call | solution.py:484
  63.3 2.2 %collective-permute-done.15.refs_0_ = f32[832,128]{1,0:T(8,128)S(1)} collective-permute-done((f32[832,128]{1,0:T(8,128)S(1)}, f32[832,128]{1,0:T(8,128)S(1)}, u32[]{:S(2)}, u32[]{:S(2)}) %collective-permute-start.15) | collective-permute-done | bytes 426016 | tf_op jit(solution)/shard_map/ppermute | solution.py:38
  65.6 1.8 %finish_first_far.1.refs_2_ = f32[4,4,4,64,128]{4,3,2,1,0:T(8,128)} custom-call(s32[2]{0:T(128)S(1)} %pad_add_fusion.place_ref, f32[128,128]{1,0:T(8,128)S(1)} %last_factor.1.factor_ref, f32[832,128]{1,0:T(8,128)S(1)} %collective-permute-done.15.refs_0_, f32[4,4,4,64,128]{4,3,2,1,0:T(8,128)} %finish_arrived.1.refs_1_), custom_call_target="tpu_custom_call", output_to_operand_aliasing={{}: (3, {})} | custom-call | flops 1 | bytes 1 | tf_op jit(solution)/shard_map/finish_first_far/pallas_call | solution.py:484
  67.4 0.0 collective-permute-done.14.refs_1_
  67.4 2.3 %finish_near.1.refs_1_ = f32[4,4,4,64,128]{4,3,2,1,0:T(8,128)} custom-call(s32[2]{0:T(128)S(1)} %pad_add_fusion.place_ref, f32[128,128]{1,0:T(8,128)S(1)} %last_factor.1.factor_ref, f32[1024,128]{1,0:T(8,128)S(1)} %project_own.1.refs_0_, f32[1024,128]{1,0:T(8,128)S(1)} %collective-permute-done.14.refs_1_, ...), custom_call_target="tpu_custom_call", output_to_operand_aliasing={{}: (4, {})} | custom-call | flops 1 | bytes 1 | tf_op jit(solution)/shard_map/finish_near/pallas_call | solution.py:484
  69.7 3.8 %collective-permute-done.13.refs_0_ = f32[704,128]{1,0:T(8,128)S(1)} collective-permute-done((f32[704,128]{1,0:T(8,128)S(1)}, f32[704,128]{1,0:T(8,128)S(1)}, u32[]{:S(2)}, u32[]{:S(2)}) %collective-permute-start.13) | collective-permute-done | bytes 360480 | tf_op jit(solution)/shard_map/ppermute | solution.py:38
  73.5 1.8 %finish_last_far.1 = f32[4,4,4,64,128]{4,3,2,1,0:T(8,128)} custom-call(s32[2]{0:T(128)S(1)} %pad_add_fusion.place_ref, f32[128,128]{1,0:T(8,128)S(1)} %last_factor.1.factor_ref, f32[704,128]{1,0:T(8,128)S(1)} %collective-permute-done.13.refs_0_, f32[4,4,4,64,128]{4,3,2,1,0:T(8,128)} %finish_near.1.refs_1_), custom_call_target="tpu_custom_call", output_to_operand_aliasing={{}: (3, {})} | custom-call | flops 1 | bytes 1 | tf_op jit(solution)/shard_map/finish_last_far/pallas_call | solution.py:484
  (6 shorter events, 0.1 us)
Async XLA Ops:
  7.9 1.7 %collective-permute-start = (f32[640,128]{1,0:T(8,128)S(1)}, f32[640,128]{1,0:T(8,128)S(1)}, u32[]{:S(2)}, u32[]{:S(2)}) collective-permute-start(f32[640,128]{1,0:T(8,128)S(1)} %get-tuple-element.37), channel_id=1, source_target_pairs={{0,1},{1,0},{2,3},{3,2},{4,5},{5,4},{6,7},{7,6},{8,9},{9,8},{10,11... | collective-permute-start | bytes 983048 | tf_op jit(solution)/shard_map/ppermute | solution.py:38
  9.6 4.9 %collective-permute-start.1 = (f32[160,128]{1,0:T(8,128)S(1)}, f32[160,128]{1,0:T(8,128)S(1)}, u32[]{:S(2)}, u32[]{:S(2)}) collective-permute-start(f32[160,128]{1,0:T(8,128)S(1)} %get-tuple-element.67), channel_id=1, source_target_pairs={{0,4},{1,5},{2,6},{3,7},{4,0},{5,1},{6,2},{7,3},{8,12},{9,13},{10,... | collective-permute-start | bytes 245768 | tf_op jit(solution)/shard_map/ppermute | solution.py:38
  12.0 4.2 %collective-permute-start.3 = (f32[160,128]{1,0:T(8,128)S(1)}, f32[160,128]{1,0:T(8,128)S(1)}, u32[]{:S(2)}, u32[]{:S(2)}) collective-permute-start(f32[160,128]{1,0:T(8,128)S(1)} %get-tuple-element.68), channel_id=1, source_target_pairs={{0,12},{1,13},{2,14},{3,15},{4,8},{5,9},{6,10},{7,11},{8,4},{9,5},... | collective-permute-start | bytes 245768 | tf_op jit(solution)/shard_map/ppermute | solution.py:38
  13.3 4.0 %collective-permute-start.2 = (f32[160,128]{1,0:T(8,128)S(1)}, f32[160,128]{1,0:T(8,128)S(1)}, u32[]{:S(2)}, u32[]{:S(2)}) collective-permute-start(f32[160,128]{1,0:T(8,128)S(1)} %get-tuple-element.69), channel_id=1, source_target_pairs={{0,8},{1,9},{2,10},{3,11},{4,12},{5,13},{6,14},{7,15},{8,0},{9,1},... | collective-permute-start | bytes 245768 | tf_op jit(solution)/shard_map/ppermute | solution.py:38
  17.3 4.3 %collective-permute-start.4 = (f32[160,128]{1,0:T(8,128)S(1)}, f32[160,128]{1,0:T(8,128)S(1)}, u32[]{:S(2)}, u32[]{:S(2)}) collective-permute-start(f32[160,128]{1,0:T(8,128)S(1)} %fusion.1), channel_id=1, source_target_pairs={{0,2},{1,3},{2,0},{3,1},{4,6},{5,7},{6,4},{7,5},{8,10},{9,11},{10,... | collective-permute-start | bytes 245768 | tf_op jit(solution)/shard_map/ppermute | solution.py:38
  19.0 18.6 %copy-start = (f32[512,128]{1,0:T(8,128)S(1)}, f32[512,128]{1,0:T(8,128)}, u32[]{:S(2)}) copy-start(f32[512,128]{1,0:T(8,128)} %start_ref.1) | copy-start | bytes 786436
  21.6 5.6 %collective-permute-start.5 = (f32[160,128]{1,0:T(8,128)S(1)}, f32[160,128]{1,0:T(8,128)S(1)}, u32[]{:S(2)}, u32[]{:S(2)}) collective-permute-start(f32[160,128]{1,0:T(8,128)S(1)} %add.26), channel_id=1, source_target_pairs={{0,16},{1,17},{2,18},{3,19},{4,20},{5,21},{6,22},{7,23},{8,24},{9,... | collective-permute-start | bytes 245768 | tf_op jit(solution)/shard_map/ppermute | solution.py:38
  24.0 11.4 %collective-permute-start.9 = (f32[4,128,128]{2,1,0:T(8,128)S(1)}, f32[4,128,128]{2,1,0:T(8,128)S(1)}, u32[]{:S(2)}, u32[]{:S(2)}) collective-permute-start(f32[4,128,128]{2,1,0:T(8,128)S(1)} %get-tuple-element.45), channel_id=1, source_target_pairs={{0,3},{1,2},{2,1},{3,0},{4,7},{5,6},{6,5},{7,4},{8,11},{9,10},{10,... | collective-permute-start | bytes 786440 | tf_op jit(solution)/shard_map/ppermute | solution.py:38
  27.2 4.3 %collective-permute-start.8 = (f32[160,128]{1,0:T(8,128)S(1)}, f32[160,128]{1,0:T(8,128)S(1)}, u32[]{:S(2)}, u32[]{:S(2)}) collective-permute-start(f32[160,128]{1,0:T(8,128)S(1)} %add.27), channel_id=1, source_target_pairs={{0,12},{1,13},{2,14},{3,15},{4,8},{5,9},{6,10},{7,11},{8,4},{9,5},... | collective-permute-start | bytes 245768 | tf_op jit(solution)/shard_map/ppermute | solution.py:38
  29.2 6.1 %collective-permute-start.7 = (f32[160,128]{1,0:T(8,128)S(1)}, f32[160,128]{1,0:T(8,128)S(1)}, u32[]{:S(2)}, u32[]{:S(2)}) collective-permute-start(f32[160,128]{1,0:T(8,128)S(1)} %add.27), channel_id=1, source_target_pairs={{0,8},{1,9},{2,10},{3,11},{4,12},{5,13},{6,14},{7,15},{8,0},{9,1},... | collective-permute-start | bytes 245768 | tf_op jit(solution)/shard_map/ppermute | solution.py:38
  29.6 5.7 %collective-permute-start.6 = (f32[160,128]{1,0:T(8,128)S(1)}, f32[160,128]{1,0:T(8,128)S(1)}, u32[]{:S(2)}, u32[]{:S(2)}) collective-permute-start(f32[160,128]{1,0:T(8,128)S(1)} %add.27), channel_id=1, source_target_pairs={{0,4},{1,5},{2,6},{3,7},{4,0},{5,1},{6,2},{7,3},{8,12},{9,13},{10,... | collective-permute-start | bytes 245768 | tf_op jit(solution)/shard_map/ppermute | solution.py:38
  29.9 22.4 %collective-permute-start.11 = (f32[4,192,128]{2,1,0:T(8,128)S(1)}, f32[4,192,128]{2,1,0:T(8,128)S(1)}, u32[]{:S(2)}, u32[]{:S(2)}) collective-permute-start(f32[4,192,128]{2,1,0:T(8,128)S(1)} %get-tuple-element.50), channel_id=1, source_target_pairs={{0,2},{1,3},{2,0},{3,1},{4,6},{5,7},{6,4},{7,5},{8,10},{9,11},{10,... | collective-permute-start | bytes 1179656 | tf_op jit(solution)/shard_map/ppermute | solution.py:38
  31.4 20.8 %collective-permute-start.12 = (f32[4,192,128]{2,1,0:T(8,128)S(1)}, f32[4,192,128]{2,1,0:T(8,128)S(1)}, u32[]{:S(2)}, u32[]{:S(2)}) collective-permute-start(f32[4,192,128]{2,1,0:T(8,128)S(1)} %get-tuple-element.51), channel_id=1, source_target_pairs={{0,3},{1,2},{2,1},{3,0},{4,7},{5,6},{6,5},{7,4},{8,11},{9,10},{10,... | collective-permute-start | bytes 1179656 | tf_op jit(solution)/shard_map/ppermute | solution.py:38
  35.4 2.2 %collective-permute-start.10 = (f32[640,128]{1,0:T(8,128)S(1)}, f32[640,128]{1,0:T(8,128)S(1)}, u32[]{:S(2)}, u32[]{:S(2)}) collective-permute-start(f32[640,128]{1,0:T(8,128)S(1)} %pad_maximum_fusion.mine_ref), channel_id=1, source_target_pairs={{0,1},{1,0},{2,3},{3,2},{4,5},{5,4},{6,7},{7,6},{8,9},{9,8},{10,11... | collective-permute-start | bytes 983048 | tf_op jit(solution)/shard_map/ppermute | solution.py:38
  53.8 13.6 %collective-permute-start.14 = (f32[1024,128]{1,0:T(8,128)S(1)}, f32[1024,128]{1,0:T(8,128)S(1)}, u32[]{:S(2)}, u32[]{:S(2)}) collective-permute-start(f32[1024,128]{1,0:T(8,128)S(1)} %get-tuple-element.60), channel_id=1, source_target_pairs={{0,1},{1,0},{2,3},{3,2},{4,5},{5,4},{6,7},{7,6},{8,9},{9,8},{10,11... | collective-permute-start | bytes 1572872 | tf_op jit(solution)/shard_map/ppermute | solution.py:38
  54.3 11.3 %collective-permute-start.15 = (f32[832,128]{1,0:T(8,128)S(1)}, f32[832,128]{1,0:T(8,128)S(1)}, u32[]{:S(2)}, u32[]{:S(2)}) collective-permute-start(f32[832,128]{1,0:T(8,128)S(1)} %get-tuple-element.61), channel_id=1, source_target_pairs={{0,2},{1,3},{2,0},{3,1},{4,6},{5,7},{6,4},{7,5},{8,10},{9,11},{10,... | collective-permute-start | bytes 1277960 | tf_op jit(solution)/shard_map/ppermute | solution.py:38
  55.5 18.0 %collective-permute-start.13 = (f32[704,128]{1,0:T(8,128)S(1)}, f32[704,128]{1,0:T(8,128)S(1)}, u32[]{:S(2)}, u32[]{:S(2)}) collective-permute-start(f32[704,128]{1,0:T(8,128)S(1)} %get-tuple-element.59), channel_id=1, source_target_pairs={{0,3},{1,2},{2,1},{3,0},{4,7},{5,6},{6,5},{7,4},{8,11},{9,10},{10,... | collective-permute-start | bytes 1081352 | tf_op jit(solution)/shard_map/ppermute | solution.py:38

commit v5 on v4

--- a/solution.py
+++ b/solution.py
@@ -10,7 +10,7 @@
 SWEEPS = 4
 SLABS = 4
 CHUNKS = 16
-EARLY = ((3, 0, 2), (2, 0, 3), (3, 2, 3))
+EARLY = ((2, 0, 4), (3, 0, 4))
 FAR = (2, 3)
 TILES = (1, 1, 2, 2, 2)
 AXES = ("wide", "slab")
@@ -31,6 +31,14 @@
     return high, (x - high.astype(jnp.float32)).astype(jnp.bfloat16)
 
 
+def split_dot(a, b):
+    a_high, a_low = halves(a)
+    b_high, b_low = halves(b)
+    both = dot(jnp.concatenate([a_high, a_low], axis=0), b_high, NN)
+    rows = a.shape[0]
+    return both[:rows] + both[rows:] + dot(a_high, b_low, NN)
+
+
 def exchange(value, axes, mask):
     size = 1
     for axis in axes if isinstance(axes, tuple) else (axes,):
@@ -38,8 +46,23 @@
     return lax.ppermute(value, axes, [(i, i ^ mask) for i in range(size)])
 
 
-def upper_blocks(blocks):
-    return [(i, j) for i in range(blocks) for j in range(i, blocks)]
+EDGE = 128
+
+
+def upper_blocks(n):
+    return [(i, j) for i in range(n // EDGE) for j in range(i + 1, n // EDGE)]
+
+
+def packed_rows(n):
+    return pl.cdiv((len(upper_blocks(n)) + n // EDGE // 2) * EDGE + 8, 64) * 64
+
+
+def span(number):
+    return slice(number * EDGE, (number + 1) * EDGE)
+
+
+def block_indices():
+    return [lax.broadcasted_iota(jnp.int32, (EDGE, EDGE), axis) for axis in (0, 1)]
 
 
 def copies(x_ref, held, sems):
@@ -57,8 +80,8 @@
     ]
 
 
-def side_by_side(ref, span):
-    return jnp.concatenate([ref[c, span, :] for c in range(ref.shape[0])], axis=1)
+def side_by_side(ref, rows):
+    return jnp.concatenate([ref[c, rows, :] for c in range(ref.shape[0])], axis=1)
 
 
 def gram_kernel(scale, place_ref, x_ref, *refs):
@@ -86,14 +109,22 @@
             acc[half:, half:] += right
         first += count
 
-    edge = 128
-    for number, (i, j) in enumerate(upper_blocks(n // edge)):
-        rows, columns = slice(i * edge, (i + 1) * edge), slice(j * edge, (j + 1) * edge)
-        cross = acc[rows, n + j * edge : n + (j + 1) * edge]
-        other = acc[columns, n + i * edge : n + (i + 1) * edge]
-        whole[number * edge : (number + 1) * edge, :] = (
-            acc[rows, columns] + cross + other.T
-        ) * scale
+    def block(i, j):
+        cross = acc[span(i), n + j * EDGE : n + (j + 1) * EDGE]
+        other = acc[span(j), n + i * EDGE : n + (i + 1) * EDGE]
+        return (acc[span(i), span(j)] + cross + other.T) * scale
+
+    above = upper_blocks(n)
+    for number, (i, j) in enumerate(above):
+        whole[span(number), :] = block(i, j)
+    row, column = block_indices()
+    tail = len(above) + n // EDGE // 2
+    whole[tail * EDGE :, :] = jnp.zeros((whole.shape[0] - tail * EDGE, EDGE), jnp.float32)
+    for pair in range(n // EDGE // 2):
+        first, second = block(2 * pair, 2 * pair), block(2 * pair + 1, 2 * pair + 1)
+        whole[span(len(above) + pair), :] = jnp.where(row <= column, first, second)
+        diagonal = jnp.sum(jnp.where(row == column, second, 0.0), axis=0, keepdims=True)
+        whole[tail * EDGE + pair : tail * EDGE + pair + 1, :] = diagonal
     place = place_ref[0]
     part = keep_ref.shape[0] // 4
     for k in range(4):
@@ -106,7 +137,7 @@
 
 def local_gram(place, rows, count):
     n = rows.shape[1]
-    tall = len(upper_blocks(n // 128)) * 128
+    tall = packed_rows(n)
     half = jax.ShapeDtypeStruct((tall // 2, 128), jnp.float32)
     held = jax.ShapeDtypeStruct((n // 128, rows.shape[0], 128), jnp.float32)
     vmem = pl.BlockSpec(memory_space=pltpu.VMEM)
@@ -229,13 +260,23 @@
         theirs = pl.multiple_of(((1 - (place & 1)) * 4 + quarter) * part, 8)
         blocks[pl.ds(mine, part), :] = mine_ref[k * part : (k + 1) * part, :]
         blocks[pl.ds(theirs, part), :] = other_ref[k * part : (k + 1) * part, :]
-    edge = 128
-    for number, (i, j) in enumerate(upper_blocks(gram.shape[0] // edge)):
-        block = blocks[number * edge : (number + 1) * edge, :]
-        gram[i * edge : (i + 1) * edge, j * edge : (j + 1) * edge] = block
-        if i != j:
-            gram[j * edge : (j + 1) * edge, i * edge : (i + 1) * edge] = block.T
-
+    n = gram.shape[0]
+    above = upper_blocks(n)
+    for number, (i, j) in enumerate(above):
+        block = blocks[span(number), :]
+        gram[span(i), span(j)] = block
+        gram[span(j), span(i)] = block.T
+    row, column = block_indices()
+    tail = len(above) + n // EDGE // 2
+    for pair in range(n // EDGE // 2):
+        block = blocks[span(len(above) + pair), :]
+        turned = block.T
+        first, second = span(2 * pair), span(2 * pair + 1)
+        diagonal = blocks[tail * EDGE + pair : tail * EDGE + pair + 1, :]
+        gram[first, first] = jnp.where(row <= column, block, turned)
+        gram[second, second] = jnp.where(
+            row == column, diagonal, jnp.where(row > column, block, turned)
+        )
     gram_high[...], gram_low[...] = halves(gram[...])
 
     def by_gram(block):
@@ -251,7 +292,7 @@
         work[...] = dot(block, block, NT, HIGHEST)
         ahead[...] = by_gram(block)
         invert_factor(work, factor)
-        block_ref[...] = dot(factor[...], ahead[...], NN, HIGHEST)
+        block_ref[...] = split_dot(factor[...], ahead[...])
         return carry
 
     lax.fori_loop(0, sweeps - 1, sweep, 0)
@@ -370,8 +411,8 @@
     begin = 0
     for out in outs:
         fibres = out.shape[0] // per
-        span = slice(begin, begin + fibres * per)
-        product = split_product(high_ref[span, :], low_ref[span, :], both)
+        part = slice(begin, begin + fibres * per)
+        product = split_product(high_ref[part, :], low_ref[part, :], both)
         for j in range(per):
             out[pl.ds(j, fibres, stride=per), :] = product[j * fibres : (j + 1) * fibres]
         begin += fibres * per
@@ -455,11 +496,11 @@
         begin = first
         while begin < last:
             length = min(per - begin % per, last - begin)
-            span = pl.ds(begin - first, length)
+            done = pl.ds(begin - first, length)
             rows = piece[(begin - first) * size : (begin - first + length) * size, :]
-            results[k][span] = dot(rows, factor, NT, HIGHEST).reshape(length, size, -1)
+            results[k][done] = dot(rows, factor, NT, HIGHEST).reshape(length, size, -1)
             send = pltpu.make_async_copy(
-                results[k].at[span],
+                results[k].at[done],
                 out.at[begin // per, place_ref[1] ^ rank, pl.ds(begin % per, length)],
                 sems.at[k, begin // per],
             )
@@ -510,14 +551,14 @@
     def send(prepared):
         *sent, high, low = prepared
         ranks = [rank for rank, _, _ in EARLY]
-        return [*to_far(sent[:1], ranks[:1]), high, low], to_far(sent[1:], ranks[1:])
+        return [high, low], to_far(sent, ranks)
 
     keep, give, held = local_gram(place, rows, count)
     prepared = prepare(place, held)
-    mine, other, (soon, high, low), later = sum_gram(keep, give, prepared, send)
+    mine, other, (high, low), arrived = sum_gram(keep, give, prepared, send)
     block = iterate(place, mine, other, start_basis)
 
-    block, *arrived = lax.optimization_barrier((block, soon, *later))
+    block, *arrived = lax.optimization_barrier((block, *arrived))
     near, *far = project_sent(high, low, block)
     block, near, *far = lax.optimization_barrier((block, near, *far))
     far = to_far(far, FAR)

time: 75.7 us -> 74.9 us (0.989)
  starting transfers between devices: 21.3 us -> 19 us
  waiting for transfers between devices: 14.1 us -> 16.4 us
  Pallas kernels: 39.6 us -> 38.8 us
    ppermute x16 -> x15, waiting for transfers between devices: 14.1 us -> 16.4 us  [exchange(): return lax.ppermute(value, axes, [(i, i ^ mask) for i in range(size)])]
    ppermute x16 -> x15, starting transfers between devices: 21.3 us -> 19 us  [exchange(): return lax.ppermute(value, axes, [(i, i ^ mask) for i in range(size)])]
  transfers between devices with their start and end apart: 16 -> 15, of which waited for: 8 -> 10; matrix products, arithmetic and copies ran while one was open for 0% -> 0% of each run, Pallas kernels for 38% -> 37%
where the time goes in v5:
time: 74.9 us; the launch traced here: 74.7 us
  Pallas kernels  38.8 us (52%)
  starting transfers between devices  19 us (25%)
  waiting for transfers between devices  16.4 us (22%)
    ppermute x15, starting transfers between devices, exchange(): return lax.ppermute(value, axes, [(i, i ^ mask) for i in range(size)])  19 us
    ppermute x15, waiting for transfers between devices, exchange(): return lax.ppermute(value, axes, [(i, i ^ mask) for i in range(size)])  16.4 us
    pallas_call x1, Pallas kernels, iterate(): pl.pallas_call(functools.partial(sweep_kernel, SWEEPS), in_specs=[pl.Bloc...  13.9 us
    pallas_call x1, Pallas kernels, local_gram(): pl.pallas_call(functools.partial(gram_kernel, 1.0 / count), in_specs=[pl....  7.8 us
    pallas_call x4, Pallas kernels, finish(): pl.pallas_call(functools.partial(finish_kernel, ranks, firsts), in_specs=...  7.51 us
    pallas_call x1, Pallas kernels, last_factor(): pl.pallas_call(factor_kernel, in_specs=[vmem], out_specs=vmem, out_shape=...  3.67 us
    pallas_call x1, Pallas kernels, prepare(): pl.pallas_call(prepare_kernel, in_specs=[pl.BlockSpec(memory_space=pltpu....  2.56 us
    pallas_call x1, Pallas kernels, project_sent(): pl.pallas_call(sent_kernel, in_specs=[vmem] * 3, out_specs=[vmem] * 3, ou...  1.56 us
  transfers between devices with their start and end apart: 15, of which 10 were waited for; matrix products, arithmetic and copies ran while one was open for 0% of the time, Pallas kernels for 37%

profile of v5, /device:TPU:1, one launch (start us, length us, event | category | flops | bytes accessed | tf_op | source)
XLA Modules:
  0.0 74.7 jit_solution(11859339348404453125)
XLA Ops:
  0.0 0.1 pad_add_fusion.place_ref
  0.1 7.8 %local_gram.1 = (f32[544,128]{1,0:T(8,128)S(1)}, f32[544,128]{1,0:T(8,128)S(1)}, f32[4,4096,128]{2,1,0:T(8,128)S(1)}) custom-call(s32[2]{0:T(128)S(1)} %pad_add_fusion.place_ref, f32[4096,512]{1,0:T(8,128)} %bitcast.4), custom_call_target="tpu_custom_call" | custom-call | flops 1 | bytes 1 | tf_op jit(solution)/shard_map/local_gram/pallas_call | solution.py:144
  7.9 0.1 collective-permute-start
  8.0 1.5 %collective-permute-done = f32[544,128]{1,0:T(8,128)S(1)} collective-permute-done((f32[544,128]{1,0:T(8,128)S(1)}, f32[544,128]{1,0:T(8,128)S(1)}, u32[]{:S(2)}, u32[]{:S(2)}) %collective-permute-start) | collective-permute-done | bytes 278560 | tf_op jit(solution)/shard_map/ppermute | solution.py:46
  9.6 2.4 %collective-permute-start.1 = (f32[136,128]{1,0:T(8,128)S(1)}, f32[136,128]{1,0:T(8,128)S(1)}, u32[]{:S(2)}, u32[]{:S(2)}) collective-permute-start(f32[136,128]{1,0:T(8,128)S(1)} %get-tuple-element.59), channel_id=1, source_target_pairs={{0,4},{1,5},{2,6},{3,7},{4,0},{5,1},{6,2},{7,3},{8,12},{9,13},{10,... | collective-permute-start | bytes 208904 | tf_op jit(solution)/shard_map/ppermute | solution.py:46
  12.0 1.3 %collective-permute-start.3 = (f32[136,128]{1,0:T(8,128)S(1)}, f32[136,128]{1,0:T(8,128)S(1)}, u32[]{:S(2)}, u32[]{:S(2)}) collective-permute-start(f32[136,128]{1,0:T(8,128)S(1)} %get-tuple-element.60), channel_id=1, source_target_pairs={{0,12},{1,13},{2,14},{3,15},{4,8},{5,9},{6,10},{7,11},{8,4},{9,5},... | collective-permute-start | bytes 208904 | tf_op jit(solution)/shard_map/ppermute | solution.py:46
  13.2 0.0 collective-permute-start.2
  13.3 0.9 %collective-permute-done.1 = f32[136,128]{1,0:T(8,128)S(1)} collective-permute-done((f32[136,128]{1,0:T(8,128)S(1)}, f32[136,128]{1,0:T(8,128)S(1)}, u32[]{:S(2)}, u32[]{:S(2)}) %collective-permute-start.1) | collective-permute-done | bytes 69664 | tf_op jit(solution)/shard_map/ppermute | solution.py:46
  14.2 1.8 %collective-permute-done.3 = f32[136,128]{1,0:T(8,128)S(1)} collective-permute-done((f32[136,128]{1,0:T(8,128)S(1)}, f32[136,128]{1,0:T(8,128)S(1)}, u32[]{:S(2)}, u32[]{:S(2)}) %collective-permute-start.3) | collective-permute-done | bytes 69664 | tf_op jit(solution)/shard_map/ppermute | solution.py:46
  16.0 0.8 %collective-permute-done.2 = f32[136,128]{1,0:T(8,128)S(1)} collective-permute-done((f32[136,128]{1,0:T(8,128)S(1)}, f32[136,128]{1,0:T(8,128)S(1)}, u32[]{:S(2)}, u32[]{:S(2)}) %collective-permute-start.2) | collective-permute-done | bytes 69664 | tf_op jit(solution)/shard_map/ppermute | solution.py:46
  16.9 1.7 %collective-permute-start.4 = (f32[136,128]{1,0:T(8,128)S(1)}, f32[136,128]{1,0:T(8,128)S(1)}, u32[]{:S(2)}, u32[]{:S(2)}) collective-permute-start(f32[136,128]{1,0:T(8,128)S(1)} %fusion.1), channel_id=1, source_target_pairs={{0,2},{1,3},{2,0},{3,1},{4,6},{5,7},{6,4},{7,5},{8,10},{9,11},{10,... | collective-permute-start | bytes 208904 | tf_op jit(solution)/shard_map/ppermute | solution.py:46
  18.6 0.0 copy-start
  18.6 2.6 %prepare.1 = (f32[4,256,128]{2,1,0:T(8,128)S(1)}, f32[4,256,128]{2,1,0:T(8,128)S(1)}, bf16[2560,512]{1,0:T(8,128)(2,1)S(1)}, bf16[2560,512]{1,0:T(8,128)(2,1)S(1)}) custom-call(s32[2]{0:T(128)S(1)} %pad_add_fusion.place_ref, f32[4,4096,128]{2,1,0:T(8,128)S(1)} %get-tuple-element.34.held), custom_call_target="tpu_custom_call" | custom-call | flops 1 | bytes 1 | tf_op jit(solution)/shard_map/prepare/pallas_call | solution.py:397
  21.2 0.0 collective-permute-done.4
  21.2 2.4 %collective-permute-start.5 = (f32[136,128]{1,0:T(8,128)S(1)}, f32[136,128]{1,0:T(8,128)S(1)}, u32[]{:S(2)}, u32[]{:S(2)}) collective-permute-start(f32[136,128]{1,0:T(8,128)S(1)} %add.26), channel_id=1, source_target_pairs={{0,16},{1,17},{2,18},{3,19},{4,20},{5,21},{6,22},{7,23},{8,24},{9,... | collective-permute-start | bytes 208904 | tf_op jit(solution)/shard_map/ppermute | solution.py:46
  23.6 0.6 collective-permute-start.10
  24.1 3.1 %collective-permute-start.11 = (f32[4,256,128]{2,1,0:T(8,128)S(1)}, f32[4,256,128]{2,1,0:T(8,128)S(1)}, u32[]{:S(2)}, u32[]{:S(2)}) collective-permute-start(f32[4,256,128]{2,1,0:T(8,128)S(1)} %get-tuple-element.44), channel_id=1, source_target_pairs={{0,3},{1,2},{2,1},{3,0},{4,7},{5,6},{6,5},{7,4},{8,11},{9,10},{10,... | collective-permute-start | bytes 1572872 | tf_op jit(solution)/shard_map/ppermute | solution.py:46
  27.2 0.0 collective-permute-done.5
  27.2 1.8 %collective-permute-start.8 = (f32[136,128]{1,0:T(8,128)S(1)}, f32[136,128]{1,0:T(8,128)S(1)}, u32[]{:S(2)}, u32[]{:S(2)}) collective-permute-start(f32[136,128]{1,0:T(8,128)S(1)} %add.27), channel_id=1, source_target_pairs={{0,12},{1,13},{2,14},{3,15},{4,8},{5,9},{6,10},{7,11},{8,4},{9,5},... | collective-permute-start | bytes 208904 | tf_op jit(solution)/shard_map/ppermute | solution.py:46
  29.0 0.6 collective-permute-start.7
  29.7 0.2 collective-permute-start.6
  29.9 1.4 %collective-permute-done.8 = f32[136,128]{1,0:T(8,128)S(1)} collective-permute-done((f32[136,128]{1,0:T(8,128)S(1)}, f32[136,128]{1,0:T(8,128)S(1)}, u32[]{:S(2)}, u32[]{:S(2)}) %collective-permute-start.8) | collective-permute-done | bytes 69664 | tf_op jit(solution)/shard_map/ppermute | solution.py:46
  31.3 1.2 %collective-permute-done.7 = f32[136,128]{1,0:T(8,128)S(1)} collective-permute-done((f32[136,128]{1,0:T(8,128)S(1)}, f32[136,128]{1,0:T(8,128)S(1)}, u32[]{:S(2)}, u32[]{:S(2)}) %collective-permute-start.7) | collective-permute-done | bytes 69664 | tf_op jit(solution)/shard_map/ppermute | solution.py:46
  32.5 1.3 %collective-permute-done.6 = f32[136,128]{1,0:T(8,128)S(1)} collective-permute-done((f32[136,128]{1,0:T(8,128)S(1)}, f32[136,128]{1,0:T(8,128)S(1)}, u32[]{:S(2)}, u32[]{:S(2)}) %collective-permute-start.6) | collective-permute-done | bytes 69664 | tf_op jit(solution)/shard_map/ppermute | solution.py:46
  33.8 2.5 %collective-permute-start.9 = (f32[544,128]{1,0:T(8,128)S(1)}, f32[544,128]{1,0:T(8,128)S(1)}, u32[]{:S(2)}, u32[]{:S(2)}) collective-permute-start(f32[544,128]{1,0:T(8,128)S(1)} %pad_maximum_fusion.mine_ref), channel_id=1, source_target_pairs={{0,1},{1,0},{2,3},{3,2},{4,5},{5,4},{6,7},{7,6},{8,9},{9,8},{10,11... | collective-permute-start | bytes 835592 | tf_op jit(solution)/shard_map/ppermute | solution.py:46
  36.4 1.2 %collective-permute-done.9.other_ref = f32[544,128]{1,0:T(8,128)S(1)} collective-permute-done((f32[544,128]{1,0:T(8,128)S(1)}, f32[544,128]{1,0:T(8,128)S(1)}, u32[]{:S(2)}, u32[]{:S(2)}) %collective-permute-start.9) | collective-permute-done | bytes 278560 | tf_op jit(solution)/shard_map/ppermute | solution.py:46
  37.5 0.0 copy-done
  37.5 13.9 %iterate.1.block_ref = f32[128,512]{1,0:T(8,128)S(1)} custom-call(s32[2]{0:T(128)S(1)} %pad_add_fusion.place_ref, f32[544,128]{1,0:T(8,128)S(1)} %pad_maximum_fusion.mine_ref, f32[544,128]{1,0:T(8,128)S(1)} %collective-permute-done.9.other_ref, f32[512,128]{1,0:T(8,128)S(1)} %copy-done), custom_call_target="tpu_custom_call" | custom-call | flops 1 | bytes 1 | tf_op jit(solution)/shard_map/iterate/pallas_call | solution.py:304
  51.4 0.0 collective-permute-done.10.refs_0_
  51.5 0.0 collective-permute-done.11.refs_1_
  51.5 1.6 %project_sent.1 = (f32[1024,128]{1,0:T(8,128)S(1)}, f32[768,128]{1,0:T(8,128)S(1)}, f32[768,128]{1,0:T(8,128)S(1)}) custom-call(bf16[2560,512]{1,0:T(8,128)(2,1)S(1)} %get-tuple-element.46.high_ref, bf16[2560,512]{1,0:T(8,128)(2,1)S(1)} %get-tuple-element.47.low_ref, f32[128,512]{1,0:T(8,128)S(1)} %iterate.1.block_ref), custom_call_target="tpu_custom_call" | custom-call | flops 1 | bytes 1 | tf_op jit(solution)/shard_map/project_sent/pallas_call | solution.py:426
  53.0 0.4 collective-permute-start.13
  53.5 1.2 %collective-permute-start.14 = (f32[768,128]{1,0:T(8,128)S(1)}, f32[768,128]{1,0:T(8,128)S(1)}, u32[]{:S(2)}, u32[]{:S(2)}) collective-permute-start(f32[768,128]{1,0:T(8,128)S(1)} %get-tuple-element.54), channel_id=1, source_target_pairs={{0,2},{1,3},{2,0},{3,1},{4,6},{5,7},{6,4},{7,5},{8,10},{9,11},{10,... | collective-permute-start | bytes 1179656 | tf_op jit(solution)/shard_map/ppermute | solution.py:46
  54.7 0.6 collective-permute-start.12
  55.3 1.3 %project_own.1.refs_0_ = f32[1024,128]{1,0:T(8,128)S(1)} custom-call(s32[2]{0:T(128)S(1)} %pad_add_fusion.place_ref, f32[4,4096,128]{2,1,0:T(8,128)S(1)} %get-tuple-element.34.held, f32[128,512]{1,0:T(8,128)S(1)} %iterate.1.block_ref), custom_call_target="tpu_custom_call" | custom-call | flops 1 | bytes 1 | tf_op jit(solution)/shard_map/project_own/pallas_call | solution.py:449
  56.6 3.7 %last_factor.1.factor_ref = f32[128,128]{1,0:T(8,128)S(1)} custom-call(f32[128,512]{1,0:T(8,128)S(1)} %iterate.1.block_ref), custom_call_target="tpu_custom_call" | custom-call | flops 1 | bytes 1 | tf_op jit(solution)/shard_map/last_factor/pallas_call | solution.py:333
  60.2 0.5 project_arrived.1
  60.7 1.7 %finish_arrived.1.refs_1_ = f32[4,4,4,64,128]{4,3,2,1,0:T(8,128)} custom-call(s32[2]{0:T(128)S(1)} %pad_add_fusion.place_ref, f32[128,128]{1,0:T(8,128)S(1)} %last_factor.1.factor_ref, f32[256,128]{1,0:T(8,128)S(1)} %get-tuple-element.57.refs_0_, f32[256,128]{1,0:T(8,128)S(1)} %get-tuple-element.58.refs_1_), custom_call_target="tpu_custom_call" | custom-call | flops 1 | bytes 1 | tf_op jit(solution)/shard_map/finish_arrived/pallas_call | solution.py:525
  62.4 1.7 %collective-permute-done.14.refs_0_ = f32[768,128]{1,0:T(8,128)S(1)} collective-permute-done((f32[768,128]{1,0:T(8,128)S(1)}, f32[768,128]{1,0:T(8,128)S(1)}, u32[]{:S(2)}, u32[]{:S(2)}) %collective-permute-start.14) | collective-permute-done | bytes 393248 | tf_op jit(solution)/shard_map/ppermute | solution.py:46
  64.0 1.8 %finish_first_far.1.refs_2_ = f32[4,4,4,64,128]{4,3,2,1,0:T(8,128)} custom-call(s32[2]{0:T(128)S(1)} %pad_add_fusion.place_ref, f32[128,128]{1,0:T(8,128)S(1)} %last_factor.1.factor_ref, f32[768,128]{1,0:T(8,128)S(1)} %collective-permute-done.14.refs_0_, f32[4,4,4,64,128]{4,3,2,1,0:T(8,128)} %finish_arrived.1.refs_1_), custom_call_target="tpu_custom_call", output_to_operand_aliasing={{}: (3, {})} | custom-call | flops 1 | bytes 1 | tf_op jit(solution)/shard_map/finish_first_far/pallas_call | solution.py:525
  65.8 0.0 collective-permute-done.13.refs_1_
  65.8 2.3 %finish_near.1.refs_1_ = f32[4,4,4,64,128]{4,3,2,1,0:T(8,128)} custom-call(s32[2]{0:T(128)S(1)} %pad_add_fusion.place_ref, f32[128,128]{1,0:T(8,128)S(1)} %last_factor.1.factor_ref, f32[1024,128]{1,0:T(8,128)S(1)} %project_own.1.refs_0_, f32[1024,128]{1,0:T(8,128)S(1)} %collective-permute-done.13.refs_1_, ...), custom_call_target="tpu_custom_call", output_to_operand_aliasing={{}: (4, {})} | custom-call | flops 1 | bytes 1 | tf_op jit(solution)/shard_map/finish_near/pallas_call | solution.py:525
  68.1 4.6 %collective-permute-done.12.refs_0_ = f32[768,128]{1,0:T(8,128)S(1)} collective-permute-done((f32[768,128]{1,0:T(8,128)S(1)}, f32[768,128]{1,0:T(8,128)S(1)}, u32[]{:S(2)}, u32[]{:S(2)}) %collective-permute-start.12) | collective-permute-done | bytes 393248 | tf_op jit(solution)/shard_map/ppermute | solution.py:46
  72.7 1.8 %finish_last_far.1 = f32[4,4,4,64,128]{4,3,2,1,0:T(8,128)} custom-call(s32[2]{0:T(128)S(1)} %pad_add_fusion.place_ref, f32[128,128]{1,0:T(8,128)S(1)} %last_factor.1.factor_ref, f32[768,128]{1,0:T(8,128)S(1)} %collective-permute-done.12.refs_0_, f32[4,4,4,64,128]{4,3,2,1,0:T(8,128)} %finish_near.1.refs_1_), custom_call_target="tpu_custom_call", output_to_operand_aliasing={{}: (3, {})} | custom-call | flops 1 | bytes 1 | tf_op jit(solution)/shard_map/finish_last_far/pallas_call | solution.py:525
  (6 shorter events, 0.1 us)
Async XLA Ops:
  7.9 1.6 %collective-permute-start = (f32[544,128]{1,0:T(8,128)S(1)}, f32[544,128]{1,0:T(8,128)S(1)}, u32[]{:S(2)}, u32[]{:S(2)}) collective-permute-start(f32[544,128]{1,0:T(8,128)S(1)} %get-tuple-element.33), channel_id=1, source_target_pairs={{0,1},{1,0},{2,3},{3,2},{4,5},{5,4},{6,7},{7,6},{8,9},{9,8},{10,11... | collective-permute-start | bytes 835592 | tf_op jit(solution)/shard_map/ppermute | solution.py:46
  9.6 4.7 %collective-permute-start.1 = (f32[136,128]{1,0:T(8,128)S(1)}, f32[136,128]{1,0:T(8,128)S(1)}, u32[]{:S(2)}, u32[]{:S(2)}) collective-permute-start(f32[136,128]{1,0:T(8,128)S(1)} %get-tuple-element.59), channel_id=1, source_target_pairs={{0,4},{1,5},{2,6},{3,7},{4,0},{5,1},{6,2},{7,3},{8,12},{9,13},{10,... | collective-permute-start | bytes 208904 | tf_op jit(solution)/shard_map/ppermute | solution.py:46
  12.0 4.1 %collective-permute-start.3 = (f32[136,128]{1,0:T(8,128)S(1)}, f32[136,128]{1,0:T(8,128)S(1)}, u32[]{:S(2)}, u32[]{:S(2)}) collective-permute-start(f32[136,128]{1,0:T(8,128)S(1)} %get-tuple-element.60), channel_id=1, source_target_pairs={{0,12},{1,13},{2,14},{3,15},{4,8},{5,9},{6,10},{7,11},{8,4},{9,5},... | collective-permute-start | bytes 208904 | tf_op jit(solution)/shard_map/ppermute | solution.py:46
  13.2 3.6 %collective-permute-start.2 = (f32[136,128]{1,0:T(8,128)S(1)}, f32[136,128]{1,0:T(8,128)S(1)}, u32[]{:S(2)}, u32[]{:S(2)}) collective-permute-start(f32[136,128]{1,0:T(8,128)S(1)} %get-tuple-element.61), channel_id=1, source_target_pairs={{0,8},{1,9},{2,10},{3,11},{4,12},{5,13},{6,14},{7,15},{8,0},{9,1},... | collective-permute-start | bytes 208904 | tf_op jit(solution)/shard_map/ppermute | solution.py:46
  16.9 4.3 %collective-permute-start.4 = (f32[136,128]{1,0:T(8,128)S(1)}, f32[136,128]{1,0:T(8,128)S(1)}, u32[]{:S(2)}, u32[]{:S(2)}) collective-permute-start(f32[136,128]{1,0:T(8,128)S(1)} %fusion.1), channel_id=1, source_target_pairs={{0,2},{1,3},{2,0},{3,1},{4,6},{5,7},{6,4},{7,5},{8,10},{9,11},{10,... | collective-permute-start | bytes 208904 | tf_op jit(solution)/shard_map/ppermute | solution.py:46
  18.6 19.0 %copy-start = (f32[512,128]{1,0:T(8,128)S(1)}, f32[512,128]{1,0:T(8,128)}, u32[]{:S(2)}) copy-start(f32[512,128]{1,0:T(8,128)} %start_ref.1) | copy-start | bytes 786436
  21.2 6.0 %collective-permute-start.5 = (f32[136,128]{1,0:T(8,128)S(1)}, f32[136,128]{1,0:T(8,128)S(1)}, u32[]{:S(2)}, u32[]{:S(2)}) collective-permute-start(f32[136,128]{1,0:T(8,128)S(1)} %add.26), channel_id=1, source_target_pairs={{0,16},{1,17},{2,18},{3,19},{4,20},{5,21},{6,22},{7,23},{8,24},{9,... | collective-permute-start | bytes 208904 | tf_op jit(solution)/shard_map/ppermute | solution.py:46
  23.6 27.9 %collective-permute-start.10 = (f32[4,256,128]{2,1,0:T(8,128)S(1)}, f32[4,256,128]{2,1,0:T(8,128)S(1)}, u32[]{:S(2)}, u32[]{:S(2)}) collective-permute-start(f32[4,256,128]{2,1,0:T(8,128)S(1)} %get-tuple-element.43), channel_id=1, source_target_pairs={{0,2},{1,3},{2,0},{3,1},{4,6},{5,7},{6,4},{7,5},{8,10},{9,11},{10,... | collective-permute-start | bytes 1572872 | tf_op jit(solution)/shard_map/ppermute | solution.py:46
  24.1 27.3 %collective-permute-start.11 = (f32[4,256,128]{2,1,0:T(8,128)S(1)}, f32[4,256,128]{2,1,0:T(8,128)S(1)}, u32[]{:S(2)}, u32[]{:S(2)}) collective-permute-start(f32[4,256,128]{2,1,0:T(8,128)S(1)} %get-tuple-element.44), channel_id=1, source_target_pairs={{0,3},{1,2},{2,1},{3,0},{4,7},{5,6},{6,5},{7,4},{8,11},{9,10},{10,... | collective-permute-start | bytes 1572872 | tf_op jit(solution)/shard_map/ppermute | solution.py:46
  27.2 4.1 %collective-permute-start.8 = (f32[136,128]{1,0:T(8,128)S(1)}, f32[136,128]{1,0:T(8,128)S(1)}, u32[]{:S(2)}, u32[]{:S(2)}) collective-permute-start(f32[136,128]{1,0:T(8,128)S(1)} %add.27), channel_id=1, source_target_pairs={{0,12},{1,13},{2,14},{3,15},{4,8},{5,9},{6,10},{7,11},{8,4},{9,5},... | collective-permute-start | bytes 208904 | tf_op jit(solution)/shard_map/ppermute | solution.py:46
  29.0 3.5 %collective-permute-start.7 = (f32[136,128]{1,0:T(8,128)S(1)}, f32[136,128]{1,0:T(8,128)S(1)}, u32[]{:S(2)}, u32[]{:S(2)}) collective-permute-start(f32[136,128]{1,0:T(8,128)S(1)} %add.27), channel_id=1, source_target_pairs={{0,8},{1,9},{2,10},{3,11},{4,12},{5,13},{6,14},{7,15},{8,0},{9,1},... | collective-permute-start | bytes 208904 | tf_op jit(solution)/shard_map/ppermute | solution.py:46
  29.7 4.1 %collective-permute-start.6 = (f32[136,128]{1,0:T(8,128)S(1)}, f32[136,128]{1,0:T(8,128)S(1)}, u32[]{:S(2)}, u32[]{:S(2)}) collective-permute-start(f32[136,128]{1,0:T(8,128)S(1)} %add.27), channel_id=1, source_target_pairs={{0,4},{1,5},{2,6},{3,7},{4,0},{5,1},{6,2},{7,3},{8,12},{9,13},{10,... | collective-permute-start | bytes 208904 | tf_op jit(solution)/shard_map/ppermute | solution.py:46
  33.8 3.7 %collective-permute-start.9 = (f32[544,128]{1,0:T(8,128)S(1)}, f32[544,128]{1,0:T(8,128)S(1)}, u32[]{:S(2)}, u32[]{:S(2)}) collective-permute-start(f32[544,128]{1,0:T(8,128)S(1)} %pad_maximum_fusion.mine_ref), channel_id=1, source_target_pairs={{0,1},{1,0},{2,3},{3,2},{4,5},{5,4},{6,7},{7,6},{8,9},{9,8},{10,11... | collective-permute-start | bytes 835592 | tf_op jit(solution)/shard_map/ppermute | solution.py:46
  53.0 12.8 %collective-permute-start.13 = (f32[1024,128]{1,0:T(8,128)S(1)}, f32[1024,128]{1,0:T(8,128)S(1)}, u32[]{:S(2)}, u32[]{:S(2)}) collective-permute-start(f32[1024,128]{1,0:T(8,128)S(1)} %get-tuple-element.53), channel_id=1, source_target_pairs={{0,1},{1,0},{2,3},{3,2},{4,5},{5,4},{6,7},{7,6},{8,9},{9,8},{10,11... | collective-permute-start | bytes 1572872 | tf_op jit(solution)/shard_map/ppermute | solution.py:46
  53.5 10.6 %collective-permute-start.14 = (f32[768,128]{1,0:T(8,128)S(1)}, f32[768,128]{1,0:T(8,128)S(1)}, u32[]{:S(2)}, u32[]{:S(2)}) collective-permute-start(f32[768,128]{1,0:T(8,128)S(1)} %get-tuple-element.54), channel_id=1, source_target_pairs={{0,2},{1,3},{2,0},{3,1},{4,6},{5,7},{6,4},{7,5},{8,10},{9,11},{10,... | collective-permute-start | bytes 1179656 | tf_op jit(solution)/shard_map/ppermute | solution.py:46
  54.7 18.0 %collective-permute-start.12 = (f32[768,128]{1,0:T(8,128)S(1)}, f32[768,128]{1,0:T(8,128)S(1)}, u32[]{:S(2)}, u32[]{:S(2)}) collective-permute-start(f32[768,128]{1,0:T(8,128)S(1)} %get-tuple-element.52), channel_id=1, source_target_pairs={{0,3},{1,2},{2,1},{3,0},{4,7},{5,6},{6,5},{7,4},{8,11},{9,10},{10,... | collective-permute-start | bytes 1179656 | tf_op jit(solution)/shard_map/ppermute | solution.py:46

commit v6 on v5

--- a/solution.py
+++ b/solution.py
@@ -405,32 +405,37 @@
     )(place, held)
 
 
-def sent_kernel(high_ref, low_ref, block_ref, *outs):
+def sent_kernel(begin, groups, high_ref, low_ref, block_ref, *outs):
     per = 8 // SLABS
     both = weights(block_ref)
-    begin = 0
-    for out in outs:
-        fibres = out.shape[0] // per
-        part = slice(begin, begin + fibres * per)
-        product = split_product(high_ref[part, :], low_ref[part, :], both)
-        for j in range(per):
-            out[pl.ds(j, fibres, stride=per), :] = product[j * fibres : (j + 1) * fibres]
+    outs = list(outs)
+    for parts in groups:
+        some = [outs.pop(0) for _ in range(parts)]
+        fibres = sum(out.shape[0] for out in some) // per
+        rows = slice(begin, begin + fibres * per)
+        product = split_product(high_ref[rows, :], low_ref[rows, :], both)
+        first = 0
+        for out in some:
+            count = out.shape[0] // per
+            for j in range(per):
+                start = j * fibres + first
+                out[pl.ds(j, count, stride=per), :] = product[start : start + count]
+            first += count
         begin += fibres * per
 
 
-def project_sent(high, low, block):
+def project_sent(high, low, block, begin, groups, name):
     rank = block.shape[0]
-    parts = [CHUNKS - chunks_of(to) for to in (1, *FAR)]
-    sizes = [part * high.shape[0] // sum(parts) for part in parts]
-    vmem = pl.BlockSpec(memory_space=pltpu.VMEM)
-    return pl.pallas_call(
-        sent_kernel,
+    sizes = [size for group in groups for size in group]
+    vmem = pl.BlockSpec(memory_space=pltpu.VMEM)
+    return pl.pallas_call(
+        functools.partial(sent_kernel, begin, [len(group) for group in groups]),
         in_specs=[vmem] * 3,
-        out_specs=[vmem] * 3,
+        out_specs=[vmem] * len(sizes),
         out_shape=[jax.ShapeDtypeStruct((size, rank), jnp.float32) for size in sizes],
         cost_estimate=BRIEF,
         compiler_params=pltpu.CompilerParams(vmem_limit_bytes=16 * MIB),
-        name="project_sent",
+        name=name,
     )(high, low, block)
 
 
@@ -559,10 +564,14 @@
     block = iterate(place, mine, other, start_basis)
 
     block, *arrived = lax.optimization_barrier((block, *arrived))
-    near, *far = project_sent(high, low, block)
-    block, near, *far = lax.optimization_barrier((block, near, *far))
+    chunk = rows.shape[0] // SLABS // CHUNKS
+    near_rows = CHUNKS * chunk
+    far_rows = [[(CHUNKS - chunks_of(rank)) * chunk] for rank in FAR]
+    far = project_sent(high, low, block, near_rows, far_rows, "project_far")
+    block, far = lax.optimization_barrier((block, far))
     far = to_far(far, FAR)
-    near = exchange(near, "slab", 1)
+    near = project_sent(high, low, block, 0, [[near_rows // 2] * 2], "project_near")
+    near = [exchange(x, "slab", 1) for x in near]
     own = project_own(place, held, block)
     arrived = project_arrived(block, arrived)
     factor = last_factor(block)
@@ -572,7 +581,7 @@
     late = [chunks_of(rank) for rank in FAR]
     out = finish(place, factor, arrived, FAR, (0, 0), out, "finish_arrived")
     out = finish(place, factor, far[:1], FAR[:1], late[:1], out, "finish_first_far")
-    out = finish(place, factor, [own, near], (0, 1), (0, 0), out, "finish_near")
+    out = finish(place, factor, [own, *near], (0, 1, 1), (0, 0, CHUNKS // 2), out, "finish_near")
     out = finish(place, factor, far[1:], FAR[1:], late[1:], out, "finish_last_far")
     return out.reshape(nv, n2 * slabs, n3 // slabs, out.shape[-1])
 

time: 74.9 us -> 73.8 us (0.985)
  waiting for transfers between devices: 16.4 us -> 14.8 us
    ppermute x15 -> x16, waiting for transfers between devices: 16.4 us -> 14.8 us  [exchange(): return lax.ppermute(value, axes, [(i, i ^ mask) for i in range(size)])]
    ppermute x15 -> x16, starting transfers between devices: 19 us -> 19.4 us  [exchange(): return lax.ppermute(value, axes, [(i, i ^ mask) for i in range(size)])]
    pallas_call x1 -> x2, Pallas kernels: 1.56 us -> 1.73 us  [project_sent(): pl.pallas_call(functools.partial(sent_kernel, begin, [len(group) for grou...]
  transfers between devices with their start and end apart: 15 -> 16, of which waited for: 10 -> 9; matrix products, arithmetic and copies ran while one was open for 0% -> 0% of each run, Pallas kernels for 37% -> 39%
where the time goes in v6:
time: 73.8 us; the launch traced here: 73.7 us
  Pallas kernels  38.9 us (53%)
  starting transfers between devices  19.4 us (26%)
  waiting for transfers between devices  14.8 us (20%)
    ppermute x16, starting transfers between devices, exchange(): return lax.ppermute(value, axes, [(i, i ^ mask) for i in range(size)])  19.4 us
    ppermute x16, waiting for transfers between devices, exchange(): return lax.ppermute(value, axes, [(i, i ^ mask) for i in range(size)])  14.8 us
    pallas_call x1, Pallas kernels, iterate(): pl.pallas_call(functools.partial(sweep_kernel, SWEEPS), in_specs=[pl.Bloc...  13.9 us
    pallas_call x1, Pallas kernels, local_gram(): pl.pallas_call(functools.partial(gram_kernel, 1.0 / count), in_specs=[pl....  7.8 us
    pallas_call x4, Pallas kernels, finish(): pl.pallas_call(functools.partial(finish_kernel, ranks, firsts), in_specs=...  7.55 us
    pallas_call x1, Pallas kernels, last_factor(): pl.pallas_call(factor_kernel, in_specs=[vmem], out_specs=vmem, out_shape=...  3.67 us
    pallas_call x1, Pallas kernels, prepare(): pl.pallas_call(prepare_kernel, in_specs=[pl.BlockSpec(memory_space=pltpu....  2.56 us
    pallas_call x2, Pallas kernels, project_sent(): pl.pallas_call(functools.partial(sent_kernel, begin, [len(group) for grou...  1.73 us
  transfers between devices with their start and end apart: 16, of which 9 were waited for; matrix products, arithmetic and copies ran while one was open for 0% of the time, Pallas kernels for 39%

profile of v6, /device:TPU:1, one launch (start us, length us, event | category | flops | bytes accessed | tf_op | source)
XLA Modules:
  0.0 73.7 jit_solution(10288285307074740703)
XLA Ops:
  0.0 0.1 pad_add_fusion.place_ref
  0.1 7.8 %local_gram.1 = (f32[544,128]{1,0:T(8,128)S(1)}, f32[544,128]{1,0:T(8,128)S(1)}, f32[4,4096,128]{2,1,0:T(8,128)S(1)}) custom-call(s32[2]{0:T(128)S(1)} %pad_add_fusion.place_ref, f32[4096,512]{1,0:T(8,128)} %bitcast.4), custom_call_target="tpu_custom_call" | custom-call | flops 1 | bytes 1 | tf_op jit(solution)/shard_map/local_gram/pallas_call | solution.py:144
  7.9 0.1 collective-permute-start
  8.0 1.5 %collective-permute-done = f32[544,128]{1,0:T(8,128)S(1)} collective-permute-done((f32[544,128]{1,0:T(8,128)S(1)}, f32[544,128]{1,0:T(8,128)S(1)}, u32[]{:S(2)}, u32[]{:S(2)}) %collective-permute-start) | collective-permute-done | bytes 278560 | tf_op jit(solution)/shard_map/ppermute | solution.py:46
  9.6 2.4 %collective-permute-start.1 = (f32[136,128]{1,0:T(8,128)S(1)}, f32[136,128]{1,0:T(8,128)S(1)}, u32[]{:S(2)}, u32[]{:S(2)}) collective-permute-start(f32[136,128]{1,0:T(8,128)S(1)} %get-tuple-element.59), channel_id=1, source_target_pairs={{0,4},{1,5},{2,6},{3,7},{4,0},{5,1},{6,2},{7,3},{8,12},{9,13},{10,... | collective-permute-start | bytes 208904 | tf_op jit(solution)/shard_map/ppermute | solution.py:46
  12.0 1.3 %collective-permute-start.3 = (f32[136,128]{1,0:T(8,128)S(1)}, f32[136,128]{1,0:T(8,128)S(1)}, u32[]{:S(2)}, u32[]{:S(2)}) collective-permute-start(f32[136,128]{1,0:T(8,128)S(1)} %get-tuple-element.60), channel_id=1, source_target_pairs={{0,12},{1,13},{2,14},{3,15},{4,8},{5,9},{6,10},{7,11},{8,4},{9,5},... | collective-permute-start | bytes 208904 | tf_op jit(solution)/shard_map/ppermute | solution.py:46
  13.2 0.0 collective-permute-start.2
  13.3 0.9 %collective-permute-done.1 = f32[136,128]{1,0:T(8,128)S(1)} collective-permute-done((f32[136,128]{1,0:T(8,128)S(1)}, f32[136,128]{1,0:T(8,128)S(1)}, u32[]{:S(2)}, u32[]{:S(2)}) %collective-permute-start.1) | collective-permute-done | bytes 69664 | tf_op jit(solution)/shard_map/ppermute | solution.py:46
  14.2 1.8 %collective-permute-done.3 = f32[136,128]{1,0:T(8,128)S(1)} collective-permute-done((f32[136,128]{1,0:T(8,128)S(1)}, f32[136,128]{1,0:T(8,128)S(1)}, u32[]{:S(2)}, u32[]{:S(2)}) %collective-permute-start.3) | collective-permute-done | bytes 69664 | tf_op jit(solution)/shard_map/ppermute | solution.py:46
  16.0 0.8 %collective-permute-done.2 = f32[136,128]{1,0:T(8,128)S(1)} collective-permute-done((f32[136,128]{1,0:T(8,128)S(1)}, f32[136,128]{1,0:T(8,128)S(1)}, u32[]{:S(2)}, u32[]{:S(2)}) %collective-permute-start.2) | collective-permute-done | bytes 69664 | tf_op jit(solution)/shard_map/ppermute | solution.py:46
  16.9 1.7 %collective-permute-start.4 = (f32[136,128]{1,0:T(8,128)S(1)}, f32[136,128]{1,0:T(8,128)S(1)}, u32[]{:S(2)}, u32[]{:S(2)}) collective-permute-start(f32[136,128]{1,0:T(8,128)S(1)} %fusion.1), channel_id=1, source_target_pairs={{0,2},{1,3},{2,0},{3,1},{4,6},{5,7},{6,4},{7,5},{8,10},{9,11},{10,... | collective-permute-start | bytes 208904 | tf_op jit(solution)/shard_map/ppermute | solution.py:46
  18.6 0.0 copy-start
  18.6 2.6 %prepare.1 = (f32[4,256,128]{2,1,0:T(8,128)S(1)}, f32[4,256,128]{2,1,0:T(8,128)S(1)}, bf16[2560,512]{1,0:T(8,128)(2,1)S(1)}, bf16[2560,512]{1,0:T(8,128)(2,1)S(1)}) custom-call(s32[2]{0:T(128)S(1)} %pad_add_fusion.place_ref, f32[4,4096,128]{2,1,0:T(8,128)S(1)} %get-tuple-element.34.held), custom_call_target="tpu_custom_call" | custom-call | flops 1 | bytes 1 | tf_op jit(solution)/shard_map/prepare/pallas_call | solution.py:397
  21.2 0.0 collective-permute-done.4
  21.2 2.4 %collective-permute-start.5 = (f32[136,128]{1,0:T(8,128)S(1)}, f32[136,128]{1,0:T(8,128)S(1)}, u32[]{:S(2)}, u32[]{:S(2)}) collective-permute-start(f32[136,128]{1,0:T(8,128)S(1)} %add.26), channel_id=1, source_target_pairs={{0,16},{1,17},{2,18},{3,19},{4,20},{5,21},{6,22},{7,23},{8,24},{9,... | collective-permute-start | bytes 208904 | tf_op jit(solution)/shard_map/ppermute | solution.py:46
  23.6 0.6 collective-permute-start.10
  24.1 3.1 %collective-permute-start.11 = (f32[4,256,128]{2,1,0:T(8,128)S(1)}, f32[4,256,128]{2,1,0:T(8,128)S(1)}, u32[]{:S(2)}, u32[]{:S(2)}) collective-permute-start(f32[4,256,128]{2,1,0:T(8,128)S(1)} %get-tuple-element.44), channel_id=1, source_target_pairs={{0,3},{1,2},{2,1},{3,0},{4,7},{5,6},{6,5},{7,4},{8,11},{9,10},{10,... | collective-permute-start | bytes 1572872 | tf_op jit(solution)/shard_map/ppermute | solution.py:46
  27.2 0.0 collective-permute-done.5
  27.2 1.8 %collective-permute-start.8 = (f32[136,128]{1,0:T(8,128)S(1)}, f32[136,128]{1,0:T(8,128)S(1)}, u32[]{:S(2)}, u32[]{:S(2)}) collective-permute-start(f32[136,128]{1,0:T(8,128)S(1)} %add.27), channel_id=1, source_target_pairs={{0,12},{1,13},{2,14},{3,15},{4,8},{5,9},{6,10},{7,11},{8,4},{9,5},... | collective-permute-start | bytes 208904 | tf_op jit(solution)/shard_map/ppermute | solution.py:46
  29.0 0.6 collective-permute-start.7
  29.7 0.2 collective-permute-start.6
  29.9 1.4 %collective-permute-done.8 = f32[136,128]{1,0:T(8,128)S(1)} collective-permute-done((f32[136,128]{1,0:T(8,128)S(1)}, f32[136,128]{1,0:T(8,128)S(1)}, u32[]{:S(2)}, u32[]{:S(2)}) %collective-permute-start.8) | collective-permute-done | bytes 69664 | tf_op jit(solution)/shard_map/ppermute | solution.py:46
  31.3 1.2 %collective-permute-done.7 = f32[136,128]{1,0:T(8,128)S(1)} collective-permute-done((f32[136,128]{1,0:T(8,128)S(1)}, f32[136,128]{1,0:T(8,128)S(1)}, u32[]{:S(2)}, u32[]{:S(2)}) %collective-permute-start.7) | collective-permute-done | bytes 69664 | tf_op jit(solution)/shard_map/ppermute | solution.py:46
  32.5 1.3 %collective-permute-done.6 = f32[136,128]{1,0:T(8,128)S(1)} collective-permute-done((f32[136,128]{1,0:T(8,128)S(1)}, f32[136,128]{1,0:T(8,128)S(1)}, u32[]{:S(2)}, u32[]{:S(2)}) %collective-permute-start.6) | collective-permute-done | bytes 69664 | tf_op jit(solution)/shard_map/ppermute | solution.py:46
  33.8 2.5 %collective-permute-start.9 = (f32[544,128]{1,0:T(8,128)S(1)}, f32[544,128]{1,0:T(8,128)S(1)}, u32[]{:S(2)}, u32[]{:S(2)}) collective-permute-start(f32[544,128]{1,0:T(8,128)S(1)} %pad_maximum_fusion.mine_ref), channel_id=1, source_target_pairs={{0,1},{1,0},{2,3},{3,2},{4,5},{5,4},{6,7},{7,6},{8,9},{9,8},{10,11... | collective-permute-start | bytes 835592 | tf_op jit(solution)/shard_map/ppermute | solution.py:46
  36.4 1.2 %collective-permute-done.9.other_ref = f32[544,128]{1,0:T(8,128)S(1)} collective-permute-done((f32[544,128]{1,0:T(8,128)S(1)}, f32[544,128]{1,0:T(8,128)S(1)}, u32[]{:S(2)}, u32[]{:S(2)}) %collective-permute-start.9) | collective-permute-done | bytes 278560 | tf_op jit(solution)/shard_map/ppermute | solution.py:46
  37.5 0.0 copy-done
  37.5 13.9 %iterate.1.block_ref = f32[128,512]{1,0:T(8,128)S(1)} custom-call(s32[2]{0:T(128)S(1)} %pad_add_fusion.place_ref, f32[544,128]{1,0:T(8,128)S(1)} %pad_maximum_fusion.mine_ref, f32[544,128]{1,0:T(8,128)S(1)} %collective-permute-done.9.other_ref, f32[512,128]{1,0:T(8,128)S(1)} %copy-done), custom_call_target="tpu_custom_call" | custom-call | flops 1 | bytes 1 | tf_op jit(solution)/shard_map/iterate/pallas_call | solution.py:304
  51.4 0.0 collective-permute-done.10.refs_0_
  51.4 0.0 collective-permute-done.11.refs_1_
  51.5 1.0 %project_far.1 = (f32[768,128]{1,0:T(8,128)S(1)}, f32[768,128]{1,0:T(8,128)S(1)}) custom-call(bf16[2560,512]{1,0:T(8,128)(2,1)S(1)} %get-tuple-element.46.high_ref, bf16[2560,512]{1,0:T(8,128)(2,1)S(1)} %get-tuple-element.47.low_ref, f32[128,512]{1,0:T(8,128)S(1)} %iterate.1.block_ref), custom_call_target="tpu_custom_call" | custom-call | flops 1 | bytes 1 | tf_op jit(solution)/shard_map/project_far/pallas_call | solution.py:431
  52.5 1.3 %collective-permute-start.15 = (f32[768,128]{1,0:T(8,128)S(1)}, f32[768,128]{1,0:T(8,128)S(1)}, u32[]{:S(2)}, u32[]{:S(2)}) collective-permute-start(f32[768,128]{1,0:T(8,128)S(1)} %get-tuple-element.54), channel_id=1, source_target_pairs={{0,2},{1,3},{2,0},{3,1},{4,6},{5,7},{6,4},{7,5},{8,10},{9,11},{10,... | collective-permute-start | bytes 1179656 | tf_op jit(solution)/shard_map/ppermute | solution.py:46
  53.8 0.8 %collective-permute-start.12 = (f32[768,128]{1,0:T(8,128)S(1)}, f32[768,128]{1,0:T(8,128)S(1)}, u32[]{:S(2)}, u32[]{:S(2)}) collective-permute-start(f32[768,128]{1,0:T(8,128)S(1)} %get-tuple-element.51), channel_id=1, source_target_pairs={{0,3},{1,2},{2,1},{3,0},{4,7},{5,6},{6,5},{7,4},{8,11},{9,10},{10,... | collective-permute-start | bytes 1179656 | tf_op jit(solution)/shard_map/ppermute | solution.py:46
  54.5 0.7 project_near.1
  55.3 0.1 collective-permute-start.13
  55.3 0.5 collective-permute-start.14
  55.8 1.3 %project_own.1.refs_0_ = f32[1024,128]{1,0:T(8,128)S(1)} custom-call(s32[2]{0:T(128)S(1)} %pad_add_fusion.place_ref, f32[4,4096,128]{2,1,0:T(8,128)S(1)} %get-tuple-element.34.held, f32[128,512]{1,0:T(8,128)S(1)} %iterate.1.block_ref), custom_call_target="tpu_custom_call" | custom-call | flops 1 | bytes 1 | tf_op jit(solution)/shard_map/project_own/pallas_call | solution.py:454
  57.1 3.7 %last_factor.1.factor_ref = f32[128,128]{1,0:T(8,128)S(1)} custom-call(f32[128,512]{1,0:T(8,128)S(1)} %iterate.1.block_ref), custom_call_target="tpu_custom_call" | custom-call | flops 1 | bytes 1 | tf_op jit(solution)/shard_map/last_factor/pallas_call | solution.py:333
  60.8 0.5 project_arrived.1
  61.3 1.7 %finish_arrived.1.refs_1_ = f32[4,4,4,64,128]{4,3,2,1,0:T(8,128)} custom-call(s32[2]{0:T(128)S(1)} %pad_add_fusion.place_ref, f32[128,128]{1,0:T(8,128)S(1)} %last_factor.1.factor_ref, f32[256,128]{1,0:T(8,128)S(1)} %get-tuple-element.57.refs_0_, f32[256,128]{1,0:T(8,128)S(1)} %get-tuple-element.58.refs_1_), custom_call_target="tpu_custom_call" | custom-call | flops 1 | bytes 1 | tf_op jit(solution)/shard_map/finish_arrived/pallas_call | solution.py:530
  63.0 0.0 collective-permute-done.15.refs_0_
  63.0 1.8 %finish_first_far.1.refs_3_ = f32[4,4,4,64,128]{4,3,2,1,0:T(8,128)} custom-call(s32[2]{0:T(128)S(1)} %pad_add_fusion.place_ref, f32[128,128]{1,0:T(8,128)S(1)} %last_factor.1.factor_ref, f32[768,128]{1,0:T(8,128)S(1)} %collective-permute-done.15.refs_0_, f32[4,4,4,64,128]{4,3,2,1,0:T(8,128)} %finish_arrived.1.refs_1_), custom_call_target="tpu_custom_call", output_to_operand_aliasing={{}: (3, {})} | custom-call | flops 1 | bytes 1 | tf_op jit(solution)/shard_map/finish_first_far/pallas_call | solution.py:530
  64.7 0.0 collective-permute-done.13.refs_1_
  64.7 0.0 collective-permute-done.14.refs_2_
  64.8 2.3 %finish_near.1.refs_1_ = f32[4,4,4,64,128]{4,3,2,1,0:T(8,128)} custom-call(s32[2]{0:T(128)S(1)} %pad_add_fusion.place_ref, f32[128,128]{1,0:T(8,128)S(1)} %last_factor.1.factor_ref, f32[1024,128]{1,0:T(8,128)S(1)} %project_own.1.refs_0_, f32[512,128]{1,0:T(8,128)S(1)} %collective-permute-done.13.refs_1_, ...), custom_call_target="tpu_custom_call", output_to_operand_aliasing={{}: (5, {})} | custom-call | flops 1 | bytes 1 | tf_op jit(solution)/shard_map/finish_near/pallas_call | solution.py:530
  67.1 4.7 %collective-permute-done.12.refs_0_ = f32[768,128]{1,0:T(8,128)S(1)} collective-permute-done((f32[768,128]{1,0:T(8,128)S(1)}, f32[768,128]{1,0:T(8,128)S(1)}, u32[]{:S(2)}, u32[]{:S(2)}) %collective-permute-start.12) | collective-permute-done | bytes 393248 | tf_op jit(solution)/shard_map/ppermute | solution.py:46
  71.8 1.8 %finish_last_far.1 = f32[4,4,4,64,128]{4,3,2,1,0:T(8,128)} custom-call(s32[2]{0:T(128)S(1)} %pad_add_fusion.place_ref, f32[128,128]{1,0:T(8,128)S(1)} %last_factor.1.factor_ref, f32[768,128]{1,0:T(8,128)S(1)} %collective-permute-done.12.refs_0_, f32[4,4,4,64,128]{4,3,2,1,0:T(8,128)} %finish_near.1.refs_1_), custom_call_target="tpu_custom_call", output_to_operand_aliasing={{}: (3, {})} | custom-call | flops 1 | bytes 1 | tf_op jit(solution)/shard_map/finish_last_far/pallas_call | solution.py:530
  (6 shorter events, 0.1 us)
Async XLA Ops:
  7.9 1.6 %collective-permute-start = (f32[544,128]{1,0:T(8,128)S(1)}, f32[544,128]{1,0:T(8,128)S(1)}, u32[]{:S(2)}, u32[]{:S(2)}) collective-permute-start(f32[544,128]{1,0:T(8,128)S(1)} %get-tuple-element.33), channel_id=1, source_target_pairs={{0,1},{1,0},{2,3},{3,2},{4,5},{5,4},{6,7},{7,6},{8,9},{9,8},{10,11... | collective-permute-start | bytes 835592 | tf_op jit(solution)/shard_map/ppermute | solution.py:46
  9.6 4.7 %collective-permute-start.1 = (f32[136,128]{1,0:T(8,128)S(1)}, f32[136,128]{1,0:T(8,128)S(1)}, u32[]{:S(2)}, u32[]{:S(2)}) collective-permute-start(f32[136,128]{1,0:T(8,128)S(1)} %get-tuple-element.59), channel_id=1, source_target_pairs={{0,4},{1,5},{2,6},{3,7},{4,0},{5,1},{6,2},{7,3},{8,12},{9,13},{10,... | collective-permute-start | bytes 208904 | tf_op jit(solution)/shard_map/ppermute | solution.py:46
  12.0 4.1 %collective-permute-start.3 = (f32[136,128]{1,0:T(8,128)S(1)}, f32[136,128]{1,0:T(8,128)S(1)}, u32[]{:S(2)}, u32[]{:S(2)}) collective-permute-start(f32[136,128]{1,0:T(8,128)S(1)} %get-tuple-element.60), channel_id=1, source_target_pairs={{0,12},{1,13},{2,14},{3,15},{4,8},{5,9},{6,10},{7,11},{8,4},{9,5},... | collective-permute-start | bytes 208904 | tf_op jit(solution)/shard_map/ppermute | solution.py:46
  13.2 3.6 %collective-permute-start.2 = (f32[136,128]{1,0:T(8,128)S(1)}, f32[136,128]{1,0:T(8,128)S(1)}, u32[]{:S(2)}, u32[]{:S(2)}) collective-permute-start(f32[136,128]{1,0:T(8,128)S(1)} %get-tuple-element.61), channel_id=1, source_target_pairs={{0,8},{1,9},{2,10},{3,11},{4,12},{5,13},{6,14},{7,15},{8,0},{9,1},... | collective-permute-start | bytes 208904 | tf_op jit(solution)/shard_map/ppermute | solution.py:46
  16.9 4.3 %collective-permute-start.4 = (f32[136,128]{1,0:T(8,128)S(1)}, f32[136,128]{1,0:T(8,128)S(1)}, u32[]{:S(2)}, u32[]{:S(2)}) collective-permute-start(f32[136,128]{1,0:T(8,128)S(1)} %fusion.1), channel_id=1, source_target_pairs={{0,2},{1,3},{2,0},{3,1},{4,6},{5,7},{6,4},{7,5},{8,10},{9,11},{10,... | collective-permute-start | bytes 208904 | tf_op jit(solution)/shard_map/ppermute | solution.py:46
  18.6 19.0 %copy-start = (f32[512,128]{1,0:T(8,128)S(1)}, f32[512,128]{1,0:T(8,128)}, u32[]{:S(2)}) copy-start(f32[512,128]{1,0:T(8,128)} %start_ref.1) | copy-start | bytes 786436
  21.2 6.0 %collective-permute-start.5 = (f32[136,128]{1,0:T(8,128)S(1)}, f32[136,128]{1,0:T(8,128)S(1)}, u32[]{:S(2)}, u32[]{:S(2)}) collective-permute-start(f32[136,128]{1,0:T(8,128)S(1)} %add.26), channel_id=1, source_target_pairs={{0,16},{1,17},{2,18},{3,19},{4,20},{5,21},{6,22},{7,23},{8,24},{9,... | collective-permute-start | bytes 208904 | tf_op jit(solution)/shard_map/ppermute | solution.py:46
  23.6 27.9 %collective-permute-start.10 = (f32[4,256,128]{2,1,0:T(8,128)S(1)}, f32[4,256,128]{2,1,0:T(8,128)S(1)}, u32[]{:S(2)}, u32[]{:S(2)}) collective-permute-start(f32[4,256,128]{2,1,0:T(8,128)S(1)} %get-tuple-element.43), channel_id=1, source_target_pairs={{0,2},{1,3},{2,0},{3,1},{4,6},{5,7},{6,4},{7,5},{8,10},{9,11},{10,... | collective-permute-start | bytes 1572872 | tf_op jit(solution)/shard_map/ppermute | solution.py:46
  24.1 27.3 %collective-permute-start.11 = (f32[4,256,128]{2,1,0:T(8,128)S(1)}, f32[4,256,128]{2,1,0:T(8,128)S(1)}, u32[]{:S(2)}, u32[]{:S(2)}) collective-permute-start(f32[4,256,128]{2,1,0:T(8,128)S(1)} %get-tuple-element.44), channel_id=1, source_target_pairs={{0,3},{1,2},{2,1},{3,0},{4,7},{5,6},{6,5},{7,4},{8,11},{9,10},{10,... | collective-permute-start | bytes 1572872 | tf_op jit(solution)/shard_map/ppermute | solution.py:46
  27.2 4.1 %collective-permute-start.8 = (f32[136,128]{1,0:T(8,128)S(1)}, f32[136,128]{1,0:T(8,128)S(1)}, u32[]{:S(2)}, u32[]{:S(2)}) collective-permute-start(f32[136,128]{1,0:T(8,128)S(1)} %add.27), channel_id=1, source_target_pairs={{0,12},{1,13},{2,14},{3,15},{4,8},{5,9},{6,10},{7,11},{8,4},{9,5},... | collective-permute-start | bytes 208904 | tf_op jit(solution)/shard_map/ppermute | solution.py:46
  29.0 3.5 %collective-permute-start.7 = (f32[136,128]{1,0:T(8,128)S(1)}, f32[136,128]{1,0:T(8,128)S(1)}, u32[]{:S(2)}, u32[]{:S(2)}) collective-permute-start(f32[136,128]{1,0:T(8,128)S(1)} %add.27), channel_id=1, source_target_pairs={{0,8},{1,9},{2,10},{3,11},{4,12},{5,13},{6,14},{7,15},{8,0},{9,1},... | collective-permute-start | bytes 208904 | tf_op jit(solution)/shard_map/ppermute | solution.py:46
  29.7 4.1 %collective-permute-start.6 = (f32[136,128]{1,0:T(8,128)S(1)}, f32[136,128]{1,0:T(8,128)S(1)}, u32[]{:S(2)}, u32[]{:S(2)}) collective-permute-start(f32[136,128]{1,0:T(8,128)S(1)} %add.27), channel_id=1, source_target_pairs={{0,4},{1,5},{2,6},{3,7},{4,0},{5,1},{6,2},{7,3},{8,12},{9,13},{10,... | collective-permute-start | bytes 208904 | tf_op jit(solution)/shard_map/ppermute | solution.py:46
  33.8 3.7 %collective-permute-start.9 = (f32[544,128]{1,0:T(8,128)S(1)}, f32[544,128]{1,0:T(8,128)S(1)}, u32[]{:S(2)}, u32[]{:S(2)}) collective-permute-start(f32[544,128]{1,0:T(8,128)S(1)} %pad_maximum_fusion.mine_ref), channel_id=1, source_target_pairs={{0,1},{1,0},{2,3},{3,2},{4,5},{5,4},{6,7},{7,6},{8,9},{9,8},{10,11... | collective-permute-start | bytes 835592 | tf_op jit(solution)/shard_map/ppermute | solution.py:46
  52.5 10.5 %collective-permute-start.15 = (f32[768,128]{1,0:T(8,128)S(1)}, f32[768,128]{1,0:T(8,128)S(1)}, u32[]{:S(2)}, u32[]{:S(2)}) collective-permute-start(f32[768,128]{1,0:T(8,128)S(1)} %get-tuple-element.54), channel_id=1, source_target_pairs={{0,2},{1,3},{2,0},{3,1},{4,6},{5,7},{6,4},{7,5},{8,10},{9,11},{10,... | collective-permute-start | bytes 1179656 | tf_op jit(solution)/shard_map/ppermute | solution.py:46
  53.8 18.0 %collective-permute-start.12 = (f32[768,128]{1,0:T(8,128)S(1)}, f32[768,128]{1,0:T(8,128)S(1)}, u32[]{:S(2)}, u32[]{:S(2)}) collective-permute-start(f32[768,128]{1,0:T(8,128)S(1)} %get-tuple-element.51), channel_id=1, source_target_pairs={{0,3},{1,2},{2,1},{3,0},{4,7},{5,6},{6,5},{7,4},{8,11},{9,10},{10,... | collective-permute-start | bytes 1179656 | tf_op jit(solution)/shard_map/ppermute | solution.py:46
  55.3 9.5 %collective-permute-start.13 = (f32[512,128]{1,0:T(8,128)S(1)}, f32[512,128]{1,0:T(8,128)S(1)}, u32[]{:S(2)}, u32[]{:S(2)}) collective-permute-start(f32[512,128]{1,0:T(8,128)S(1)} %get-tuple-element.52), channel_id=1, source_target_pairs={{0,1},{1,0},{2,3},{3,2},{4,5},{5,4},{6,7},{7,6},{8,9},{9,8},{10,11... | collective-permute-start | bytes 786440 | tf_op jit(solution)/shard_map/ppermute | solution.py:46
  55.3 9.4 %collective-permute-start.14 = (f32[512,128]{1,0:T(8,128)S(1)}, f32[512,128]{1,0:T(8,128)S(1)}, u32[]{:S(2)}, u32[]{:S(2)}) collective-permute-start(f32[512,128]{1,0:T(8,128)S(1)} %get-tuple-element.53), channel_id=1, source_target_pairs={{0,1},{1,0},{2,3},{3,2},{4,5},{5,4},{6,7},{7,6},{8,9},{9,8},{10,11... | collective-permute-start | bytes 786440 | tf_op jit(solution)/shard_map/ppermute | solution.py:46

commit v7 on v6

--- a/solution.py
+++ b/solution.py
@@ -31,12 +31,10 @@
     return high, (x - high.astype(jnp.float32)).astype(jnp.bfloat16)
 
 
-def split_dot(a, b):
-    a_high, a_low = halves(a)
-    b_high, b_low = halves(b)
-    both = dot(jnp.concatenate([a_high, a_low], axis=0), b_high, NN)
-    rows = a.shape[0]
-    return both[:rows] + both[rows:] + dot(a_high, b_low, NN)
+def thirds(x):
+    high = x.astype(jnp.bfloat16)
+    middle, low = halves(x - high.astype(jnp.float32))
+    return high, middle, low
 
 
 def exchange(value, axes, mask):
@@ -249,7 +247,7 @@
 
 
 def sweep_kernel(
-    sweeps, place_ref, mine_ref, other_ref, start_ref, block_ref, blocks, gram, gram_high, gram_low,
+    sweeps, place_ref, mine_ref, other_ref, start_ref, block_ref, blocks, gram, gram_high, gram_middle, gram_low,
     ahead, work, factor,
 ):
     place = place_ref[0]
@@ -277,13 +275,15 @@
         gram[second, second] = jnp.where(
             row == column, diagonal, jnp.where(row > column, block, turned)
         )
-    gram_high[...], gram_low[...] = halves(gram[...])
+    gram_high[...], gram_middle[...], gram_low[...] = thirds(gram[...])
 
     def by_gram(block):
-        high, low = halves(block)
-        both = dot(jnp.concatenate([high, low], axis=0), gram_high[...], NN)
         rank = block.shape[0]
-        return both[:rank] + both[rank:] + dot(high, gram_low[...], NN)
+        parts = jnp.concatenate(thirds(block), axis=0)
+        large = dot(parts, gram_high[...], NN)
+        small = dot(parts[: 2 * rank], gram_middle[...], NN)
+        least = dot(parts[:rank], gram_low[...], NN) + small[rank:] + large[2 * rank :]
+        return large[:rank] + (large[rank : 2 * rank] + small[:rank] + least)
 
     block_ref[...] = by_gram(start_ref[...].T)
 
@@ -292,7 +292,7 @@
         work[...] = dot(block, block, NT, HIGHEST)
         ahead[...] = by_gram(block)
         invert_factor(work, factor)
-        block_ref[...] = split_dot(factor[...], ahead[...])
+        block_ref[...] = dot(factor[...], ahead[...], NN, HIGHEST)
         return carry
 
     lax.fori_loop(0, sweeps - 1, sweep, 0)
@@ -309,6 +309,7 @@
         scratch_shapes=[
             pltpu.VMEM((2 * mine.shape[0], 128), jnp.float32),
             pltpu.VMEM((n, n), jnp.float32),
+            pltpu.VMEM((n, n), jnp.bfloat16),
             pltpu.VMEM((n, n), jnp.bfloat16),
             pltpu.VMEM((n, n), jnp.bfloat16),
             pltpu.VMEM((rank, n), jnp.float32),

time: 73.8 us -> 76.5 us (1.037)
  Pallas kernels: 38.9 us -> 41.6 us
    pallas_call x1, Pallas kernels: 13.9 us -> 16.5 us  [iterate(): pl.pallas_call(functools.partial(sweep_kernel, SWEEPS), in_specs=[pl.Bloc...]
  transfers between devices with their start and end apart: 16 -> 16, of which waited for: 9 -> 9; matrix products, arithmetic and copies ran while one was open for 0% -> 0% of each run, Pallas kernels for 39% -> 41%
where the time goes in v7:
time: 76.5 us; the launch traced here: 76.3 us
  Pallas kernels  41.6 us (54%)
  starting transfers between devices  19.4 us (25%)
  waiting for transfers between devices  14.8 us (19%)
    ppermute x16, starting transfers between devices, exchange(): return lax.ppermute(value, axes, [(i, i ^ mask) for i in range(size)])  19.4 us
    pallas_call x1, Pallas kernels, iterate(): pl.pallas_call(functools.partial(sweep_kernel, SWEEPS), in_specs=[pl.Bloc...  16.5 us
    ppermute x16, waiting for transfers between devices, exchange(): return lax.ppermute(value, axes, [(i, i ^ mask) for i in range(size)])  14.8 us
    pallas_call x1, Pallas kernels, local_gram(): pl.pallas_call(functools.partial(gram_kernel, 1.0 / count), in_specs=[pl....  7.8 us
    pallas_call x4, Pallas kernels, finish(): pl.pallas_call(functools.partial(finish_kernel, ranks, firsts), in_specs=...  7.55 us
    pallas_call x1, Pallas kernels, last_factor(): pl.pallas_call(factor_kernel, in_specs=[vmem], out_specs=vmem, out_shape=...  3.67 us
    pallas_call x1, Pallas kernels, prepare(): pl.pallas_call(prepare_kernel, in_specs=[pl.BlockSpec(memory_space=pltpu....  2.56 us
    pallas_call x2, Pallas kernels, project_sent(): pl.pallas_call(functools.partial(sent_kernel, begin, [len(group) for grou...  1.73 us
  transfers between devices with their start and end apart: 16, of which 9 were waited for; matrix products, arithmetic and copies ran while one was open for 0% of the time, Pallas kernels for 41%

profile of v7, /device:TPU:1, one launch (start us, length us, event | category | flops | bytes accessed | tf_op | source)
XLA Modules:
  0.0 76.3 jit_solution(6321815168653150979)
XLA Ops:
  0.0 0.1 pad_add_fusion.place_ref
  0.1 7.8 %local_gram.1 = (f32[544,128]{1,0:T(8,128)S(1)}, f32[544,128]{1,0:T(8,128)S(1)}, f32[4,4096,128]{2,1,0:T(8,128)S(1)}) custom-call(s32[2]{0:T(128)S(1)} %pad_add_fusion.place_ref, f32[4096,512]{1,0:T(8,128)} %bitcast.4), custom_call_target="tpu_custom_call" | custom-call | flops 1 | bytes 1 | tf_op jit(solution)/shard_map/local_gram/pallas_call | solution.py:142
  7.9 0.1 collective-permute-start
  8.0 1.5 %collective-permute-done = f32[544,128]{1,0:T(8,128)S(1)} collective-permute-done((f32[544,128]{1,0:T(8,128)S(1)}, f32[544,128]{1,0:T(8,128)S(1)}, u32[]{:S(2)}, u32[]{:S(2)}) %collective-permute-start) | collective-permute-done | bytes 278560 | tf_op jit(solution)/shard_map/ppermute | solution.py:44
  9.6 2.4 %collective-permute-start.1 = (f32[136,128]{1,0:T(8,128)S(1)}, f32[136,128]{1,0:T(8,128)S(1)}, u32[]{:S(2)}, u32[]{:S(2)}) collective-permute-start(f32[136,128]{1,0:T(8,128)S(1)} %get-tuple-element.59), channel_id=1, source_target_pairs={{0,4},{1,5},{2,6},{3,7},{4,0},{5,1},{6,2},{7,3},{8,12},{9,13},{10,... | collective-permute-start | bytes 208904 | tf_op jit(solution)/shard_map/ppermute | solution.py:44
  12.0 1.3 %collective-permute-start.3 = (f32[136,128]{1,0:T(8,128)S(1)}, f32[136,128]{1,0:T(8,128)S(1)}, u32[]{:S(2)}, u32[]{:S(2)}) collective-permute-start(f32[136,128]{1,0:T(8,128)S(1)} %get-tuple-element.60), channel_id=1, source_target_pairs={{0,12},{1,13},{2,14},{3,15},{4,8},{5,9},{6,10},{7,11},{8,4},{9,5},... | collective-permute-start | bytes 208904 | tf_op jit(solution)/shard_map/ppermute | solution.py:44
  13.2 0.0 collective-permute-start.2
  13.3 0.9 %collective-permute-done.1 = f32[136,128]{1,0:T(8,128)S(1)} collective-permute-done((f32[136,128]{1,0:T(8,128)S(1)}, f32[136,128]{1,0:T(8,128)S(1)}, u32[]{:S(2)}, u32[]{:S(2)}) %collective-permute-start.1) | collective-permute-done | bytes 69664 | tf_op jit(solution)/shard_map/ppermute | solution.py:44
  14.2 1.8 %collective-permute-done.3 = f32[136,128]{1,0:T(8,128)S(1)} collective-permute-done((f32[136,128]{1,0:T(8,128)S(1)}, f32[136,128]{1,0:T(8,128)S(1)}, u32[]{:S(2)}, u32[]{:S(2)}) %collective-permute-start.3) | collective-permute-done | bytes 69664 | tf_op jit(solution)/shard_map/ppermute | solution.py:44
  16.0 0.8 %collective-permute-done.2 = f32[136,128]{1,0:T(8,128)S(1)} collective-permute-done((f32[136,128]{1,0:T(8,128)S(1)}, f32[136,128]{1,0:T(8,128)S(1)}, u32[]{:S(2)}, u32[]{:S(2)}) %collective-permute-start.2) | collective-permute-done | bytes 69664 | tf_op jit(solution)/shard_map/ppermute | solution.py:44
  16.9 1.7 %collective-permute-start.4 = (f32[136,128]{1,0:T(8,128)S(1)}, f32[136,128]{1,0:T(8,128)S(1)}, u32[]{:S(2)}, u32[]{:S(2)}) collective-permute-start(f32[136,128]{1,0:T(8,128)S(1)} %fusion.1), channel_id=1, source_target_pairs={{0,2},{1,3},{2,0},{3,1},{4,6},{5,7},{6,4},{7,5},{8,10},{9,11},{10,... | collective-permute-start | bytes 208904 | tf_op jit(solution)/shard_map/ppermute | solution.py:44
  18.6 0.0 copy-start
  18.6 2.6 %prepare.1 = (f32[4,256,128]{2,1,0:T(8,128)S(1)}, f32[4,256,128]{2,1,0:T(8,128)S(1)}, bf16[2560,512]{1,0:T(8,128)(2,1)S(1)}, bf16[2560,512]{1,0:T(8,128)(2,1)S(1)}) custom-call(s32[2]{0:T(128)S(1)} %pad_add_fusion.place_ref, f32[4,4096,128]{2,1,0:T(8,128)S(1)} %get-tuple-element.34.held), custom_call_target="tpu_custom_call" | custom-call | flops 1 | bytes 1 | tf_op jit(solution)/shard_map/prepare/pallas_call | solution.py:398
  21.2 0.0 collective-permute-done.4
  21.2 2.4 %collective-permute-start.5 = (f32[136,128]{1,0:T(8,128)S(1)}, f32[136,128]{1,0:T(8,128)S(1)}, u32[]{:S(2)}, u32[]{:S(2)}) collective-permute-start(f32[136,128]{1,0:T(8,128)S(1)} %add.26), channel_id=1, source_target_pairs={{0,16},{1,17},{2,18},{3,19},{4,20},{5,21},{6,22},{7,23},{8,24},{9,... | collective-permute-start | bytes 208904 | tf_op jit(solution)/shard_map/ppermute | solution.py:44
  23.6 0.6 collective-permute-start.10
  24.1 3.1 %collective-permute-start.11 = (f32[4,256,128]{2,1,0:T(8,128)S(1)}, f32[4,256,128]{2,1,0:T(8,128)S(1)}, u32[]{:S(2)}, u32[]{:S(2)}) collective-permute-start(f32[4,256,128]{2,1,0:T(8,128)S(1)} %get-tuple-element.44), channel_id=1, source_target_pairs={{0,3},{1,2},{2,1},{3,0},{4,7},{5,6},{6,5},{7,4},{8,11},{9,10},{10,... | collective-permute-start | bytes 1572872 | tf_op jit(solution)/shard_map/ppermute | solution.py:44
  27.2 0.0 collective-permute-done.5
  27.2 1.8 %collective-permute-start.8 = (f32[136,128]{1,0:T(8,128)S(1)}, f32[136,128]{1,0:T(8,128)S(1)}, u32[]{:S(2)}, u32[]{:S(2)}) collective-permute-start(f32[136,128]{1,0:T(8,128)S(1)} %add.27), channel_id=1, source_target_pairs={{0,12},{1,13},{2,14},{3,15},{4,8},{5,9},{6,10},{7,11},{8,4},{9,5},... | collective-permute-start | bytes 208904 | tf_op jit(solution)/shard_map/ppermute | solution.py:44
  29.0 0.6 collective-permute-start.7
  29.7 0.2 collective-permute-start.6
  29.9 1.4 %collective-permute-done.8 = f32[136,128]{1,0:T(8,128)S(1)} collective-permute-done((f32[136,128]{1,0:T(8,128)S(1)}, f32[136,128]{1,0:T(8,128)S(1)}, u32[]{:S(2)}, u32[]{:S(2)}) %collective-permute-start.8) | collective-permute-done | bytes 69664 | tf_op jit(solution)/shard_map/ppermute | solution.py:44
  31.3 1.2 %collective-permute-done.7 = f32[136,128]{1,0:T(8,128)S(1)} collective-permute-done((f32[136,128]{1,0:T(8,128)S(1)}, f32[136,128]{1,0:T(8,128)S(1)}, u32[]{:S(2)}, u32[]{:S(2)}) %collective-permute-start.7) | collective-permute-done | bytes 69664 | tf_op jit(solution)/shard_map/ppermute | solution.py:44
  32.5 1.3 %collective-permute-done.6 = f32[136,128]{1,0:T(8,128)S(1)} collective-permute-done((f32[136,128]{1,0:T(8,128)S(1)}, f32[136,128]{1,0:T(8,128)S(1)}, u32[]{:S(2)}, u32[]{:S(2)}) %collective-permute-start.6) | collective-permute-done | bytes 69664 | tf_op jit(solution)/shard_map/ppermute | solution.py:44
  33.8 2.5 %collective-permute-start.9 = (f32[544,128]{1,0:T(8,128)S(1)}, f32[544,128]{1,0:T(8,128)S(1)}, u32[]{:S(2)}, u32[]{:S(2)}) collective-permute-start(f32[544,128]{1,0:T(8,128)S(1)} %pad_maximum_fusion.mine_ref), channel_id=1, source_target_pairs={{0,1},{1,0},{2,3},{3,2},{4,5},{5,4},{6,7},{7,6},{8,9},{9,8},{10,11... | collective-permute-start | bytes 835592 | tf_op jit(solution)/shard_map/ppermute | solution.py:44
  36.4 1.2 %collective-permute-done.9.other_ref = f32[544,128]{1,0:T(8,128)S(1)} collective-permute-done((f32[544,128]{1,0:T(8,128)S(1)}, f32[544,128]{1,0:T(8,128)S(1)}, u32[]{:S(2)}, u32[]{:S(2)}) %collective-permute-start.9) | collective-permute-done | bytes 278560 | tf_op jit(solution)/shard_map/ppermute | solution.py:44
  37.5 0.0 copy-done
  37.5 16.5 %iterate.1.block_ref = f32[128,512]{1,0:T(8,128)S(1)} custom-call(s32[2]{0:T(128)S(1)} %pad_add_fusion.place_ref, f32[544,128]{1,0:T(8,128)S(1)} %pad_maximum_fusion.mine_ref, f32[544,128]{1,0:T(8,128)S(1)} %collective-permute-done.9.other_ref, f32[512,128]{1,0:T(8,128)S(1)} %copy-done), custom_call_target="tpu_custom_call" | custom-call | flops 1 | bytes 1 | tf_op jit(solution)/shard_map/iterate/pallas_call | solution.py:304
  54.1 0.0 collective-permute-done.10.refs_0_
  54.1 0.0 collective-permute-done.11.refs_1_
  54.1 1.0 %project_far.1 = (f32[768,128]{1,0:T(8,128)S(1)}, f32[768,128]{1,0:T(8,128)S(1)}) custom-call(bf16[2560,512]{1,0:T(8,128)(2,1)S(1)} %get-tuple-element.46.high_ref, bf16[2560,512]{1,0:T(8,128)(2,1)S(1)} %get-tuple-element.47.low_ref, f32[128,512]{1,0:T(8,128)S(1)} %iterate.1.block_ref), custom_call_target="tpu_custom_call" | custom-call | flops 1 | bytes 1 | tf_op jit(solution)/shard_map/project_far/pallas_call | solution.py:432
  55.1 1.3 %collective-permute-start.15 = (f32[768,128]{1,0:T(8,128)S(1)}, f32[768,128]{1,0:T(8,128)S(1)}, u32[]{:S(2)}, u32[]{:S(2)}) collective-permute-start(f32[768,128]{1,0:T(8,128)S(1)} %get-tuple-element.54), channel_id=1, source_target_pairs={{0,2},{1,3},{2,0},{3,1},{4,6},{5,7},{6,4},{7,5},{8,10},{9,11},{10,... | collective-permute-start | bytes 1179656 | tf_op jit(solution)/shard_map/ppermute | solution.py:44
  56.4 0.8 collective-permute-start.12
  57.2 0.7 project_near.1
  57.9 0.1 collective-permute-start.13
  58.0 0.5 collective-permute-start.14
  58.5 1.3 %project_own.1.refs_0_ = f32[1024,128]{1,0:T(8,128)S(1)} custom-call(s32[2]{0:T(128)S(1)} %pad_add_fusion.place_ref, f32[4,4096,128]{2,1,0:T(8,128)S(1)} %get-tuple-element.34.held, f32[128,512]{1,0:T(8,128)S(1)} %iterate.1.block_ref), custom_call_target="tpu_custom_call" | custom-call | flops 1 | bytes 1 | tf_op jit(solution)/shard_map/project_own/pallas_call | solution.py:455
  59.8 3.7 %last_factor.1.factor_ref = f32[128,128]{1,0:T(8,128)S(1)} custom-call(f32[128,512]{1,0:T(8,128)S(1)} %iterate.1.block_ref), custom_call_target="tpu_custom_call" | custom-call | flops 1 | bytes 1 | tf_op jit(solution)/shard_map/last_factor/pallas_call | solution.py:334
  63.4 0.5 project_arrived.1
  63.9 1.7 %finish_arrived.1.refs_1_ = f32[4,4,4,64,128]{4,3,2,1,0:T(8,128)} custom-call(s32[2]{0:T(128)S(1)} %pad_add_fusion.place_ref, f32[128,128]{1,0:T(8,128)S(1)} %last_factor.1.factor_ref, f32[256,128]{1,0:T(8,128)S(1)} %get-tuple-element.57.refs_0_, f32[256,128]{1,0:T(8,128)S(1)} %get-tuple-element.58.refs_1_), custom_call_target="tpu_custom_call" | custom-call | flops 1 | bytes 1 | tf_op jit(solution)/shard_map/finish_arrived/pallas_call | solution.py:531
  65.6 0.0 collective-permute-done.15.refs_0_
  65.6 1.8 %finish_first_far.1.refs_3_ = f32[4,4,4,64,128]{4,3,2,1,0:T(8,128)} custom-call(s32[2]{0:T(128)S(1)} %pad_add_fusion.place_ref, f32[128,128]{1,0:T(8,128)S(1)} %last_factor.1.factor_ref, f32[768,128]{1,0:T(8,128)S(1)} %collective-permute-done.15.refs_0_, f32[4,4,4,64,128]{4,3,2,1,0:T(8,128)} %finish_arrived.1.refs_1_), custom_call_target="tpu_custom_call", output_to_operand_aliasing={{}: (3, {})} | custom-call | flops 1 | bytes 1 | tf_op jit(solution)/shard_map/finish_first_far/pallas_call | solution.py:531
  67.4 0.0 collective-permute-done.13.refs_1_
  67.4 0.0 collective-permute-done.14.refs_2_
  67.4 2.3 %finish_near.1.refs_1_ = f32[4,4,4,64,128]{4,3,2,1,0:T(8,128)} custom-call(s32[2]{0:T(128)S(1)} %pad_add_fusion.place_ref, f32[128,128]{1,0:T(8,128)S(1)} %last_factor.1.factor_ref, f32[1024,128]{1,0:T(8,128)S(1)} %project_own.1.refs_0_, f32[512,128]{1,0:T(8,128)S(1)} %collective-permute-done.13.refs_1_, ...), custom_call_target="tpu_custom_call", output_to_operand_aliasing={{}: (5, {})} | custom-call | flops 1 | bytes 1 | tf_op jit(solution)/shard_map/finish_near/pallas_call | solution.py:531
  69.7 4.7 %collective-permute-done.12.refs_0_ = f32[768,128]{1,0:T(8,128)S(1)} collective-permute-done((f32[768,128]{1,0:T(8,128)S(1)}, f32[768,128]{1,0:T(8,128)S(1)}, u32[]{:S(2)}, u32[]{:S(2)}) %collective-permute-start.12) | collective-permute-done | bytes 393248 | tf_op jit(solution)/shard_map/ppermute | solution.py:44
  74.4 1.8 %finish_last_far.1 = f32[4,4,4,64,128]{4,3,2,1,0:T(8,128)} custom-call(s32[2]{0:T(128)S(1)} %pad_add_fusion.place_ref, f32[128,128]{1,0:T(8,128)S(1)} %last_factor.1.factor_ref, f32[768,128]{1,0:T(8,128)S(1)} %collective-permute-done.12.refs_0_, f32[4,4,4,64,128]{4,3,2,1,0:T(8,128)} %finish_near.1.refs_1_), custom_call_target="tpu_custom_call", output_to_operand_aliasing={{}: (3, {})} | custom-call | flops 1 | bytes 1 | tf_op jit(solution)/shard_map/finish_last_far/pallas_call | solution.py:531
  (6 shorter events, 0.1 us)
Async XLA Ops:
  7.9 1.6 %collective-permute-start = (f32[544,128]{1,0:T(8,128)S(1)}, f32[544,128]{1,0:T(8,128)S(1)}, u32[]{:S(2)}, u32[]{:S(2)}) collective-permute-start(f32[544,128]{1,0:T(8,128)S(1)} %get-tuple-element.33), channel_id=1, source_target_pairs={{0,1},{1,0},{2,3},{3,2},{4,5},{5,4},{6,7},{7,6},{8,9},{9,8},{10,11... | collective-permute-start | bytes 835592 | tf_op jit(solution)/shard_map/ppermute | solution.py:44
  9.6 4.7 %collective-permute-start.1 = (f32[136,128]{1,0:T(8,128)S(1)}, f32[136,128]{1,0:T(8,128)S(1)}, u32[]{:S(2)}, u32[]{:S(2)}) collective-permute-start(f32[136,128]{1,0:T(8,128)S(1)} %get-tuple-element.59), channel_id=1, source_target_pairs={{0,4},{1,5},{2,6},{3,7},{4,0},{5,1},{6,2},{7,3},{8,12},{9,13},{10,... | collective-permute-start | bytes 208904 | tf_op jit(solution)/shard_map/ppermute | solution.py:44
  12.0 4.1 %collective-permute-start.3 = (f32[136,128]{1,0:T(8,128)S(1)}, f32[136,128]{1,0:T(8,128)S(1)}, u32[]{:S(2)}, u32[]{:S(2)}) collective-permute-start(f32[136,128]{1,0:T(8,128)S(1)} %get-tuple-element.60), channel_id=1, source_target_pairs={{0,12},{1,13},{2,14},{3,15},{4,8},{5,9},{6,10},{7,11},{8,4},{9,5},... | collective-permute-start | bytes 208904 | tf_op jit(solution)/shard_map/ppermute | solution.py:44
  13.2 3.6 %collective-permute-start.2 = (f32[136,128]{1,0:T(8,128)S(1)}, f32[136,128]{1,0:T(8,128)S(1)}, u32[]{:S(2)}, u32[]{:S(2)}) collective-permute-start(f32[136,128]{1,0:T(8,128)S(1)} %get-tuple-element.61), channel_id=1, source_target_pairs={{0,8},{1,9},{2,10},{3,11},{4,12},{5,13},{6,14},{7,15},{8,0},{9,1},... | collective-permute-start | bytes 208904 | tf_op jit(solution)/shard_map/ppermute | solution.py:44
  16.9 4.3 %collective-permute-start.4 = (f32[136,128]{1,0:T(8,128)S(1)}, f32[136,128]{1,0:T(8,128)S(1)}, u32[]{:S(2)}, u32[]{:S(2)}) collective-permute-start(f32[136,128]{1,0:T(8,128)S(1)} %fusion.1), channel_id=1, source_target_pairs={{0,2},{1,3},{2,0},{3,1},{4,6},{5,7},{6,4},{7,5},{8,10},{9,11},{10,... | collective-permute-start | bytes 208904 | tf_op jit(solution)/shard_map/ppermute | solution.py:44
  18.6 19.0 %copy-start = (f32[512,128]{1,0:T(8,128)S(1)}, f32[512,128]{1,0:T(8,128)}, u32[]{:S(2)}) copy-start(f32[512,128]{1,0:T(8,128)} %start_ref.1) | copy-start | bytes 786436
  21.2 6.0 %collective-permute-start.5 = (f32[136,128]{1,0:T(8,128)S(1)}, f32[136,128]{1,0:T(8,128)S(1)}, u32[]{:S(2)}, u32[]{:S(2)}) collective-permute-start(f32[136,128]{1,0:T(8,128)S(1)} %add.26), channel_id=1, source_target_pairs={{0,16},{1,17},{2,18},{3,19},{4,20},{5,21},{6,22},{7,23},{8,24},{9,... | collective-permute-start | bytes 208904 | tf_op jit(solution)/shard_map/ppermute | solution.py:44
  23.6 30.5 %collective-permute-start.10 = (f32[4,256,128]{2,1,0:T(8,128)S(1)}, f32[4,256,128]{2,1,0:T(8,128)S(1)}, u32[]{:S(2)}, u32[]{:S(2)}) collective-permute-start(f32[4,256,128]{2,1,0:T(8,128)S(1)} %get-tuple-element.43), channel_id=1, source_target_pairs={{0,2},{1,3},{2,0},{3,1},{4,6},{5,7},{6,4},{7,5},{8,10},{9,11},{10,... | collective-permute-start | bytes 1572872 | tf_op jit(solution)/shard_map/ppermute | solution.py:44
  24.1 30.0 %collective-permute-start.11 = (f32[4,256,128]{2,1,0:T(8,128)S(1)}, f32[4,256,128]{2,1,0:T(8,128)S(1)}, u32[]{:S(2)}, u32[]{:S(2)}) collective-permute-start(f32[4,256,128]{2,1,0:T(8,128)S(1)} %get-tuple-element.44), channel_id=1, source_target_pairs={{0,3},{1,2},{2,1},{3,0},{4,7},{5,6},{6,5},{7,4},{8,11},{9,10},{10,... | collective-permute-start | bytes 1572872 | tf_op jit(solution)/shard_map/ppermute | solution.py:44
  27.2 4.1 %collective-permute-start.8 = (f32[136,128]{1,0:T(8,128)S(1)}, f32[136,128]{1,0:T(8,128)S(1)}, u32[]{:S(2)}, u32[]{:S(2)}) collective-permute-start(f32[136,128]{1,0:T(8,128)S(1)} %add.27), channel_id=1, source_target_pairs={{0,12},{1,13},{2,14},{3,15},{4,8},{5,9},{6,10},{7,11},{8,4},{9,5},... | collective-permute-start | bytes 208904 | tf_op jit(solution)/shard_map/ppermute | solution.py:44
  29.0 3.5 %collective-permute-start.7 = (f32[136,128]{1,0:T(8,128)S(1)}, f32[136,128]{1,0:T(8,128)S(1)}, u32[]{:S(2)}, u32[]{:S(2)}) collective-permute-start(f32[136,128]{1,0:T(8,128)S(1)} %add.27), channel_id=1, source_target_pairs={{0,8},{1,9},{2,10},{3,11},{4,12},{5,13},{6,14},{7,15},{8,0},{9,1},... | collective-permute-start | bytes 208904 | tf_op jit(solution)/shard_map/ppermute | solution.py:44
  29.7 4.1 %collective-permute-start.6 = (f32[136,128]{1,0:T(8,128)S(1)}, f32[136,128]{1,0:T(8,128)S(1)}, u32[]{:S(2)}, u32[]{:S(2)}) collective-permute-start(f32[136,128]{1,0:T(8,128)S(1)} %add.27), channel_id=1, source_target_pairs={{0,4},{1,5},{2,6},{3,7},{4,0},{5,1},{6,2},{7,3},{8,12},{9,13},{10,... | collective-permute-start | bytes 208904 | tf_op jit(solution)/shard_map/ppermute | solution.py:44
  33.8 3.7 %collective-permute-start.9 = (f32[544,128]{1,0:T(8,128)S(1)}, f32[544,128]{1,0:T(8,128)S(1)}, u32[]{:S(2)}, u32[]{:S(2)}) collective-permute-start(f32[544,128]{1,0:T(8,128)S(1)} %pad_maximum_fusion.mine_ref), channel_id=1, source_target_pairs={{0,1},{1,0},{2,3},{3,2},{4,5},{5,4},{6,7},{7,6},{8,9},{9,8},{10,11... | collective-permute-start | bytes 835592 | tf_op jit(solution)/shard_map/ppermute | solution.py:44
  55.1 10.5 %collective-permute-start.15 = (f32[768,128]{1,0:T(8,128)S(1)}, f32[768,128]{1,0:T(8,128)S(1)}, u32[]{:S(2)}, u32[]{:S(2)}) collective-permute-start(f32[768,128]{1,0:T(8,128)S(1)} %get-tuple-element.54), channel_id=1, source_target_pairs={{0,2},{1,3},{2,0},{3,1},{4,6},{5,7},{6,4},{7,5},{8,10},{9,11},{10,... | collective-permute-start | bytes 1179656 | tf_op jit(solution)/shard_map/ppermute | solution.py:44
  56.4 18.0 %collective-permute-start.12 = (f32[768,128]{1,0:T(8,128)S(1)}, f32[768,128]{1,0:T(8,128)S(1)}, u32[]{:S(2)}, u32[]{:S(2)}) collective-permute-start(f32[768,128]{1,0:T(8,128)S(1)} %get-tuple-element.51), channel_id=1, source_target_pairs={{0,3},{1,2},{2,1},{3,0},{4,7},{5,6},{6,5},{7,4},{8,11},{9,10},{10,... | collective-permute-start | bytes 1179656 | tf_op jit(solution)/shard_map/ppermute | solution.py:44
  57.9 9.5 %collective-permute-start.13 = (f32[512,128]{1,0:T(8,128)S(1)}, f32[512,128]{1,0:T(8,128)S(1)}, u32[]{:S(2)}, u32[]{:S(2)}) collective-permute-start(f32[512,128]{1,0:T(8,128)S(1)} %get-tuple-element.52), channel_id=1, source_target_pairs={{0,1},{1,0},{2,3},{3,2},{4,5},{5,4},{6,7},{7,6},{8,9},{9,8},{10,11... | collective-permute-start | bytes 786440 | tf_op jit(solution)/shard_map/ppermute | solution.py:44
  58.0 9.4 %collective-permute-start.14 = (f32[512,128]{1,0:T(8,128)S(1)}, f32[512,128]{1,0:T(8,128)S(1)}, u32[]{:S(2)}, u32[]{:S(2)}) collective-permute-start(f32[512,128]{1,0:T(8,128)S(1)} %get-tuple-element.53), channel_id=1, source_target_pairs={{0,1},{1,0},{2,3},{3,2},{4,5},{5,4},{6,7},{7,6},{8,9},{9,8},{10,11... | collective-permute-start | bytes 786440 | tf_op jit(solution)/shard_map/ppermute | solution.py:44

commit v8 on v6

--- a/solution.py
+++ b/solution.py
@@ -249,7 +249,7 @@
 
 
 def sweep_kernel(
-    sweeps, place_ref, mine_ref, other_ref, start_ref, block_ref, blocks, gram, gram_high, gram_low,
+    sweeps, place_ref, mine_ref, other_ref, start_ref, block_ref, blocks, gram_high, gram_low,
     ahead, work, factor,
 ):
     place = place_ref[0]
@@ -260,24 +260,25 @@
         theirs = pl.multiple_of(((1 - (place & 1)) * 4 + quarter) * part, 8)
         blocks[pl.ds(mine, part), :] = mine_ref[k * part : (k + 1) * part, :]
         blocks[pl.ds(theirs, part), :] = other_ref[k * part : (k + 1) * part, :]
-    n = gram.shape[0]
+    n = gram_high.shape[0]
+
+    def place_block(i, j, block):
+        gram_high[span(i), span(j)], gram_low[span(i), span(j)] = halves(block)
+
     above = upper_blocks(n)
     for number, (i, j) in enumerate(above):
         block = blocks[span(number), :]
-        gram[span(i), span(j)] = block
-        gram[span(j), span(i)] = block.T
+        place_block(i, j, block)
+        place_block(j, i, block.T)
     row, column = block_indices()
     tail = len(above) + n // EDGE // 2
     for pair in range(n // EDGE // 2):
         block = blocks[span(len(above) + pair), :]
         turned = block.T
-        first, second = span(2 * pair), span(2 * pair + 1)
         diagonal = blocks[tail * EDGE + pair : tail * EDGE + pair + 1, :]
-        gram[first, first] = jnp.where(row <= column, block, turned)
-        gram[second, second] = jnp.where(
-            row == column, diagonal, jnp.where(row > column, block, turned)
-        )
-    gram_high[...], gram_low[...] = halves(gram[...])
+        place_block(2 * pair, 2 * pair, jnp.where(row <= column, block, turned))
+        second = jnp.where(row == column, diagonal, jnp.where(row > column, block, turned))
+        place_block(2 * pair + 1, 2 * pair + 1, second)
 
     def by_gram(block):
         high, low = halves(block)
@@ -308,7 +309,6 @@
         out_shape=jax.ShapeDtypeStruct((rank, n), jnp.float32),
         scratch_shapes=[
             pltpu.VMEM((2 * mine.shape[0], 128), jnp.float32),
-            pltpu.VMEM((n, n), jnp.float32),
             pltpu.VMEM((n, n), jnp.bfloat16),
             pltpu.VMEM((n, n), jnp.bfloat16),
             pltpu.VMEM((rank, n), jnp.float32),
@@ -493,7 +493,7 @@
 def finish_kernel(ranks, firsts, place_ref, factor_ref, *refs):
     pieces = refs[: len(ranks)]
     out, *results, sems = refs[-2 - len(ranks) :]
-    factor = factor_ref[...]
+    both = weights(factor_ref)
     per, size = out.shape[2], out.shape[3]
     sends = []
     for k, (rank, first, piece) in enumerate(zip(ranks, firsts, pieces, strict=True)):
@@ -503,7 +503,7 @@
             length = min(per - begin % per, last - begin)
             done = pl.ds(begin - first, length)
             rows = piece[(begin - first) * size : (begin - first + length) * size, :]
-            results[k][done] = dot(rows, factor, NT, HIGHEST).reshape(length, size, -1)
+            results[k][done] = halved_product(rows, both).reshape(length, size, -1)
             send = pltpu.make_async_copy(
                 results[k].at[done],
                 out.at[begin // per, place_ref[1] ^ rank, pl.ds(begin % per, length)],

time: 73.8 us -> 73.7 us (level)
  Pallas kernels: 38.9 us -> 38 us
  waiting for transfers between devices: 14.8 us -> 15.6 us
    pallas_call x4, Pallas kernels: 7.55 us -> 6.58 us  [finish(): pl.pallas_call(functools.partial(finish_kernel, ranks, firsts), in_specs=...]
    ppermute x16, waiting for transfers between devices: 14.8 us -> 15.6 us  [exchange(): return lax.ppermute(value, axes, [(i, i ^ mask) for i in range(size)])]
  transfers between devices with their start and end apart: 16 -> 16, of which waited for: 9 -> 9; matrix products, arithmetic and copies ran while one was open for 0% -> 0% of each run, Pallas kernels for 39% -> 38%
where the time goes in v8:
time: 73.7 us; the launch traced here: 73.6 us
  Pallas kernels  38 us (52%)
  starting transfers between devices  19.4 us (26%)
  waiting for transfers between devices  15.6 us (21%)
    ppermute x16, starting transfers between devices, exchange(): return lax.ppermute(value, axes, [(i, i ^ mask) for i in range(size)])  19.4 us
    ppermute x16, waiting for transfers between devices, exchange(): return lax.ppermute(value, axes, [(i, i ^ mask) for i in range(size)])  15.6 us
    pallas_call x1, Pallas kernels, iterate(): pl.pallas_call(functools.partial(sweep_kernel, SWEEPS), in_specs=[pl.Bloc...  13.9 us
    pallas_call x1, Pallas kernels, local_gram(): pl.pallas_call(functools.partial(gram_kernel, 1.0 / count), in_specs=[pl....  7.8 us
    pallas_call x4, Pallas kernels, finish(): pl.pallas_call(functools.partial(finish_kernel, ranks, firsts), in_specs=...  6.58 us
    pallas_call x1, Pallas kernels, last_factor(): pl.pallas_call(factor_kernel, in_specs=[vmem], out_specs=vmem, out_shape=...  3.67 us
    pallas_call x1, Pallas kernels, prepare(): pl.pallas_call(prepare_kernel, in_specs=[pl.BlockSpec(memory_space=pltpu....  2.56 us
    pallas_call x2, Pallas kernels, project_sent(): pl.pallas_call(functools.partial(sent_kernel, begin, [len(group) for grou...  1.73 us
  transfers between devices with their start and end apart: 16, of which 9 were waited for; matrix products, arithmetic and copies ran while one was open for 0% of the time, Pallas kernels for 38%

profile of v8, /device:TPU:1, one launch (start us, length us, event | category | flops | bytes accessed | tf_op | source)
XLA Modules:
  0.0 73.6 jit_solution(10947400253277033401)
XLA Ops:
  0.0 0.1 pad_add_fusion.place_ref
  0.1 7.8 %local_gram.1 = (f32[544,128]{1,0:T(8,128)S(1)}, f32[544,128]{1,0:T(8,128)S(1)}, f32[4,4096,128]{2,1,0:T(8,128)S(1)}) custom-call(s32[2]{0:T(128)S(1)} %pad_add_fusion.place_ref, f32[4096,512]{1,0:T(8,128)} %bitcast.4), custom_call_target="tpu_custom_call" | custom-call | flops 1 | bytes 1 | tf_op jit(solution)/shard_map/local_gram/pallas_call | solution.py:144
  7.9 0.1 collective-permute-start
  8.0 1.5 %collective-permute-done = f32[544,128]{1,0:T(8,128)S(1)} collective-permute-done((f32[544,128]{1,0:T(8,128)S(1)}, f32[544,128]{1,0:T(8,128)S(1)}, u32[]{:S(2)}, u32[]{:S(2)}) %collective-permute-start) | collective-permute-done | bytes 278560 | tf_op jit(solution)/shard_map/ppermute | solution.py:46
  9.6 2.4 %collective-permute-start.1 = (f32[136,128]{1,0:T(8,128)S(1)}, f32[136,128]{1,0:T(8,128)S(1)}, u32[]{:S(2)}, u32[]{:S(2)}) collective-permute-start(f32[136,128]{1,0:T(8,128)S(1)} %get-tuple-element.59), channel_id=1, source_target_pairs={{0,4},{1,5},{2,6},{3,7},{4,0},{5,1},{6,2},{7,3},{8,12},{9,13},{10,... | collective-permute-start | bytes 208904 | tf_op jit(solution)/shard_map/ppermute | solution.py:46
  12.0 1.3 %collective-permute-start.3 = (f32[136,128]{1,0:T(8,128)S(1)}, f32[136,128]{1,0:T(8,128)S(1)}, u32[]{:S(2)}, u32[]{:S(2)}) collective-permute-start(f32[136,128]{1,0:T(8,128)S(1)} %get-tuple-element.60), channel_id=1, source_target_pairs={{0,12},{1,13},{2,14},{3,15},{4,8},{5,9},{6,10},{7,11},{8,4},{9,5},... | collective-permute-start | bytes 208904 | tf_op jit(solution)/shard_map/ppermute | solution.py:46
  13.2 0.0 collective-permute-start.2
  13.3 0.9 %collective-permute-done.1 = f32[136,128]{1,0:T(8,128)S(1)} collective-permute-done((f32[136,128]{1,0:T(8,128)S(1)}, f32[136,128]{1,0:T(8,128)S(1)}, u32[]{:S(2)}, u32[]{:S(2)}) %collective-permute-start.1) | collective-permute-done | bytes 69664 | tf_op jit(solution)/shard_map/ppermute | solution.py:46
  14.2 1.8 %collective-permute-done.3 = f32[136,128]{1,0:T(8,128)S(1)} collective-permute-done((f32[136,128]{1,0:T(8,128)S(1)}, f32[136,128]{1,0:T(8,128)S(1)}, u32[]{:S(2)}, u32[]{:S(2)}) %collective-permute-start.3) | collective-permute-done | bytes 69664 | tf_op jit(solution)/shard_map/ppermute | solution.py:46
  16.0 0.8 %collective-permute-done.2 = f32[136,128]{1,0:T(8,128)S(1)} collective-permute-done((f32[136,128]{1,0:T(8,128)S(1)}, f32[136,128]{1,0:T(8,128)S(1)}, u32[]{:S(2)}, u32[]{:S(2)}) %collective-permute-start.2) | collective-permute-done | bytes 69664 | tf_op jit(solution)/shard_map/ppermute | solution.py:46
  16.9 1.7 %collective-permute-start.4 = (f32[136,128]{1,0:T(8,128)S(1)}, f32[136,128]{1,0:T(8,128)S(1)}, u32[]{:S(2)}, u32[]{:S(2)}) collective-permute-start(f32[136,128]{1,0:T(8,128)S(1)} %fusion.1), channel_id=1, source_target_pairs={{0,2},{1,3},{2,0},{3,1},{4,6},{5,7},{6,4},{7,5},{8,10},{9,11},{10,... | collective-permute-start | bytes 208904 | tf_op jit(solution)/shard_map/ppermute | solution.py:46
  18.6 0.0 copy-start
  18.6 2.6 %prepare.1 = (f32[4,256,128]{2,1,0:T(8,128)S(1)}, f32[4,256,128]{2,1,0:T(8,128)S(1)}, bf16[2560,512]{1,0:T(8,128)(2,1)S(1)}, bf16[2560,512]{1,0:T(8,128)(2,1)S(1)}) custom-call(s32[2]{0:T(128)S(1)} %pad_add_fusion.place_ref, f32[4,4096,128]{2,1,0:T(8,128)S(1)} %get-tuple-element.34.held), custom_call_target="tpu_custom_call" | custom-call | flops 1 | bytes 1 | tf_op jit(solution)/shard_map/prepare/pallas_call | solution.py:397
  21.2 0.0 collective-permute-done.4
  21.2 2.4 %collective-permute-start.5 = (f32[136,128]{1,0:T(8,128)S(1)}, f32[136,128]{1,0:T(8,128)S(1)}, u32[]{:S(2)}, u32[]{:S(2)}) collective-permute-start(f32[136,128]{1,0:T(8,128)S(1)} %add.26), channel_id=1, source_target_pairs={{0,16},{1,17},{2,18},{3,19},{4,20},{5,21},{6,22},{7,23},{8,24},{9,... | collective-permute-start | bytes 208904 | tf_op jit(solution)/shard_map/ppermute | solution.py:46
  23.6 0.6 collective-permute-start.10
  24.1 3.1 %collective-permute-start.11 = (f32[4,256,128]{2,1,0:T(8,128)S(1)}, f32[4,256,128]{2,1,0:T(8,128)S(1)}, u32[]{:S(2)}, u32[]{:S(2)}) collective-permute-start(f32[4,256,128]{2,1,0:T(8,128)S(1)} %get-tuple-element.44), channel_id=1, source_target_pairs={{0,3},{1,2},{2,1},{3,0},{4,7},{5,6},{6,5},{7,4},{8,11},{9,10},{10,... | collective-permute-start | bytes 1572872 | tf_op jit(solution)/shard_map/ppermute | solution.py:46
  27.2 0.0 collective-permute-done.5
  27.2 1.8 %collective-permute-start.8 = (f32[136,128]{1,0:T(8,128)S(1)}, f32[136,128]{1,0:T(8,128)S(1)}, u32[]{:S(2)}, u32[]{:S(2)}) collective-permute-start(f32[136,128]{1,0:T(8,128)S(1)} %add.27), channel_id=1, source_target_pairs={{0,12},{1,13},{2,14},{3,15},{4,8},{5,9},{6,10},{7,11},{8,4},{9,5},... | collective-permute-start | bytes 208904 | tf_op jit(solution)/shard_map/ppermute | solution.py:46
  29.0 0.6 collective-permute-start.7
  29.7 0.2 collective-permute-start.6
  29.9 1.4 %collective-permute-done.8 = f32[136,128]{1,0:T(8,128)S(1)} collective-permute-done((f32[136,128]{1,0:T(8,128)S(1)}, f32[136,128]{1,0:T(8,128)S(1)}, u32[]{:S(2)}, u32[]{:S(2)}) %collective-permute-start.8) | collective-permute-done | bytes 69664 | tf_op jit(solution)/shard_map/ppermute | solution.py:46
  31.3 1.2 %collective-permute-done.7 = f32[136,128]{1,0:T(8,128)S(1)} collective-permute-done((f32[136,128]{1,0:T(8,128)S(1)}, f32[136,128]{1,0:T(8,128)S(1)}, u32[]{:S(2)}, u32[]{:S(2)}) %collective-permute-start.7) | collective-permute-done | bytes 69664 | tf_op jit(solution)/shard_map/ppermute | solution.py:46
  32.5 1.3 %collective-permute-done.6 = f32[136,128]{1,0:T(8,128)S(1)} collective-permute-done((f32[136,128]{1,0:T(8,128)S(1)}, f32[136,128]{1,0:T(8,128)S(1)}, u32[]{:S(2)}, u32[]{:S(2)}) %collective-permute-start.6) | collective-permute-done | bytes 69664 | tf_op jit(solution)/shard_map/ppermute | solution.py:46
  33.8 2.5 %collective-permute-start.9 = (f32[544,128]{1,0:T(8,128)S(1)}, f32[544,128]{1,0:T(8,128)S(1)}, u32[]{:S(2)}, u32[]{:S(2)}) collective-permute-start(f32[544,128]{1,0:T(8,128)S(1)} %pad_maximum_fusion.mine_ref), channel_id=1, source_target_pairs={{0,1},{1,0},{2,3},{3,2},{4,5},{5,4},{6,7},{7,6},{8,9},{9,8},{10,11... | collective-permute-start | bytes 835592 | tf_op jit(solution)/shard_map/ppermute | solution.py:46
  36.4 1.2 %collective-permute-done.9.other_ref = f32[544,128]{1,0:T(8,128)S(1)} collective-permute-done((f32[544,128]{1,0:T(8,128)S(1)}, f32[544,128]{1,0:T(8,128)S(1)}, u32[]{:S(2)}, u32[]{:S(2)}) %collective-permute-start.9) | collective-permute-done | bytes 278560 | tf_op jit(solution)/shard_map/ppermute | solution.py:46
  37.5 0.0 copy-done
  37.5 13.9 %iterate.1.block_ref = f32[128,512]{1,0:T(8,128)S(1)} custom-call(s32[2]{0:T(128)S(1)} %pad_add_fusion.place_ref, f32[544,128]{1,0:T(8,128)S(1)} %pad_maximum_fusion.mine_ref, f32[544,128]{1,0:T(8,128)S(1)} %collective-permute-done.9.other_ref, f32[512,128]{1,0:T(8,128)S(1)} %copy-done), custom_call_target="tpu_custom_call" | custom-call | flops 1 | bytes 1 | tf_op jit(solution)/shard_map/iterate/pallas_call | solution.py:305
  51.5 0.0 collective-permute-done.10.refs_0_
  51.5 0.0 collective-permute-done.11.refs_1_
  51.5 1.0 %project_far.1 = (f32[768,128]{1,0:T(8,128)S(1)}, f32[768,128]{1,0:T(8,128)S(1)}) custom-call(bf16[2560,512]{1,0:T(8,128)(2,1)S(1)} %get-tuple-element.46.high_ref, bf16[2560,512]{1,0:T(8,128)(2,1)S(1)} %get-tuple-element.47.low_ref, f32[128,512]{1,0:T(8,128)S(1)} %iterate.1.block_ref), custom_call_target="tpu_custom_call" | custom-call | flops 1 | bytes 1 | tf_op jit(solution)/shard_map/project_far/pallas_call | solution.py:431
  52.5 1.3 %collective-permute-start.15 = (f32[768,128]{1,0:T(8,128)S(1)}, f32[768,128]{1,0:T(8,128)S(1)}, u32[]{:S(2)}, u32[]{:S(2)}) collective-permute-start(f32[768,128]{1,0:T(8,128)S(1)} %get-tuple-element.54), channel_id=1, source_target_pairs={{0,2},{1,3},{2,0},{3,1},{4,6},{5,7},{6,4},{7,5},{8,10},{9,11},{10,... | collective-permute-start | bytes 1179656 | tf_op jit(solution)/shard_map/ppermute | solution.py:46
  53.8 0.8 %collective-permute-start.12 = (f32[768,128]{1,0:T(8,128)S(1)}, f32[768,128]{1,0:T(8,128)S(1)}, u32[]{:S(2)}, u32[]{:S(2)}) collective-permute-start(f32[768,128]{1,0:T(8,128)S(1)} %get-tuple-element.51), channel_id=1, source_target_pairs={{0,3},{1,2},{2,1},{3,0},{4,7},{5,6},{6,5},{7,4},{8,11},{9,10},{10,... | collective-permute-start | bytes 1179656 | tf_op jit(solution)/shard_map/ppermute | solution.py:46
  54.6 0.7 project_near.1
  55.3 0.1 collective-permute-start.13
  55.4 0.5 collective-permute-start.14
  55.9 1.3 %project_own.1.refs_0_ = f32[1024,128]{1,0:T(8,128)S(1)} custom-call(s32[2]{0:T(128)S(1)} %pad_add_fusion.place_ref, f32[4,4096,128]{2,1,0:T(8,128)S(1)} %get-tuple-element.34.held, f32[128,512]{1,0:T(8,128)S(1)} %iterate.1.block_ref), custom_call_target="tpu_custom_call" | custom-call | flops 1 | bytes 1 | tf_op jit(solution)/shard_map/project_own/pallas_call | solution.py:454
  57.2 3.7 %last_factor.1.factor_ref = f32[128,128]{1,0:T(8,128)S(1)} custom-call(f32[128,512]{1,0:T(8,128)S(1)} %iterate.1.block_ref), custom_call_target="tpu_custom_call" | custom-call | flops 1 | bytes 1 | tf_op jit(solution)/shard_map/last_factor/pallas_call | solution.py:333
  60.9 0.5 project_arrived.1
  61.3 1.5 %finish_arrived.1.refs_1_ = f32[4,4,4,64,128]{4,3,2,1,0:T(8,128)} custom-call(s32[2]{0:T(128)S(1)} %pad_add_fusion.place_ref, f32[128,128]{1,0:T(8,128)S(1)} %last_factor.1.factor_ref, f32[256,128]{1,0:T(8,128)S(1)} %get-tuple-element.57.refs_0_, f32[256,128]{1,0:T(8,128)S(1)} %get-tuple-element.58.refs_1_), custom_call_target="tpu_custom_call" | custom-call | flops 1 | bytes 1 | tf_op jit(solution)/shard_map/finish_arrived/pallas_call | solution.py:530
  62.9 0.0 collective-permute-done.15.refs_0_
  62.9 1.6 %finish_first_far.1.refs_3_ = f32[4,4,4,64,128]{4,3,2,1,0:T(8,128)} custom-call(s32[2]{0:T(128)S(1)} %pad_add_fusion.place_ref, f32[128,128]{1,0:T(8,128)S(1)} %last_factor.1.factor_ref, f32[768,128]{1,0:T(8,128)S(1)} %collective-permute-done.15.refs_0_, f32[4,4,4,64,128]{4,3,2,1,0:T(8,128)} %finish_arrived.1.refs_1_), custom_call_target="tpu_custom_call", output_to_operand_aliasing={{}: (3, {})} | custom-call | flops 1 | bytes 1 | tf_op jit(solution)/shard_map/finish_first_far/pallas_call | solution.py:530
  64.5 0.0 collective-permute-done.13.refs_1_
  64.5 0.0 collective-permute-done.14.refs_2_
  64.5 1.9 %finish_near.1.refs_1_ = f32[4,4,4,64,128]{4,3,2,1,0:T(8,128)} custom-call(s32[2]{0:T(128)S(1)} %pad_add_fusion.place_ref, f32[128,128]{1,0:T(8,128)S(1)} %last_factor.1.factor_ref, f32[1024,128]{1,0:T(8,128)S(1)} %project_own.1.refs_0_, f32[512,128]{1,0:T(8,128)S(1)} %collective-permute-done.13.refs_1_, ...), custom_call_target="tpu_custom_call", output_to_operand_aliasing={{}: (5, {})} | custom-call | flops 1 | bytes 1 | tf_op jit(solution)/shard_map/finish_near/pallas_call | solution.py:530
  66.4 5.4 %collective-permute-done.12.refs_0_ = f32[768,128]{1,0:T(8,128)S(1)} collective-permute-done((f32[768,128]{1,0:T(8,128)S(1)}, f32[768,128]{1,0:T(8,128)S(1)}, u32[]{:S(2)}, u32[]{:S(2)}) %collective-permute-start.12) | collective-permute-done | bytes 393248 | tf_op jit(solution)/shard_map/ppermute | solution.py:46
  71.8 1.6 %finish_last_far.1 = f32[4,4,4,64,128]{4,3,2,1,0:T(8,128)} custom-call(s32[2]{0:T(128)S(1)} %pad_add_fusion.place_ref, f32[128,128]{1,0:T(8,128)S(1)} %last_factor.1.factor_ref, f32[768,128]{1,0:T(8,128)S(1)} %collective-permute-done.12.refs_0_, f32[4,4,4,64,128]{4,3,2,1,0:T(8,128)} %finish_near.1.refs_1_), custom_call_target="tpu_custom_call", output_to_operand_aliasing={{}: (3, {})} | custom-call | flops 1 | bytes 1 | tf_op jit(solution)/shard_map/finish_last_far/pallas_call | solution.py:530
  (6 shorter events, 0.1 us)
Async XLA Ops:
  7.9 1.6 %collective-permute-start = (f32[544,128]{1,0:T(8,128)S(1)}, f32[544,128]{1,0:T(8,128)S(1)}, u32[]{:S(2)}, u32[]{:S(2)}) collective-permute-start(f32[544,128]{1,0:T(8,128)S(1)} %get-tuple-element.33), channel_id=1, source_target_pairs={{0,1},{1,0},{2,3},{3,2},{4,5},{5,4},{6,7},{7,6},{8,9},{9,8},{10,11... | collective-permute-start | bytes 835592 | tf_op jit(solution)/shard_map/ppermute | solution.py:46
  9.6 4.7 %collective-permute-start.1 = (f32[136,128]{1,0:T(8,128)S(1)}, f32[136,128]{1,0:T(8,128)S(1)}, u32[]{:S(2)}, u32[]{:S(2)}) collective-permute-start(f32[136,128]{1,0:T(8,128)S(1)} %get-tuple-element.59), channel_id=1, source_target_pairs={{0,4},{1,5},{2,6},{3,7},{4,0},{5,1},{6,2},{7,3},{8,12},{9,13},{10,... | collective-permute-start | bytes 208904 | tf_op jit(solution)/shard_map/ppermute | solution.py:46
  12.0 4.1 %collective-permute-start.3 = (f32[136,128]{1,0:T(8,128)S(1)}, f32[136,128]{1,0:T(8,128)S(1)}, u32[]{:S(2)}, u32[]{:S(2)}) collective-permute-start(f32[136,128]{1,0:T(8,128)S(1)} %get-tuple-element.60), channel_id=1, source_target_pairs={{0,12},{1,13},{2,14},{3,15},{4,8},{5,9},{6,10},{7,11},{8,4},{9,5},... | collective-permute-start | bytes 208904 | tf_op jit(solution)/shard_map/ppermute | solution.py:46
  13.2 3.6 %collective-permute-start.2 = (f32[136,128]{1,0:T(8,128)S(1)}, f32[136,128]{1,0:T(8,128)S(1)}, u32[]{:S(2)}, u32[]{:S(2)}) collective-permute-start(f32[136,128]{1,0:T(8,128)S(1)} %get-tuple-element.61), channel_id=1, source_target_pairs={{0,8},{1,9},{2,10},{3,11},{4,12},{5,13},{6,14},{7,15},{8,0},{9,1},... | collective-permute-start | bytes 208904 | tf_op jit(solution)/shard_map/ppermute | solution.py:46
  16.9 4.3 %collective-permute-start.4 = (f32[136,128]{1,0:T(8,128)S(1)}, f32[136,128]{1,0:T(8,128)S(1)}, u32[]{:S(2)}, u32[]{:S(2)}) collective-permute-start(f32[136,128]{1,0:T(8,128)S(1)} %fusion.1), channel_id=1, source_target_pairs={{0,2},{1,3},{2,0},{3,1},{4,6},{5,7},{6,4},{7,5},{8,10},{9,11},{10,... | collective-permute-start | bytes 208904 | tf_op jit(solution)/shard_map/ppermute | solution.py:46
  18.6 19.0 %copy-start = (f32[512,128]{1,0:T(8,128)S(1)}, f32[512,128]{1,0:T(8,128)}, u32[]{:S(2)}) copy-start(f32[512,128]{1,0:T(8,128)} %start_ref.1) | copy-start | bytes 786436
  21.2 6.0 %collective-permute-start.5 = (f32[136,128]{1,0:T(8,128)S(1)}, f32[136,128]{1,0:T(8,128)S(1)}, u32[]{:S(2)}, u32[]{:S(2)}) collective-permute-start(f32[136,128]{1,0:T(8,128)S(1)} %add.26), channel_id=1, source_target_pairs={{0,16},{1,17},{2,18},{3,19},{4,20},{5,21},{6,22},{7,23},{8,24},{9,... | collective-permute-start | bytes 208904 | tf_op jit(solution)/shard_map/ppermute | solution.py:46
  23.6 27.9 %collective-permute-start.10 = (f32[4,256,128]{2,1,0:T(8,128)S(1)}, f32[4,256,128]{2,1,0:T(8,128)S(1)}, u32[]{:S(2)}, u32[]{:S(2)}) collective-permute-start(f32[4,256,128]{2,1,0:T(8,128)S(1)} %get-tuple-element.43), channel_id=1, source_target_pairs={{0,2},{1,3},{2,0},{3,1},{4,6},{5,7},{6,4},{7,5},{8,10},{9,11},{10,... | collective-permute-start | bytes 1572872 | tf_op jit(solution)/shard_map/ppermute | solution.py:46
  24.1 27.4 %collective-permute-start.11 = (f32[4,256,128]{2,1,0:T(8,128)S(1)}, f32[4,256,128]{2,1,0:T(8,128)S(1)}, u32[]{:S(2)}, u32[]{:S(2)}) collective-permute-start(f32[4,256,128]{2,1,0:T(8,128)S(1)} %get-tuple-element.44), channel_id=1, source_target_pairs={{0,3},{1,2},{2,1},{3,0},{4,7},{5,6},{6,5},{7,4},{8,11},{9,10},{10,... | collective-permute-start | bytes 1572872 | tf_op jit(solution)/shard_map/ppermute | solution.py:46
  27.2 4.1 %collective-permute-start.8 = (f32[136,128]{1,0:T(8,128)S(1)}, f32[136,128]{1,0:T(8,128)S(1)}, u32[]{:S(2)}, u32[]{:S(2)}) collective-permute-start(f32[136,128]{1,0:T(8,128)S(1)} %add.27), channel_id=1, source_target_pairs={{0,12},{1,13},{2,14},{3,15},{4,8},{5,9},{6,10},{7,11},{8,4},{9,5},... | collective-permute-start | bytes 208904 | tf_op jit(solution)/shard_map/ppermute | solution.py:46
  29.0 3.5 %collective-permute-start.7 = (f32[136,128]{1,0:T(8,128)S(1)}, f32[136,128]{1,0:T(8,128)S(1)}, u32[]{:S(2)}, u32[]{:S(2)}) collective-permute-start(f32[136,128]{1,0:T(8,128)S(1)} %add.27), channel_id=1, source_target_pairs={{0,8},{1,9},{2,10},{3,11},{4,12},{5,13},{6,14},{7,15},{8,0},{9,1},... | collective-permute-start | bytes 208904 | tf_op jit(solution)/shard_map/ppermute | solution.py:46
  29.7 4.1 %collective-permute-start.6 = (f32[136,128]{1,0:T(8,128)S(1)}, f32[136,128]{1,0:T(8,128)S(1)}, u32[]{:S(2)}, u32[]{:S(2)}) collective-permute-start(f32[136,128]{1,0:T(8,128)S(1)} %add.27), channel_id=1, source_target_pairs={{0,4},{1,5},{2,6},{3,7},{4,0},{5,1},{6,2},{7,3},{8,12},{9,13},{10,... | collective-permute-start | bytes 208904 | tf_op jit(solution)/shard_map/ppermute | solution.py:46
  33.8 3.7 %collective-permute-start.9 = (f32[544,128]{1,0:T(8,128)S(1)}, f32[544,128]{1,0:T(8,128)S(1)}, u32[]{:S(2)}, u32[]{:S(2)}) collective-permute-start(f32[544,128]{1,0:T(8,128)S(1)} %pad_maximum_fusion.mine_ref), channel_id=1, source_target_pairs={{0,1},{1,0},{2,3},{3,2},{4,5},{5,4},{6,7},{7,6},{8,9},{9,8},{10,11... | collective-permute-start | bytes 835592 | tf_op jit(solution)/shard_map/ppermute | solution.py:46
  52.5 10.4 %collective-permute-start.15 = (f32[768,128]{1,0:T(8,128)S(1)}, f32[768,128]{1,0:T(8,128)S(1)}, u32[]{:S(2)}, u32[]{:S(2)}) collective-permute-start(f32[768,128]{1,0:T(8,128)S(1)} %get-tuple-element.54), channel_id=1, source_target_pairs={{0,2},{1,3},{2,0},{3,1},{4,6},{5,7},{6,4},{7,5},{8,10},{9,11},{10,... | collective-permute-start | bytes 1179656 | tf_op jit(solution)/shard_map/ppermute | solution.py:46
  53.8 18.0 %collective-permute-start.12 = (f32[768,128]{1,0:T(8,128)S(1)}, f32[768,128]{1,0:T(8,128)S(1)}, u32[]{:S(2)}, u32[]{:S(2)}) collective-permute-start(f32[768,128]{1,0:T(8,128)S(1)} %get-tuple-element.51), channel_id=1, source_target_pairs={{0,3},{1,2},{2,1},{3,0},{4,7},{5,6},{6,5},{7,4},{8,11},{9,10},{10,... | collective-permute-start | bytes 1179656 | tf_op jit(solution)/shard_map/ppermute | solution.py:46
  55.3 9.2 %collective-permute-start.13 = (f32[512,128]{1,0:T(8,128)S(1)}, f32[512,128]{1,0:T(8,128)S(1)}, u32[]{:S(2)}, u32[]{:S(2)}) collective-permute-start(f32[512,128]{1,0:T(8,128)S(1)} %get-tuple-element.52), channel_id=1, source_target_pairs={{0,1},{1,0},{2,3},{3,2},{4,5},{5,4},{6,7},{7,6},{8,9},{9,8},{10,11... | collective-permute-start | bytes 786440 | tf_op jit(solution)/shard_map/ppermute | solution.py:46
  55.4 9.1 %collective-permute-start.14 = (f32[512,128]{1,0:T(8,128)S(1)}, f32[512,128]{1,0:T(8,128)S(1)}, u32[]{:S(2)}, u32[]{:S(2)}) collective-permute-start(f32[512,128]{1,0:T(8,128)S(1)} %get-tuple-element.53), channel_id=1, source_target_pairs={{0,1},{1,0},{2,3},{3,2},{4,5},{5,4},{6,7},{7,6},{8,9},{9,8},{10,11... | collective-permute-start | bytes 786440 | tf_op jit(solution)/shard_map/ppermute | solution.py:46
